TPU v7x, 32 devices: a whole 2x2x4 slice. The times are simulated.
32 devices in a mesh: seq: 4 (over y, x), seg: 8 (over z, core).
Axes of the slice: x: 2, y: 2, z: 4, core: 2. Of those that a mesh axis runs over, the one named last changes fastest.
Arguments:
- tokens: bfloat16 [8, 512, 2048], P('seg', 'seq'), may hold values from -6 to 6
- cotangent: bfloat16 [8, 512, 2048], P('seg', 'seq'), may hold values from -6 to 6
- start_state: float32 [8, 2560], P('seg'), may hold values from -6 to 6
- start_window: float32 [8, 3, 2560], P('seg'), may hold values from -6 to 6
- first_gain: float32 [2048], replicated, may hold values from 0.1 to 1.9
- recur_in: bfloat16 [2048, 2, 2560], P('seg', None, 'seq'), may hold values from -0.125 to 0.125
- conv_taps: float32 [4, 2560], replicated, may hold values from -3 to 3
- conv_bias: float32 [2560], replicated, may hold values from -3 to 3
- decay_gate: bfloat16 [10, 256, 256], replicated, may hold values from -0.375 to 0.375
- input_gate: bfloat16 [10, 256, 256], replicated, may hold values from -0.375 to 0.375
- decay_bias: float32 [2560], replicated, may hold values from -4 to 4
- input_bias: float32 [2560], replicated, may hold values from -4 to 4
- decay_logit: float32 [2560], replicated, may hold values from -9.3 to -3.4
- recur_out: bfloat16 [2048, 2560], P('seg', 'seq'), may hold values from -0.125 to 0.125
- second_gain: float32 [2048], replicated, may hold values from 0.1 to 1.9
- feed_in: bfloat16 [2048, 2, 6144], P('seg', None, 'seq'), may hold values from -0.125 to 0.125
- feed_out: bfloat16 [2048, 6144], P('seg', 'seq'), may hold values from -0.078125 to 0.078125
Outputs:
- output: bfloat16 [8, 512, 2048], P('seg', 'seq')
- input_grad: bfloat16 [8, 512, 2048], P('seg', 'seq')
- start_state_grad: float32 [8, 2560], P('seg')
- start_window_grad: float32 [8, 3, 2560], P('seg')
- first_gain_grad: float32 [2048], replicated
- recur_in_grad: float32 [2048, 2, 2560], P('seg', None, 'seq')
- conv_taps_grad: float32 [4, 2560], replicated
- conv_bias_grad: float32 [2560], replicated
- decay_gate_grad: float32 [10, 256, 256], replicated
- input_gate_grad: float32 [10, 256, 256], replicated
- decay_bias_grad: float32 [2560], replicated
- input_bias_grad: float32 [2560], replicated
- decay_logit_grad: float32 [2560], replicated
- recur_out_grad: float32 [2048, 2560], P('seg', 'seq')
- second_gain_grad: float32 [2048], replicated
- feed_in_grad: float32 [2048, 2, 6144], P('seg', None, 'seq')
- feed_out_grad: float32 [2048, 6144], P('seg', 'seq')
All inputs are finite; a program needn't handle non-finite values.
Results may differ from a plain program's by a relative error of at most 0.011.
Values may be sent and summed in bfloat16 or wider, within the bound.
No kernel may reach another device: no remote copies, remote signals or barrier semaphores. Data moves between devices by JAX's collectives and lax.ppermute only.
A program may use at most 448 MiB of HBM per device.

v0:
```python
import jax
import jax.numpy as jnp
from jax import lax
from jax.sharding import PartitionSpec as P

EPSILON = 1e-06
RATE_SCALE = 8.0


def shifted_2(value, axis, steps):
    count = lax.axis_size(axis)
    first, last = (max(0, -steps), min(count, count - steps))
    return lax.ppermute(value, axis, [(source, source + steps) for source in range(first, last)])


def entering(value, axis, join, neutral, backward):
    count, mine = (lax.axis_size(axis), lax.axis_index(axis))
    pieces = jax.tree.map(lambda part: lax.all_gather(part, axis), value)
    if backward:
        pieces = jax.tree.map(lambda part: part[::-1], pieces)
        mine = count - 1 - mine
    subtotal = jax.tree.map(
        lambda part, zero: jnp.full_like(part, 0) + jnp.asarray(zero, part.dtype), value, neutral
    )

    def turn(position, subtotal):
        longer = join(subtotal, jax.tree.map(lambda part: part[position], pieces))
        return jax.tree.map(lambda new, old: jnp.where(position < mine, new, old), longer, subtotal)

    return lax.fori_loop(0, count - 1, turn, subtotal)


def rms_norm(values, scale_gain):
    factor = lax.rsqrt(jnp.mean(values * values, axis=-1, keepdims=True) + EPSILON)
    return values * factor * scale_gain


def gelu_tanh(values):
    return jax.nn.gelu(values, approximate=True)


def gelu_back(values, grads):
    return jax.vjp(gelu_tanh, values)[1](grads)[0]


def combine_pairs(earlier, later):
    return (earlier[0] * later[0], later[0] * earlier[1] + later[1])


def conv_apply(padded, taps, offset):
    edge_rows = taps.shape[0] - 1
    length = padded.shape[-2] - edge_rows
    summed = padded[..., edge_rows:, :] * taps[0] + offset
    for back_step in range(1, taps.shape[0]):
        summed = (
            summed
            + padded[..., edge_rows - back_step : edge_rows - back_step + length, :]
            * taps[back_step]
        )
    return summed


def recurrence_terms(gate_pre, input_pre, conv_out, decay_logit):
    log_decay = -RATE_SCALE * jax.nn.sigmoid(gate_pre) * jax.nn.softplus(decay_logit)
    decays = jnp.exp(log_decay)
    drive_terms = jnp.sqrt(-jnp.expm1(2.0 * log_decay)) * jax.nn.sigmoid(input_pre) * conv_out
    return (decays, drive_terms)


def contract_last(left, right):
    return lax.dot_general(
        left, right, (((1,), (1,)), ((), ())), preferred_element_type=jnp.float32
    )


def contract_first(left, right):
    return lax.dot_general(
        left, right, (((0,), (0,)), ((), ())), preferred_element_type=jnp.float32
    )


def over_rows(block_rows, first_row, how_many, model_width):
    return jnp.concatenate(
        [
            block_rows(first_row // model_width + offset, 0, model_width)
            for offset in range(how_many // model_width)
        ],
        axis=0,
    )


def shards(
    tokens,
    cotangent,
    start_state,
    start_window,
    first_gain,
    recur_in,
    conv_taps,
    conv_bias,
    decay_gate,
    input_gate,
    decay_bias,
    input_bias,
    decay_logit,
    recur_out,
    second_gain,
    feed_in,
    feed_out,
):
    segments, length, model_width = tokens.shape
    recur_width = conv_taps.shape[1]
    head_count = decay_gate.shape[0]
    block_size = decay_gate.shape[1]
    edge_rows = conv_taps.shape[0] - 1
    row_count = segments * length
    seq_parts = lax.axis_size("seq")
    seq_place = lax.axis_index("seq")
    seg_place = lax.axis_index("seg")
    at_start = seq_place == 0
    recur_part = recur_in.shape[2]
    feed_part = feed_in.shape[2]
    own_rows = recur_in.shape[0]
    rows_rin, rows_rout, rows_fin, rows_fout = (
        lax.all_gather(recur_in, "seg", axis=0, tiled=True),
        lax.all_gather(recur_out, "seg", axis=0, tiled=True),
        lax.all_gather(feed_in, "seg", axis=0, tiled=True),
        lax.all_gather(feed_out, "seg", axis=0, tiled=True),
    )
    full_rin, full_rout = (
        lax.all_gather(rows_rin, "seq", axis=2, tiled=True),
        lax.all_gather(rows_rout, "seq", axis=1, tiled=True),
    )
    inputs = tokens.astype(jnp.float32).reshape(row_count, model_width)
    low1 = rms_norm(inputs, first_gain).astype(jnp.bfloat16)
    recur_matrix = full_rin.reshape(model_width, 2 * recur_width)
    projected = jnp.dot(low1, recur_matrix, preferred_element_type=jnp.float32)
    branch_pre = projected[:, :recur_width]
    conv_in = projected[:, recur_width:].reshape(segments, length, recur_width)
    tail_rows = conv_in[:, length - edge_rows :, :]
    arrived = shifted_2(tail_rows, "seq", 1)
    prior_rows = jnp.where(at_start, start_window, arrived)
    padded = jnp.concatenate([prior_rows, conv_in], axis=1)
    flat_conv = conv_apply(padded, conv_taps, conv_bias).reshape(row_count, recur_width)
    conv_low = flat_conv.astype(jnp.bfloat16).reshape(row_count, head_count, block_size)
    gate_pre = (
        jnp.einsum(
            "nhb,hbc->nhc", conv_low, decay_gate, preferred_element_type=jnp.float32
        ).reshape(row_count, recur_width)
        + decay_bias
    )
    input_pre = (
        jnp.einsum(
            "nhb,hbc->nhc", conv_low, input_gate, preferred_element_type=jnp.float32
        ).reshape(row_count, recur_width)
        + input_bias
    )
    decays, drive_terms = recurrence_terms(gate_pre, input_pre, flat_conv, decay_logit)
    decays = decays.reshape(segments, length, recur_width)
    drive_terms = drive_terms.reshape(segments, length, recur_width)
    prod_local, state_local = lax.associative_scan(combine_pairs, (decays, drive_terms), axis=1)
    group_prod = prod_local[:, -1]
    group_state = state_local[:, -1]
    before_prod, before_state = entering(
        (group_prod, group_state),
        "seq",
        combine_pairs,
        (jnp.ones_like(group_prod), jnp.zeros_like(group_state)),
        False,
    )
    entry_state = before_prod * start_state + before_state
    states = prod_local * entry_state[:, None, :] + state_local
    flat_states = states.reshape(row_count, recur_width)
    branch_act = gelu_tanh(branch_pre)
    mixed_low = (flat_states * branch_act).astype(jnp.bfloat16)
    residual = inputs + contract_last(mixed_low, full_rout)
    low2 = rms_norm(residual, second_gain).astype(jnp.bfloat16)
    upstream = cotangent.reshape(row_count, model_width)
    all_rows, all_cot = (
        lax.all_gather(low2, "seq", axis=0, tiled=True),
        lax.all_gather(upstream, "seq", axis=0, tiled=True),
    )
    feed_matrix = rows_fin.reshape(model_width, 2 * feed_part)
    gate_up = jnp.dot(all_rows, feed_matrix, preferred_element_type=jnp.float32)
    gate_val = gate_up[:, :feed_part]
    up_val = gate_up[:, feed_part:]
    gate_act = gelu_tanh(gate_val)
    hidden = (gate_act * up_val).astype(jnp.bfloat16)
    result = residual + lax.psum_scatter(
        contract_last(hidden, rows_fout), "seq", scatter_dimension=0, tiled=True
    )
    hidden_grad = jnp.dot(all_cot, rows_fout, preferred_element_type=jnp.float32)
    gate_grad = gelu_back(gate_val, hidden_grad * up_val).astype(jnp.bfloat16)
    up_grad = (hidden_grad * gate_act).astype(jnp.bfloat16)
    gate_up_grad = jnp.concatenate([gate_grad, up_grad], axis=1)
    normed2_grad = lax.psum_scatter(
        contract_last(gate_up_grad, feed_matrix), "seq", scatter_dimension=0, tiled=True
    )
    feed_summed = lax.psum_scatter(
        jnp.concatenate(
            [contract_first(all_rows, gate_up_grad), contract_first(all_cot, hidden)], axis=1
        ),
        "seg",
        scatter_dimension=0,
        tiled=True,
    )
    feed_in_grad = feed_summed[:, : 2 * feed_part].reshape(own_rows, 2, feed_part)
    feed_out_grad = feed_summed[:, 2 * feed_part :]
    output = result.astype(jnp.bfloat16).reshape(segments, length, model_width)
    norm2_pull = jax.vjp(rms_norm, residual, second_gain)[1]
    residual_norm_grad, second_gain_grad = norm2_pull(normed2_grad)
    residual_grad = upstream.astype(jnp.float32) + residual_norm_grad
    mixer_grad = residual_grad.astype(jnp.bfloat16)
    mixed_grad = jnp.dot(mixer_grad, full_rout, preferred_element_type=jnp.float32)
    state_grad = (mixed_grad * branch_act).reshape(segments, length, recur_width)
    branch_grad = gelu_back(branch_pre, mixed_grad * flat_states).astype(jnp.bfloat16)
    shifted = jnp.concatenate([decays[:, 1:], jnp.ones_like(decays[:, :1])], axis=1)
    suffix_prod, adjoint_local = lax.associative_scan(
        combine_pairs, (shifted, state_grad), reverse=True, axis=1
    )
    passed = decays[:, 0] * adjoint_local[:, 0]
    after_prod, after_adjoint = entering(
        (group_prod, passed),
        "seq",
        combine_pairs,
        (jnp.ones_like(passed), jnp.zeros_like(passed)),
        True,
    )
    adjoint = adjoint_local + suffix_prod * after_adjoint[:, None, :]
    previous = jnp.concatenate([entry_state[:, None, :], states[:, :-1]], axis=1)
    terms_pull = jax.vjp(recurrence_terms, gate_pre, input_pre, flat_conv, decay_logit)[1]
    gate_pre_grad, input_pre_grad, conv_direct, decay_logit_grad = terms_pull(
        (
            (adjoint * previous).reshape(row_count, recur_width),
            adjoint.reshape(row_count, recur_width),
        )
    )
    gate_low_grad = gate_pre_grad.astype(jnp.bfloat16).reshape(row_count, head_count, block_size)
    input_low_grad = input_pre_grad.astype(jnp.bfloat16).reshape(row_count, head_count, block_size)
    decay_bias_grad = jnp.sum(gate_low_grad.astype(jnp.float32), axis=0).reshape(recur_width)
    input_bias_grad = jnp.sum(input_low_grad.astype(jnp.float32), axis=0).reshape(recur_width)
    decay_gate_grad = jnp.einsum(
        "nhb,nhc->hbc", conv_low, gate_low_grad, preferred_element_type=jnp.float32
    )
    input_gate_grad = jnp.einsum(
        "nhb,nhc->hbc", conv_low, input_low_grad, preferred_element_type=jnp.float32
    )
    conv_back = conv_direct + (
        jnp.einsum("nhc,hbc->nhb", gate_low_grad, decay_gate, preferred_element_type=jnp.float32)
        + jnp.einsum("nhc,hbc->nhb", input_low_grad, input_gate, preferred_element_type=jnp.float32)
    ).reshape(row_count, recur_width)
    conv_pull = jax.vjp(conv_apply, padded, conv_taps, conv_bias)[1]
    padded_grad, conv_taps_grad, conv_bias_grad = conv_pull(
        conv_back.reshape(segments, length, recur_width)
    )
    prior_grad = padded_grad[:, :edge_rows]
    returned = shifted_2(prior_grad, "seq", -1)
    conv_in_grad = padded_grad[:, edge_rows:].at[:, length - edge_rows :].add(returned)
    proj_grad = jnp.concatenate(
        [branch_grad, conv_in_grad.reshape(row_count, recur_width).astype(jnp.bfloat16)], axis=1
    )
    normed1_grad = contract_last(proj_grad, recur_matrix)
    norm1_pull = jax.vjp(rms_norm, inputs, first_gain)[1]
    input_norm_grad, first_gain_grad = norm1_pull(normed1_grad)
    input_grad = (
        (residual_grad + input_norm_grad)
        .astype(jnp.bfloat16)
        .reshape(segments, length, model_width)
    )
    proj_blocks = proj_grad.reshape(row_count, 2, seq_parts, recur_part)
    mixed_blocks = mixed_low.reshape(row_count, seq_parts, recur_part)

    def mixer_block(block, first_row, how_many):
        grads = lax.dynamic_index_in_dim(proj_blocks, block, 2, False).reshape(
            row_count, 2 * recur_part
        )
        mixed = lax.dynamic_index_in_dim(mixed_blocks, block, 1, False)
        return jnp.concatenate(
            [contract_first(low1, grads), contract_first(mixer_grad, mixed)], axis=1
        )

    summed = lax.psum_scatter(
        over_rows(mixer_block, jnp.int32(0), lax.axis_size(("seq", "seg")) * own_rows, model_width),
        ("seq", "seg"),
        scatter_dimension=0,
        tiled=True,
    )
    recur_in_grad = summed[:, : 2 * recur_part].reshape(own_rows, 2, recur_part)
    recur_out_grad = summed[:, 2 * recur_part :]
    seg_total = segments * lax.axis_size("seg")
    seg_first = seg_place * segments
    state_full = lax.dynamic_update_slice_in_dim(
        jnp.zeros((seg_total, recur_width), jnp.float32), before_prod * passed, seg_first, 0
    )
    window_full = lax.dynamic_update_slice_in_dim(
        jnp.zeros((seg_total, edge_rows, recur_width), jnp.float32),
        jnp.where(at_start, prior_grad, jnp.zeros_like(prior_grad)),
        seg_first,
        0,
    )
    (
        first_gain_grad,
        conv_taps_grad,
        conv_bias_grad,
        decay_gate_grad,
        input_gate_grad,
        decay_bias_grad,
        input_bias_grad,
        decay_logit_grad,
        second_gain_grad,
        state_sum,
        window_sum,
    ) = lax.psum(
        (
            first_gain_grad,
            conv_taps_grad,
            conv_bias_grad,
            decay_gate_grad,
            input_gate_grad,
            decay_bias_grad,
            input_bias_grad,
            decay_logit_grad,
            second_gain_grad,
            state_full,
            window_full,
        ),
        ("seq", "seg"),
    )
    start_state_grad = lax.dynamic_slice_in_dim(state_sum, seg_first, segments, 0)
    start_window_grad = lax.dynamic_slice_in_dim(window_sum, seg_first, segments, 0)
    return (
        output,
        input_grad,
        start_state_grad,
        start_window_grad,
        first_gain_grad,
        recur_in_grad,
        conv_taps_grad,
        conv_bias_grad,
        decay_gate_grad,
        input_gate_grad,
        decay_bias_grad,
        input_bias_grad,
        decay_logit_grad,
        recur_out_grad,
        second_gain_grad,
        feed_in_grad,
        feed_out_grad,
    )


def solution(mesh):
    placed = (
        P("seg", "seq", None),
        P("seg", "seq", None),
        P("seg", None),
        P("seg", None, None),
        P(),
        P("seg", None, "seq"),
        P(),
        P(),
        P(),
        P(),
        P(),
        P(),
        P(),
        P("seg", "seq"),
        P(),
        P("seg", None, "seq"),
        P("seg", "seq"),
    )
    return jax.shard_map(
        shards,
        mesh=mesh,
        in_specs=placed,
        out_specs=(
            P("seg", "seq", None),
            P("seg", "seq", None),
            P("seg", None),
            P("seg", None, None),
            P(),
            P("seg", None, "seq"),
            P(),
            P(),
            P(),
            P(),
            P(),
            P(),
            P(),
            P("seg", "seq"),
            P(),
            P("seg", None, "seq"),
            P("seg", "seq"),
        ),
        check_vma=False,
    )
```

profile of v0, /device:TPU:0, one launch (start us, length us, event | category | flops | bytes accessed | tf_op | source)
XLA Modules:
  0.0 2249.9 jit_solution(11135387777145673067)
XLA Ops:
  8.7 59.7 %all-gather.10.cloned.1.call-done = bf16[2048,2,640]{2,1,0:T(2,128)(2,1)} async-done(((bf16[256,2,640]{2,1,0:T(2,128)(2,1)}), bf16[2048,2,640]{2,1,0:T(2,128)(2,1)}) %all-gather.10.cloned.1.call-update) | async-done | bytes 5242896 | tf_op jit(solution)/shard_map/all_gather | solution.py:125
  68.5 34.3 %all-gather.14.cloned.1.call-done = bf16[2048,640]{1,0:T(8,128)(2,1)} async-done(((bf16[256,640]{1,0:T(8,128)(2,1)}), bf16[2048,640]{1,0:T(8,128)(2,1)}) %all-gather.14.cloned.1.call-update) | async-done | bytes 2621456 | tf_op jit(solution)/shard_map/all_gather | solution.py:126
  104.6 353.5 %all-gather.12.cloned.1.call-done = bf16[2048,2,2560]{2,1,0:T(2,128)(2,1)} async-done(((bf16[2048,2,640]{2,1,0:T(2,128)(2,1)}), bf16[2048,2,2560]{2,1,0:T(2,128)(2,1)}) %all-gather.12.cloned.1.call-update) | async-done | bytes 20971536 | tf_op jit(solution)/shard_map/all_gather | solution.py:131
  458.1 14.8 copy.129
  577.0 11.3 all_gather.37
  612.8 70.8 %all-gather.20.cloned.1.call-done = bf16[2048,2,1536]{2,1,0:T(2,128)(2,1)} async-done(((bf16[256,2,1536]{2,1,0:T(2,128)(2,1)}), bf16[2048,2,1536]{2,1,0:T(2,128)(2,1)}) %all-gather.20.cloned.1.call-update) | async-done | bytes 12582928 | tf_op jit(solution)/shard_map/all_gather | solution.py:127
  683.6 12.8 copy.130
  696.4 23.0 %all-gather.18.cloned.1.call-done = bf16[512,2048]{1,0:T(8,128)(2,1)} async-done(((bf16[128,2048]{1,0:T(8,128)(2,1)}), bf16[512,2048]{1,0:T(8,128)(2,1)}) %all-gather.18.cloned.1.call-update) | async-done | bytes 2097168 | tf_op jit(solution)/shard_map/all_gather | solution.py:180
  719.4 11.9 fusion.117
  731.4 25.2 %all-gather.24.cloned.1.call-done = bf16[1,512,2048]{2,1,0:T(8,128)(2,1)} async-done(((bf16[1,128,2048]{2,1,0:T(8,128)(2,1)}), bf16[1,512,2048]{2,1,0:T(8,128)(2,1)}) %all-gather.24.cloned.1.call-update) | async-done | bytes 2097168 | tf_op jit(solution)/shard_map/all_gather | solution.py:181
  756.6 66.4 %all-gather.22.cloned.1.call-done = bf16[2048,1536]{1,0:T(8,128)(2,1)} async-done(((bf16[256,1536]{1,0:T(8,128)(2,1)}), bf16[2048,1536]{1,0:T(8,128)(2,1)}) %all-gather.22.cloned.1.call-update) | async-done | bytes 6291472 | tf_op jit(solution)/shard_map/all_gather | solution.py:128
  823.1 11.7 fusion.6
  836.4 11.1 fusion.11
  862.2 9.9 slice.607
  872.1 9.9 slice.600
  897.1 14.6 fusion.10
  1005.7 10.7 rev.18
  1065.1 10.0 convolution_bitcast_fusion
  1075.1 25.3 %pad_maximum_fusion = f32[2048,4608]{1,0:T(8,128)} fusion(f32[2048,1536]{1,0:T(8,128)} %convolution_bitcast_fusion, f32[2048,3072]{1,0:T(8,128)} %fusion.10), kind=kLoop, calls=%fused_computation.11 | loop fusion | flops 9437184 | bytes 75497472 | tf_op jit(solution)/shard_map/concatenate | solution.py:200
  1153.7 54.6 %maximum_maximum_fusion = f32[8192,1920]{0,1:T(8,128)} fusion(f32[2048,640]{0,1:T(8,128)S(1)} %bitcast.187, f32[2048,1280]{0,1:T(8,128)} %fusion.90, f32[2048,640]{0,1:T(8,128)} %fusion.56, f32[2048,1280]{0,1:T(8,128)} %fusion.88, f32[2048,640]{0,1:T(8,128)} %fusion.57, f32[2048,1280]{0,1:T(8,128)} %fusion.86, f32[2048,640]{0,1:T(8,128)} %fusion.58, ...), kind=kLoop, calls=%fused_computation.10 | loop fusion | flops 110100480 | bytes 125829120 | tf_op jit(solution)/shard_map/concatenate | solution.py:83
  1221.9 13.4 fusion.39
  1241.6 339.7 %reduce-scatter.11.cloned.1.call-done = f32[256,4608]{1,0:T(8,128)} async-done(((f32[2048,4608]{1,0:T(8,128)}), f32[256,4608]{1,0:T(8,128)}) %reduce-scatter.11.cloned.1.call-update) | async-done | bytes 4718608 | tf_op jit(solution)/shard_map/reduce_scatter | solution.py:199
  1593.4 508.0 %reduce-scatter.9.cloned.1.call-done = f32[256,1920]{0,1:T(8,128)} async-done(((f32[8192,1920]{0,1:T(8,128)}), f32[256,1920]{0,1:T(8,128)}) %reduce-scatter.9.cloned.1.call-update) | async-done | bytes 1966096 | tf_op jit(solution)/shard_map/reduce_scatter | solution.py:282
  2105.8 125.8 %all-reduce.71.cloned.1.call-done = (f32[2048]{0:T(1024)}, f32[4,2560]{1,0:T(4,128)}, f32[2560]{0:T(1024)}, f32[2560]{0:T(1024)}, f32[2560]{0:T(1024)}, /*index=5*/f32[2560]{0:T(1024)}, f32[2048]{0:T(1024)}) async-done(((f32[2048]{0:T(1024)}, f32[4,2560]{1,0:T(4,128)}, f32[2560]{0:T(1024)}, f32[2560]{0:T(1024)}, f32[2560]{0:T(1024)}, /*index=5*/f32[2560]{0:T(1024)}, f32[2048]{0:T(1024)}), (f32[2048]{0:T(1024)}, ...) | async-done | bytes 98320 | tf_op jit(solution)/shard_map/psum | solution.py:313
  (643 shorter events, 407.3 us)
Async XLA Ops:
  7.2 485.5 %copy-start = (bf16[10,256,256]{2,1,0:T(8,128)(2,1)S(1)}, bf16[10,256,256]{2,1,0:T(8,128)(2,1)}, u32[]{:S(2)}) copy-start(bf16[10,256,256]{2,1,0:T(8,128)(2,1)} %param.31) | copy-start | bytes 3932164
  7.2 61.3 %all-gather.10.cloned.1.call-start = ((), (), s32[]{:S(2)}) async-start(), calls=%async_computation.4 | async-start | bytes 5898240 | tf_op jit(solution)/shard_map/all_gather | solution.py:125
  7.9 94.8 %all-gather.14.cloned.1.call-start = ((), (), s32[]{:S(2)}) async-start(), calls=%async_computation.6 | async-start | bytes 2949120 | tf_op jit(solution)/shard_map/all_gather | solution.py:126
  8.7 449.4 %all-gather.12.cloned.1.call-start = ((), (), s32[]{:S(2)}) async-start(), calls=%async_computation.5 | async-start | bytes 26214400 | tf_op jit(solution)/shard_map/all_gather | solution.py:131
  68.5 533.4 %all-gather.16.cloned.1.call-start = ((), (), s32[]{:S(2)}) async-start(), calls=%async_computation.7 | async-start | bytes 13107200 | tf_op jit(solution)/shard_map/all_gather | solution.py:132
  102.8 580.8 %all-gather.20.cloned.1.call-start = ((), (), s32[]{:S(2)}) async-start(), calls=%async_computation.9 | async-start | bytes 14155776 | tf_op jit(solution)/shard_map/all_gather | solution.py:127
  103.4 616.0 %all-gather.18.cloned.1.call-start = ((), (), s32[]{:S(2)}) async-start(), calls=%async_computation.8 | async-start | bytes 2621440 | tf_op jit(solution)/shard_map/all_gather | solution.py:180
  104.6 368.4 %copy-start.112 = (f32[128]{0:T(128)}, f32[128]{0:T(128)S(1)}, u32[]{:S(2)}) copy-start(f32[128]{0:T(128)S(1)} %fusion.76) | copy-start | bytes 1540
  104.6 400.0 %copy-start.67 = (f32[2560]{0:T(1024)}, f32[2560]{0:T(1024)S(1)}, u32[]{:S(2)}) copy-start(f32[2560]{0:T(1024)S(1)} %broadcast_multiply_fusion.4) | copy-start | bytes 30724
  481.4 5.7 collective-permute-start
  558.9 29.4 %copy-start.36 = (f32[1,128,2560]{2,1,0:T(8,128)}, f32[1,128,2560]{2,1,0:T(8,128)S(1)}, u32[]{:S(2)}) copy-start(f32[1,128,2560]{2,1,0:T(8,128)S(1)} %pad.226) | copy-start | bytes 3932164
  571.1 25.4 %copy-start.118 = (f32[1,2560]{1,0:T(1,128)S(1)}, f32[1,2560]{1,0:T(1,128)}, u32[]{:S(2)}) copy-start(f32[1,2560]{1,0:T(1,128)} %param.25) | copy-start | bytes 30724
  609.7 304.2 %copy-start.5 = (f32[128,2048]{1,0:T(8,128)}, f32[128,2048]{1,0:T(8,128)S(1)}, u32[]{:S(2)}) copy-start(f32[128,2048]{1,0:T(8,128)S(1)} %get-tuple-element.478) | copy-start | bytes 3145732
  610.2 303.7 %copy-start.120 = (f32[128]{0:T(128)}, f32[128]{0:T(128)S(1)}, u32[]{:S(2)}) copy-start(f32[128]{0:T(128)S(1)} %fusion.77) | copy-start | bytes 1540
  611.2 145.4 %all-gather.24.cloned.1.call-start = ((), (), s32[]{:S(2)}) async-start(), calls=%async_computation.15 | async-start | bytes 2621440 | tf_op jit(solution)/shard_map/all_gather | solution.py:181
  612.0 211.1 %all-gather.22.cloned.1.call-start = ((), (), s32[]{:S(2)}) async-start(), calls=%async_computation.10 | async-start | bytes 7077888 | tf_op jit(solution)/shard_map/all_gather | solution.py:128
  612.7 299.0 %reduce-scatter.7.cloned.1.call-start = ((), (), s32[]{:S(2)}) async-start(), calls=%async_computation.12 | async-start | bytes 5242880 | tf_op jit(solution)/shard_map/reduce_scatter | solution.py:196
  847.6 387.7 %reduce-scatter.5.cloned.1.call-start = ((), (), s32[]{:S(2)}) async-start(), calls=%async_computation.11 | async-start | bytes 5242880 | tf_op jit(solution)/shard_map/reduce_scatter | solution.py:189
  897.1 341.4 %all-reduce.73.cloned.1.call-start = ((), (), s32[]{:S(2)}) async-start(), calls=%async_computation.17 | async-start | bytes 11141120 | tf_op jit(solution)/shard_map/psum | solution.py:313
  897.1 16.8 copy-start.40
  1064.6 516.7 %reduce-scatter.11.cloned.1.call-start = ((), (), s32[]{:S(2)}) async-start(), calls=%async_computation.14 | async-start | bytes 42467328 | tf_op jit(solution)/shard_map/reduce_scatter | solution.py:199
  1100.4 1000.9 %reduce-scatter.9.cloned.1.call-start = ((), (), s32[]{:S(2)}) async-start(), calls=%async_computation.13 | async-start | bytes 64880640 | tf_op jit(solution)/shard_map/reduce_scatter | solution.py:282
  1106.2 15.8 collective-permute-start.1
  1208.3 1023.3 %all-reduce.71.cloned.1.call-start = ((), (), s32[]{:S(2)}) async-start(), calls=%async_computation.16 | async-start | bytes 212992 | tf_op jit(solution)/shard_map/psum | solution.py:313
  (126 other events, 488.4 us)
Sparse Core Ops, SparseCore 0:
  9.7 58.7 all-gather.9
  70.1 32.6 all-gather.13
  104.3 353.7 all-gather.11
  459.8 105.4 all-gather.15
  566.8 116.7 all-gather.19
  685.9 33.5 all-gather.17
  721.3 35.2 all-gather.23
  758.3 64.7 all-gather.21
  847.7 51.3 reduce-scatter.6
  902.2 52.6 reduce-scatter.4
  1064.8 149.8 all-reduce.72
  1216.9 364.3 reduce-scatter.10
  1588.9 512.4 reduce-scatter.8
  2108.8 122.7 all-reduce.70
where the time goes:
time: 2260 us; the launch traced here: 2250 us
  waiting for transfers between devices  1610 us (71%)
  local copies, waits for them, and re-layouts  278 us (12%)
  other arithmetic  165 us (7%)
  matrix products  146 us (6%)
  blocking collectives  26.9 us (1%)
    reduce_scatter x1, waiting for transfers between devices, shards(): lax.psum_scatter(over_rows(mixer_block, jnp.int32(0), lax.axis_size(('seq...  508 us
    all_gather x1, waiting for transfers between devices, shards(): lax.all_gather(rows_rin, 'seq', axis=2, tiled=True)  353 us
    reduce_scatter x1, waiting for transfers between devices, shards(): lax.psum_scatter(jnp.concatenate([contract_first(all_rows, gate_up_grad),...  340 us
    psum x2, waiting for transfers between devices, shards(): lax.psum((first_gain_grad, conv_taps_grad, conv_bias_grad, decay_gate_gra...  126 us
    all_gather x1, waiting for transfers between devices, shards(): lax.all_gather(feed_in, 'seg', axis=0, tiled=True)  70.8 us
    all_gather x1, waiting for transfers between devices, shards(): lax.all_gather(feed_out, 'seg', axis=0, tiled=True)  66.4 us
    unnamed x281, local copies, waits for them, and re-layouts  60.5 us
    all_gather x1, waiting for transfers between devices, shards(): lax.all_gather(recur_in, 'seg', axis=0, tiled=True)  59.7 us
  transfers between devices with their start and end apart: 16, of which 11 were waited for; matrix products, arithmetic and copies ran while one was open for 24% of the time, Pallas kernels for 0%

commit v1 on v0

v1 whole, which is shorter than its diff:
```python
import jax
import jax.numpy as jnp
from jax import lax
from jax.experimental import pallas as pl
from jax.experimental.pallas import tpu as pltpu
from jax.sharding import PartitionSpec as P

EPSILON = 1e-06
RATE_SCALE = 8.0
LANES = 128
CHUNK = 64
BF = jnp.bfloat16
F32 = jnp.float32


def rms_norm(values, scale_gain):
    factor = lax.rsqrt(jnp.mean(values * values, axis=-1, keepdims=True) + EPSILON)
    return values * factor * scale_gain


def gelu_tanh(values):
    return jax.nn.gelu(values, approximate=True)


def gelu_back(values, grads):
    return jax.vjp(gelu_tanh, values)[1](grads)[0]


def contract_last(left, right):
    return lax.dot_general(left, right, (((1,), (1,)), ((), ())), preferred_element_type=F32)


def contract_first(left, right):
    return lax.dot_general(left, right, (((0,), (0,)), ((), ())), preferred_element_type=F32)


def contract(left, right):
    return jnp.dot(left, right, preferred_element_type=F32)


def conv_apply(padded, taps, offset):
    edge_rows = taps.shape[0] - 1
    length = padded.shape[-2] - edge_rows
    summed = padded[..., edge_rows:, :] * taps[0] + offset
    for back_step in range(1, taps.shape[0]):
        first = edge_rows - back_step
        summed = summed + padded[..., first : first + length, :] * taps[back_step]
    return summed


def swap(value, bit):
    return lax.ppermute(value, "seq", [(i, i ^ bit) for i in range(lax.axis_size("seq"))])


def gather_seq(value):
    half = value.shape[0] // 2
    one = swap(value, 1)
    two = swap(value, 2)
    three = jnp.concatenate([swap(one[:half], 2), swap(two[half:], 1)], axis=0)
    return value, one, two, three


def scatter_seq(blocks):
    half = blocks[0].shape[0] // 2
    low = [block.astype(BF) for block in blocks]
    from_one = swap(jnp.concatenate([low[3][:half], low[1][:half]], axis=0), 1).astype(F32)
    from_two = swap(jnp.concatenate([low[3][half:], low[2][half:]], axis=0), 2).astype(F32)
    pass_two = (blocks[2][:half] + from_one[:half]).astype(BF)
    pass_one = (blocks[1][half:] + from_two[:half]).astype(BF)
    last_two = swap(pass_two, 2).astype(F32)
    last_one = swap(pass_one, 1).astype(F32)
    top = blocks[0][:half] + from_one[half:] + last_two
    bottom = blocks[0][half:] + from_two[half:] + last_one
    return jnp.concatenate([top, bottom], axis=0)


def in_order(blocks, place):
    rows = blocks[0].shape[0]
    whole = jnp.zeros((rows * len(blocks),) + blocks[0].shape[1:], blocks[0].dtype)
    for step, block in enumerate(blocks):
        whole = lax.dynamic_update_slice_in_dim(whole, block, (place ^ step) * rows, 0)
    return whole


def neg_expm1(values):
    total = 1.0 + values * (1.0 / 9.0)
    for order in range(8, 1, -1):
        total = 1.0 + values * (1.0 / order) * total
    return jnp.where(values > -0.7, -values * total, 1.0 - jnp.exp(values))


def scan_kernel(
    blk_ref, low_ref, wd_ref, wi_ref, par_ref, conv_ref, branch_ref,
    states_ref, decay_ref, rate_ref, open_ref, mixed_ref,
):
    length = conv_ref.shape[0]
    par = par_ref[...]
    soft = par[2:3]
    row = lax.broadcasted_iota(jnp.int32, (CHUNK // 8, 8, LANES), 1)

    def body(step, carry):
        rows = pl.ds(pl.multiple_of(step * CHUNK, CHUNK), CHUNK)
        low = low_ref[rows, :]
        rate = jax.nn.sigmoid(contract(low, wd_ref[0]) + par[0:1])
        opened = jax.nn.sigmoid(contract(low, wi_ref[0]) + par[1:2])
        log_decay = -RATE_SCALE * rate * soft
        decay = jnp.exp(log_decay)
        drive = jnp.sqrt(neg_expm1(2.0 * log_decay)) * opened * conv_ref[rows, :]
        rate_ref[rows, :] = rate
        open_ref[rows, :] = opened
        decay_ref[rows, :] = decay
        prod = decay.reshape(CHUNK // 8, 8, LANES)
        total = drive.reshape(CHUNK // 8, 8, LANES)
        for shift in (1, 2, 4):
            inside = row >= shift
            moved = jnp.where(inside, pltpu.roll(total, shift, 1), 0.0)
            total = total + prod * moved
            prod = prod * jnp.where(inside, pltpu.roll(prod, shift, 1), 1.0)
        pieces = []
        for group in range(CHUNK // 8):
            piece = total[group] + prod[group] * carry
            carry = piece[7:8]
            pieces.append(piece)
        states = jnp.concatenate(pieces, axis=0)
        states_ref[rows, :] = states
        mixed_ref[rows, :] = (states * gelu_tanh(branch_ref[rows, :])).astype(BF)
        return carry

    lax.fori_loop(0, length // CHUNK, body, par[3:4])


def scan_forward(blk, conv_ext, decay_w, input_w, params, conv_out, branch_pre):
    length, width = conv_out.shape
    tiles = width // LANES
    tile = pl.BlockSpec((length, LANES), lambda i, blk: (0, i))
    weight = pl.BlockSpec((1, decay_w.shape[1], LANES), lambda i, blk: (i, 0, 0))
    whole = jax.ShapeDtypeStruct((length, width), F32)
    return pl.pallas_call(
        scan_kernel,
        grid_spec=pltpu.PrefetchScalarGridSpec(
            num_scalar_prefetch=1,
            grid=(tiles,),
            in_specs=[
                pl.BlockSpec((length, decay_w.shape[1]), lambda i, blk: (0, blk[i])),
                weight,
                weight,
                pl.BlockSpec((8, LANES), lambda i, blk: (0, i)),
                tile,
                tile,
            ],
            out_specs=[tile] * 5,
        ),
        out_shape=[whole, whole, whole, whole, jax.ShapeDtypeStruct((length, width), BF)],
        compiler_params=pltpu.CompilerParams(vmem_limit_bytes=32 * 2**20),
        cost_estimate=pl.CostEstimate(
            flops=4 * length * width * 256, bytes_accessed=length * width * 28, transcendentals=0
        ),
        name="scan_forward",
    )(blk, conv_ext, decay_w, input_w, params, conv_out, branch_pre)


def back_kernel(
    par_ref, mixed_ref, branch_ref, states_ref, decay_ref, rate_ref, open_ref, conv_ref,
    branch_out, gate_out, input_out, direct_out, sums_out,
):
    length = conv_ref.shape[0]
    groups = CHUNK // 8
    par = par_ref[...]
    soft = par[2:3]
    row = lax.broadcasted_iota(jnp.int32, (groups, 8, LANES), 1)
    flat_row = lax.broadcasted_iota(jnp.int32, (CHUNK, LANES), 0)
    steps = length // CHUNK

    def body(turn, carried):
        carry, gate_sum, input_sum, logit_sum = carried
        step = steps - 1 - turn
        first = pl.multiple_of(step * CHUNK, CHUNK)
        rows = pl.ds(first, CHUNK)
        mixed_grad = mixed_ref[rows, :]
        branch = branch_ref[rows, :]
        states = states_ref[rows, :]
        decay = decay_ref[rows, :]
        branch_act, pull = jax.vjp(gelu_tanh, branch)
        branch_out[rows, :] = pull(mixed_grad * states)[0].astype(BF)
        state_grad = mixed_grad * branch_act
        prod = decay.reshape(groups, 8, LANES)
        total = (decay * state_grad).reshape(groups, 8, LANES)
        for shift in (1, 2, 4):
            inside = row < 8 - shift
            moved = jnp.where(inside, pltpu.roll(total, 8 - shift, 1), 0.0)
            total = total + prod * moved
            prod = prod * jnp.where(inside, pltpu.roll(prod, 8 - shift, 1), 1.0)
        pieces = [None] * groups
        after = carry
        for group in reversed(range(groups)):
            piece = total[group] + prod[group] * after
            after = piece[0:1]
            pieces[group] = piece
        passed = jnp.concatenate(pieces, axis=0)
        shifted = jnp.where(flat_row == CHUNK - 1, carry, pltpu.roll(passed, CHUNK - 1, 0))
        adjoint = state_grad + shifted
        before = states_ref[pl.ds(pl.multiple_of(jnp.maximum(first - 8, 0), 8), 8), :][7:8]
        before = jnp.where(step == 0, par[3:4], before)
        previous = jnp.where(flat_row == 0, before, pltpu.roll(states, 1, 0))
        rate = rate_ref[rows, :]
        opened = open_ref[rows, :]
        conv = conv_ref[rows, :]
        log_decay = -RATE_SCALE * rate * soft
        scale = jnp.sqrt(neg_expm1(2.0 * log_decay))
        opened_conv = opened * conv
        log_grad = decay * (adjoint * previous - adjoint * opened_conv * (decay / scale))
        scaled = adjoint * scale
        direct_out[rows, :] = scaled * opened
        input_grad = (scaled * conv * opened * (1.0 - opened)).astype(BF)
        rate_grad = log_grad * rate
        gate_grad = (rate_grad * (1.0 - rate) * (-RATE_SCALE * soft)).astype(BF)
        gate_out[rows, :] = gate_grad
        input_out[rows, :] = input_grad

        def folded(value):
            return jnp.sum(value.astype(F32).reshape(groups, 8, LANES), axis=0)

        return (
            after,
            gate_sum + folded(gate_grad),
            input_sum + folded(input_grad),
            logit_sum + folded(rate_grad),
        )

    zero = jnp.zeros((8, LANES), F32)
    after, gate_sum, input_sum, logit_sum = lax.fori_loop(
        0, steps, body, (jnp.zeros((1, LANES), F32), zero, zero, zero)
    )
    sums_out[...] = jnp.concatenate(
        [
            jnp.sum(gate_sum, axis=0, keepdims=True),
            jnp.sum(input_sum, axis=0, keepdims=True),
            jnp.sum(logit_sum, axis=0, keepdims=True) * (-RATE_SCALE * par[4:5]),
            after,
            jnp.zeros((4, LANES), F32),
        ],
        axis=0,
    )


def scan_backward(params, mixed_grad, branch_pre, states, decays, rate, opened, conv_out):
    length, width = conv_out.shape
    tiles = width // LANES
    tile = pl.BlockSpec((length, LANES), lambda i: (0, i))
    small = pl.BlockSpec((8, LANES), lambda i: (0, i))
    low = jax.ShapeDtypeStruct((length, width), BF)
    return pl.pallas_call(
        back_kernel,
        grid=(tiles,),
        in_specs=[small] + [tile] * 7,
        out_specs=[tile] * 4 + [small],
        out_shape=[
            low,
            low,
            low,
            jax.ShapeDtypeStruct((length, width), F32),
            jax.ShapeDtypeStruct((8, width), F32),
        ],
        compiler_params=pltpu.CompilerParams(vmem_limit_bytes=32 * 2**20),
        cost_estimate=pl.CostEstimate(
            flops=100 * length * width, bytes_accessed=length * width * 38, transcendentals=0
        ),
        name="scan_backward",
    )(params, mixed_grad, branch_pre, states, decays, rate, opened, conv_out)


def shards(
    tokens,
    cotangent,
    start_state,
    start_window,
    first_gain,
    recur_in,
    conv_taps,
    conv_bias,
    decay_gate,
    input_gate,
    decay_bias,
    input_bias,
    decay_logit,
    recur_out,
    second_gain,
    feed_in,
    feed_out,
):
    segments, length, model_width = tokens.shape
    recur_width = conv_taps.shape[1]
    head_count, block_size = decay_gate.shape[:2]
    edge_rows = conv_taps.shape[0] - 1
    seq_parts = lax.axis_size("seq")
    place = lax.axis_index("seq")
    own_rows, _, recur_part = recur_in.shape
    feed_part = feed_in.shape[2]
    first_channel = place * recur_part
    first_block = first_channel // block_size
    block_count = -(-recur_part // block_size)
    strip = block_count * block_size - recur_part
    odd = place % 2 == 1

    def own(value):
        return lax.dynamic_slice_in_dim(value, first_channel, recur_part, value.ndim - 1)

    def spread(value):
        sent = jnp.where(odd, value[:, :strip], value[:, recur_part - strip :])
        arrived = swap(sent, 1)
        return jnp.where(
            odd,
            jnp.concatenate([arrived, value], axis=1),
            jnp.concatenate([value, arrived], axis=1),
        )

    def gather_seg(value):
        return lax.all_gather(value, "seg", axis=0, tiled=True)

    def scatter_seg(value):
        return lax.psum_scatter(value.astype(BF), "seg", scatter_dimension=0, tiled=True).astype(F32)

    full_rin = gather_seg(recur_in.reshape(own_rows, 2 * recur_part))
    full_rout = gather_seg(recur_out)
    full_fin = gather_seg(feed_in.reshape(own_rows, 2 * feed_part))
    full_fout = gather_seg(feed_out)

    inputs = tokens.astype(F32).reshape(length, model_width)
    upstream = cotangent.reshape(length, model_width)
    low1 = rms_norm(inputs, first_gain).astype(BF)
    all_low1 = in_order(gather_seq(low1), place)
    all_cot = jnp.concatenate(gather_seq(upstream), axis=0)

    taps = own(conv_taps)
    logit = own(decay_logit[None])
    params = jnp.concatenate(
        [
            own(decay_bias[None]),
            own(input_bias[None]),
            jax.nn.softplus(logit),
            own(start_state),
            jax.nn.sigmoid(logit),
            jnp.zeros((3, recur_part), F32),
        ],
        axis=0,
    )
    window = own(start_window)[0]
    decay_blocks = lax.dynamic_slice_in_dim(decay_gate, first_block, block_count, 0)
    input_blocks = lax.dynamic_slice_in_dim(input_gate, first_block, block_count, 0)
    tiles = recur_part // LANES
    halves = block_size // LANES
    first_tile = jnp.where(odd, strip // LANES, 0)

    def tiled(blocks):
        parts = blocks.reshape(block_count, block_size, halves, LANES).transpose(0, 2, 1, 3)
        parts = parts.reshape(block_count * halves, block_size, LANES)
        return lax.dynamic_slice_in_dim(parts, first_tile, tiles, 0)

    tile_block = ((first_tile + jnp.arange(tiles)) // halves).astype(jnp.int32)

    projected = contract(all_low1, full_rin)
    branch_pre = projected[:, :recur_part]
    padded = jnp.concatenate([window, projected[:, recur_part:]], axis=0)
    conv_out = conv_apply(padded, taps, own(conv_bias[None]))
    conv_ext = spread(conv_out.astype(BF))
    states, decays, rate, opened, mixed_low = scan_forward(
        tile_block, conv_ext, tiled(decay_blocks), tiled(input_blocks), params, conv_out, branch_pre
    )

    def for_places(left, right):
        return [
            contract_last(
                lax.dynamic_slice_in_dim(left, (place ^ step) * length, length, 0), right
            )
            for step in range(seq_parts)
        ]

    residual = inputs + scatter_seq(for_places(mixed_low, full_rout))

    low2 = rms_norm(residual, second_gain).astype(BF)
    all_low2 = jnp.concatenate(gather_seq(low2), axis=0)
    gate_up = contract(all_low2, full_fin)
    gate_val = gate_up[:, :feed_part]
    up_val = gate_up[:, feed_part:]
    gate_act = gelu_tanh(gate_val)
    hidden = (gate_act * up_val).astype(BF)
    hidden_grad = contract(all_cot, full_fout)
    gate_grad = gelu_back(gate_val, hidden_grad * up_val).astype(BF)
    up_grad = (hidden_grad * gate_act).astype(BF)
    gate_up_grad = jnp.concatenate([gate_grad, up_grad], axis=1)

    def rows_split(value):
        return [value[step * length : (step + 1) * length] for step in range(seq_parts)]

    normed2_grad = scatter_seq(rows_split(contract_last(gate_up_grad, full_fin)))
    mlp_out = scatter_seq(rows_split(contract_last(hidden, full_fout)))
    output = (residual + mlp_out).astype(BF).reshape(tokens.shape)
    feed_in_grad = scatter_seg(contract_first(all_low2, gate_up_grad))
    feed_out_grad = scatter_seg(contract_first(all_cot, hidden))

    residual_norm_grad, second_gain_grad = jax.vjp(rms_norm, residual, second_gain)[1](normed2_grad)
    residual_grad = upstream.astype(F32) + residual_norm_grad

    mixer_grad = in_order(gather_seq(residual_grad.astype(BF)), place)
    mixed_grad = contract(mixer_grad, full_rout)
    branch_grad, gate_low_grad, input_low_grad, conv_direct, sums = scan_backward(
        params, mixed_grad, branch_pre, states, decays, rate, opened, conv_out
    )
    gates_ext = spread(jnp.concatenate([gate_low_grad, input_low_grad], axis=0))
    all_rows = seq_parts * length

    def blocked(value):
        return value.reshape(value.shape[0], block_count, block_size)

    gate_ext, input_ext = (blocked(gates_ext[:all_rows]), blocked(gates_ext[all_rows:]))
    back_ext = (
        jnp.einsum("nhc,hbc->nhb", gate_ext, decay_blocks, preferred_element_type=F32)
        + jnp.einsum("nhc,hbc->nhb", input_ext, input_blocks, preferred_element_type=F32)
    ).reshape(all_rows, block_count * block_size)

    def own_of(ext):
        return jnp.where(odd, ext[:, strip:], ext[:, :recur_part])

    conv_back = conv_direct + own_of(back_ext)
    low_ext = blocked(conv_ext)
    gate_grads = [
        own_of(
            jnp.einsum("nhb,nhc->bhc", low_ext, ext, preferred_element_type=F32).reshape(
                block_size, block_count * block_size
            )
        )
        for ext in (gate_ext, input_ext)
    ]
    conv_pull = jax.vjp(conv_apply, padded, taps, own(conv_bias[None]))[1]
    padded_grad, taps_grad, conv_bias_grad = conv_pull(conv_back)
    conv_in_grad = padded_grad[edge_rows:].astype(BF)
    proj_grad = jnp.concatenate([branch_grad, conv_in_grad], axis=1)
    normed1_grad = scatter_seq(for_places(proj_grad, full_rin))
    input_norm_grad, first_gain_grad = jax.vjp(rms_norm, inputs, first_gain)[1](normed1_grad)
    input_grad = (residual_grad + input_norm_grad).astype(BF).reshape(tokens.shape)

    recur_in_grad = scatter_seg(contract_first(all_low1, proj_grad))
    recur_out_grad = scatter_seg(contract_first(mixer_grad, mixed_low))

    small = lax.psum(
        jnp.concatenate(gate_grads + [taps_grad, conv_bias_grad, sums[:3]], axis=0), "seg"
    )
    small = jnp.concatenate([small, sums[3:4], padded_grad[:edge_rows]], axis=0)
    small = lax.all_gather(small, "seq", axis=1, tiled=True)

    def take(first, count):
        return small[first : first + count]

    def as_blocks(value):
        return value.reshape(block_size, head_count, block_size).transpose(1, 0, 2)

    gains = lax.psum(jnp.stack([first_gain_grad, second_gain_grad]), ("seq", "seg"))
    at = 2 * block_size
    kernel_taps = conv_taps.shape[0]
    return (
        output,
        input_grad,
        take(at + kernel_taps + 4, 1),
        take(at + kernel_taps + 5, edge_rows)[None],
        gains[0],
        recur_in_grad.reshape(own_rows, 2, recur_part),
        take(at, kernel_taps),
        small[at + kernel_taps],
        as_blocks(take(0, block_size)),
        as_blocks(take(block_size, block_size)),
        small[at + kernel_taps + 1],
        small[at + kernel_taps + 2],
        small[at + kernel_taps + 3],
        recur_out_grad,
        gains[1],
        feed_in_grad.reshape(own_rows, 2, feed_part),
        feed_out_grad,
    )


def solution(mesh):
    placed = (
        P("seg", "seq", None),
        P("seg", "seq", None),
        P("seg", None),
        P("seg", None, None),
        P(),
        P("seg", None, "seq"),
        P(),
        P(),
        P(),
        P(),
        P(),
        P(),
        P(),
        P("seg", "seq"),
        P(),
        P("seg", None, "seq"),
        P("seg", "seq"),
    )
    return jax.shard_map(
        shards,
        mesh=mesh,
        in_specs=placed,
        out_specs=(
            P("seg", "seq", None),
            P("seg", "seq", None),
            P("seg", None),
            P("seg", None, None),
            P(),
            P("seg", None, "seq"),
            P(),
            P(),
            P(),
            P(),
            P(),
            P(),
            P(),
            P("seg", "seq"),
            P(),
            P("seg", None, "seq"),
            P("seg", "seq"),
        ),
        check_vma=False,
    )
```

time: 2260 us -> 879 us (0.39)
  waiting for transfers between devices: 1610 us -> 527 us
  local copies, waits for them, and re-layouts: 278 us -> 97.1 us
  other arithmetic: 165 us -> 34.1 us
  matrix products: 146 us -> 98.9 us
  starting transfers between devices: 6.11 us -> 42.3 us
    reduce_scatter x4, waiting for transfers between devices: 848 us -> 206 us  [scatter_seg(): lax.psum_scatter(value.astype(BF), 'seg', scatter_dimension=0, tiled=True)]
    all_gather x8 -> x5, waiting for transfers between devices: 633 us -> 143 us  [the longest x4 143 us: gather_seg(): return lax.all_gather(value, 'seg', axis=0, tiled=True)]
    ppermute x2 -> x34, waiting for transfers between devices: 2.05 us -> 127 us  [swap(): lax.ppermute(value, 'seq', [(i, i ^ bit) for i in range(lax.axis_size('se...]
    concatenate x25 -> x12, other arithmetic: 86 us -> 5.24 us  [the longest x1 3.05 us: shards(): small = jnp.concatenate([small, sums[3:4], padded_grad[:edge_rows]], axis=0)]
    psum x2 -> x1, waiting for transfers between devices: 126 us -> 49.8 us  [shards(): lax.psum(jnp.concatenate(gate_grads + [taps_grad, conv_bias_grad, sums[:3...]
    slice x98 -> x33, local copies, waits for them, and re-layouts: 80.7 us -> 27.7 us  [the longest x1 7.79 us: shards(): small[at + kernel_taps + 3]]
    pad x48 -> x0, local copies, waits for them, and re-layouts: 50.5 us -> none  [the longest x24 25.8 us: shards(): lax.associative_scan(combine_pairs, (decays, drive_terms), axis=1)]
    psum x0 -> x1, blocking collectives: none -> 38.3 us  [shards(): lax.psum(jnp.stack([first_gain_grad, second_gain_grad]), ('seq', 'seg'))]
  transfers between devices with their start and end apart: 16 -> 44, of which waited for: 11 -> 33; matrix products, arithmetic and copies ran while one was open for 24% -> 17% of each run, Pallas kernels for 0% -> 1%
where the time goes in v1:
time: 879 us; the launch traced here: 872 us
  waiting for transfers between devices  527 us (60%)
  matrix products  98.9 us (11%)
  local copies, waits for them, and re-layouts  97.1 us (11%)
  starting transfers between devices  42.3 us (5%)
  blocking collectives  38.3 us (4%)
  other arithmetic  34.1 us (4%)
  Pallas kernels  19.4 us (2%)
  between operations  15.7 us (2%)
    reduce_scatter x4, waiting for transfers between devices, scatter_seg(): lax.psum_scatter(value.astype(BF), 'seg', scatter_dimension=0, tiled=True)  206 us
    all_gather x4, waiting for transfers between devices, gather_seg(): return lax.all_gather(value, 'seg', axis=0, tiled=True)  143 us
    ppermute x34, waiting for transfers between devices, swap(): lax.ppermute(value, 'seq', [(i, i ^ bit) for i in range(lax.axis_size('se...  127 us
    psum x1, waiting for transfers between devices, shards(): lax.psum(jnp.concatenate(gate_grads + [taps_grad, conv_bias_grad, sums[:3...  49.8 us
    unnamed x138, local copies, waits for them, and re-layouts  43.9 us
    ppermute x34, starting transfers between devices, swap(): lax.ppermute(value, 'seq', [(i, i ^ bit) for i in range(lax.axis_size('se...  41.9 us
    psum x1, blocking collectives, shards(): lax.psum(jnp.stack([first_gain_grad, second_gain_grad]), ('seq', 'seg'))  38.3 us
    dot_general x10, matrix products, contract_last(): lax.dot_general(left, right, (((1,), (1,)), ((), ())), preferred_element_...  32.2 us
  transfers between devices with their start and end apart: 44, of which 33 were waited for; matrix products, arithmetic and copies ran while one was open for 17% of the time, Pallas kernels for 1%

profile of v1, /device:TPU:0, one launch (start us, length us, event | category | flops | bytes accessed | tf_op | source)
XLA Modules:
  0.0 872.3 jit_solution(2309522969650137121)
XLA Ops:
  38.1 7.5 collective-permute-done.3
  47.1 22.0 %all-gather.6.cloned.1.call-done = bf16[2048,1280]{1,0:T(8,128)(2,1)} async-done(((bf16[256,1280]{1,0:T(8,128)(2,1)}), bf16[2048,1280]{1,0:T(8,128)(2,1)}) %all-gather.6.cloned.1.call-update) | async-done | bytes 5242896 | tf_op jit(solution)/shard_map/all_gather | solution.py:318
  87.1 11.7 %scan_forward.1 = (f32[512,640]{1,0:T(8,128)S(1)}, f32[512,640]{1,0:T(8,128)S(1)}, f32[512,640]{1,0:T(8,128)S(1)}, f32[512,640]{1,0:T(8,128)S(1)}, bf16[512,640]{1,0:T(8,128)(2,1)S(1)}) custom-call(s32[5]{0:T(128)S(1)} %and_select_fusion.blk_ref, bf16[512,768]{1,0:T(8,128)(2,1)S(1)} %maximum_select_fusion.1.low_ref, ...), custom_call_target="tpu_custom_call" | custom-call | flops 335544320 | bytes 9175040 | tf_op jit(solution)/shard_map/scan_forward/pallas_call | solution.py:138
  114.0 8.1 collective-permute-done.5
  153.1 68.3 %all-gather.10.cloned.1.call-done = bf16[2048,3072]{1,0:T(8,128)(2,1)} async-done(((bf16[256,3072]{1,0:T(8,128)(2,1)}), bf16[2048,3072]{1,0:T(8,128)(2,1)}) %all-gather.10.cloned.1.call-update) | async-done | bytes 12582928 | tf_op jit(solution)/shard_map/all_gather | solution.py:318
  221.3 11.9 %fusion.103 = f32[512,3072]{1,0:T(8,128)} fusion(bf16[512,2048]{1,0:T(8,128)(2,1)} %constant_dynamic-update-slice_fusion, bf16[2048,3072]{1,0:T(8,128)(2,1)} %all-gather.10.cloned.1.call-done), kind=kOutput, calls=%fused_computation.237 | convolution fusion | flops 6442450944 | bytes 20971520 | tf_op jit(solution)/shard_map/dot_general | solution.py:38
  233.2 52.6 %all-gather.12.cloned.1.call-done = bf16[2048,1536]{1,0:T(8,128)(2,1)} async-done(((bf16[256,1536]{1,0:T(8,128)(2,1)}), bf16[2048,1536]{1,0:T(8,128)(2,1)}) %all-gather.12.cloned.1.call-update) | async-done | bytes 6291472 | tf_op jit(solution)/shard_map/all_gather | solution.py:318
  285.9 11.7 %fusion.6 = (bf16[512,1536]{1,0:T(8,128)(2,1)S(1)}, bf16[512,1536]{1,0:T(8,128)(2,1)S(1)}, bf16[512,1536]{1,0:T(8,128)(2,1)}) fusion(f32[512,3072]{1,0:T(8,128)} %fusion.103, bf16[512,2048]{1,0:T(8,128)(2,1)} %constant_dynamic-update-slice_fusion.5, bf16[2048,1536]{1,0:T(8,128)(2,1)} %all-gather.12.cloned.1.call-done), kind=kOutput, calls=%fused_computation.12 | convolution fusion | flops 3241672704 | bytes 19398656 | tf_op jit(solution)/shard_map/dot_general | solution.py:38
  297.6 11.2 %fusion.100 = (bf16[512,2048]{1,0:T(8,128)(2,1)S(1)}, f32[512,2048]{1,0:T(8,128)S(1)}) fusion(bf16[2048,3072]{1,0:T(8,128)(2,1)} %all-gather.10.cloned.1.call-done, bf16[512,1536]{1,0:T(8,128)(2,1)S(1)} %get-tuple-element.101, bf16[512,1536]{1,0:T(8,128)(2,1)S(1)} %get-tuple-element.100), kind=kOutput, calls=%fused_computation.234 | convolution fusion | flops 6449790976 | bytes 22020096 | tf_op jit(solution)/shard_map/dot_general | solution.py:30
  312.1 11.0 %collective-permute-done.21 = bf16[128,2048]{1,0:T(8,128)(2,1)S(1)} collective-permute-done((bf16[128,2048]{1,0:T(8,128)(2,1)S(1)}, bf16[128,2048]{1,0:T(8,128)(2,1)S(1)}, u32[]{:S(2)}, u32[]{:S(2)}) %collective-permute-start.21) | collective-permute-done | bytes 524320 | tf_op jit(solution)/shard_map/ppermute | solution.py:52
  343.4 8.5 collective-permute-done.26
  364.6 7.6 scan_backward.1
  419.3 49.8 %all-reduce.10.cloned.1.call-done = f32[520,640]{0,1:T(8,128)} async-done(((f32[520,640]{0,1:T(8,128)}), f32[520,640]{0,1:T(8,128)}) %all-reduce.10.cloned.1.call-update) | async-done | bytes 1331216 | tf_op jit(solution)/shard_map/psum | solution.py:445
  472.3 8.1 convolution_convert_fusion.2
  489.1 11.6 %convolution_convert_fusion = bf16[2048,3072]{1,0:T(8,128)(2,1)} fusion(bf16[512,2048]{1,0:T(8,128)(2,1)} %constant_dynamic-update-slice_fusion, bf16[512,1536]{1,0:T(8,128)(2,1)} %copy-done.57, bf16[512,1536]{1,0:T(8,128)(2,1)S(1)} %copy-done.56), kind=kOutput, calls=%fused_computation | convolution fusion | flops 6455033856 | bytes 17825792 | tf_op jit(solution)/shard_map/dot_general | solution.py:34
  511.0 9.4 %collective-permute-done.13 = bf16[128,2048]{1,0:T(8,128)(2,1)S(1)} collective-permute-done((bf16[128,2048]{1,0:T(8,128)(2,1)S(1)}, bf16[128,2048]{1,0:T(8,128)(2,1)S(1)}, u32[]{:S(2)}, u32[]{:S(2)}) %collective-permute-start.13) | collective-permute-done | bytes 524320 | tf_op jit(solution)/shard_map/ppermute | solution.py:52
  524.1 10.2 %collective-permute-done.14 = bf16[64,2048]{1,0:T(8,128)(2,1)S(1)} collective-permute-done((bf16[64,2048]{1,0:T(8,128)(2,1)S(1)}, bf16[64,2048]{1,0:T(8,128)(2,1)S(1)}, u32[]{:S(2)}, u32[]{:S(2)}) %collective-permute-start.14) | collective-permute-done | bytes 262176 | tf_op jit(solution)/shard_map/ppermute | solution.py:52
  548.8 13.1 %collective-permute-done.30 = bf16[128,2048]{1,0:T(8,128)(2,1)S(1)} collective-permute-done((bf16[128,2048]{1,0:T(8,128)(2,1)S(1)}, bf16[128,2048]{1,0:T(8,128)(2,1)S(1)}, u32[]{:S(2)}, u32[]{:S(2)}) %collective-permute-start.30) | collective-permute-done | bytes 524320 | tf_op jit(solution)/shard_map/ppermute | solution.py:52
  570.7 6.3 collective-permute-done.31
  582.2 38.3 %psum.15 = f32[2,2048]{1,0:T(2,128)S(1)} all-reduce(f32[2,2048]{1,0:T(2,128)S(1)} %pad_maximum_fusion.19), channel_id=1, replica_groups=mesh['seq'=4,'seg'=8] {'seq','seg'}, use_global_device_ids=true, to_apply=%region_12.13 | all-reduce | flops 4096 | bytes 32768 | tf_op jit(solution)/shard_map/psum | solution.py:457
  626.3 7.8 slice_reduce_fusion
  649.0 20.6 %reduce-scatter.11.cloned.1.call-done = bf16[256,1536]{1,0:T(8,128)(2,1)} async-done(((bf16[2048,1536]{1,0:T(8,128)(2,1)}), bf16[256,1536]{1,0:T(8,128)(2,1)}) %reduce-scatter.11.cloned.1.call-update) | async-done | bytes 786448 | tf_op jit(solution)/shard_map/reduce_scatter | solution.py:321
  672.0 58.1 %reduce-scatter.5.cloned.1.call-done = bf16[256,1280]{1,0:T(8,128)(2,1)} async-done(((bf16[2048,1280]{1,0:T(8,128)(2,1)}), bf16[256,1280]{1,0:T(8,128)(2,1)}) %reduce-scatter.5.cloned.1.call-update) | async-done | bytes 655376 | tf_op jit(solution)/shard_map/reduce_scatter | solution.py:321
  732.9 127.0 %reduce-scatter.9.cloned.1.call-done = bf16[256,3072]{1,0:T(8,128)(2,1)} async-done(((bf16[2048,3072]{1,0:T(8,128)(2,1)}), bf16[256,3072]{1,0:T(8,128)(2,1)}) %reduce-scatter.9.cloned.1.call-update) | async-done | bytes 1572880 | tf_op jit(solution)/shard_map/reduce_scatter | solution.py:321
  (367 shorter events, 264.1 us)
Async XLA Ops:
  7.2 61.8 %all-gather.6.cloned.1.call-start = ((), (), s32[]{:S(2)}) async-start(), calls=%async_computation.4 | async-start | bytes 5898240 | tf_op jit(solution)/shard_map/all_gather | solution.py:318
  9.4 95.4 %all-gather.8.cloned.1.call-start = ((), (), s32[]{:S(2)}) async-start(), calls=%async_computation.5 | async-start | bytes 2949120 | tf_op jit(solution)/shard_map/all_gather | solution.py:318
  10.1 211.2 %all-gather.10.cloned.1.call-start = ((), (), s32[]{:S(2)}) async-start(), calls=%async_computation.6 | async-start | bytes 14155776 | tf_op jit(solution)/shard_map/all_gather | solution.py:318
  11.6 274.3 %all-gather.12.cloned.1.call-start = ((), (), s32[]{:S(2)}) async-start(), calls=%async_computation.7 | async-start | bytes 7077888 | tf_op jit(solution)/shard_map/all_gather | solution.py:318
  13.6 19.2 %collective-permute-start = (bf16[128,2048]{1,0:T(8,128)(2,1)}, bf16[128,2048]{1,0:T(8,128)(2,1)}, u32[]{:S(2)}, u32[]{:S(2)}) collective-permute-start(bf16[128,2048]{1,0:T(8,128)(2,1)} %get-tuple-element.99), channel_id=1, source_target_pairs={{0,8},{8,0},{16,24},{24,16},{1,9},{9,1},{17,25},{25,17},{2,10},{10... | collective-permute-start | bytes 1572872 | tf_op jit(solution)/shard_map/ppermute | solution.py:52
  16.6 15.2 %collective-permute-start.1 = (bf16[128,2048]{1,0:T(8,128)(2,1)}, bf16[128,2048]{1,0:T(8,128)(2,1)}, u32[]{:S(2)}, u32[]{:S(2)}) collective-permute-start(bf16[128,2048]{1,0:T(8,128)(2,1)} %get-tuple-element.99), channel_id=1, source_target_pairs={{0,16},{8,24},{16,0},{24,8},{1,17},{9,25},{17,1},{25,9},{2,18},{10... | collective-permute-start | bytes 1572872 | tf_op jit(solution)/shard_map/ppermute | solution.py:52
  18.1 63.4 %collective-permute-start.17 = (bf16[128,2048]{1,0:T(8,128)(2,1)}, bf16[128,2048]{1,0:T(8,128)(2,1)}, u32[]{:S(2)}, u32[]{:S(2)}) collective-permute-start(bf16[128,2048]{1,0:T(8,128)(2,1)} %bitcast.7), channel_id=1, source_target_pairs={{0,8},{8,0},{16,24},{24,16},{1,9},{9,1},{17,25},{25,17},{2,10},{10... | collective-permute-start | bytes 1572872 | tf_op jit(solution)/shard_map/ppermute | solution.py:52
  18.6 66.0 %collective-permute-start.18 = (bf16[128,2048]{1,0:T(8,128)(2,1)}, bf16[128,2048]{1,0:T(8,128)(2,1)}, u32[]{:S(2)}, u32[]{:S(2)}) collective-permute-start(bf16[128,2048]{1,0:T(8,128)(2,1)} %bitcast.7), channel_id=1, source_target_pairs={{0,16},{8,24},{16,0},{24,8},{1,17},{9,25},{17,1},{25,9},{2,18},{10... | collective-permute-start | bytes 1572872 | tf_op jit(solution)/shard_map/ppermute | solution.py:52
  18.7 450.5 %all-reduce.10.cloned.1.call-start = ((), (), s32[]{:S(2)}) async-start(), calls=%async_computation.8 | async-start | bytes 3276800 | tf_op jit(solution)/shard_map/psum | solution.py:445
  83.2 53.0 %collective-permute-start.19 = (bf16[64,2048]{1,0:T(8,128)(2,1)}, bf16[64,2048]{1,0:T(8,128)(2,1)}, u32[]{:S(2)}, u32[]{:S(2)}) collective-permute-start(bf16[64,2048]{1,0:T(8,128)(2,1)} %slice.468), channel_id=1, source_target_pairs={{0,16},{8,24},{16,0},{24,8},{1,17},{9,25},{17,1},{25,9},{2,18},{10... | collective-permute-start | bytes 786440 | tf_op jit(solution)/shard_map/ppermute | solution.py:52
  86.3 51.5 %collective-permute-start.20 = (bf16[64,2048]{1,0:T(8,128)(2,1)}, bf16[64,2048]{1,0:T(8,128)(2,1)}, u32[]{:S(2)}, u32[]{:S(2)}) collective-permute-start(bf16[64,2048]{1,0:T(8,128)(2,1)} %slice.469), channel_id=1, source_target_pairs={{0,8},{8,0},{16,24},{24,16},{1,9},{9,1},{17,25},{25,17},{2,10},{10... | collective-permute-start | bytes 786440 | tf_op jit(solution)/shard_map/ppermute | solution.py:52
  111.4 13.9 %collective-permute-start.7 = (bf16[128,2048]{1,0:T(8,128)(2,1)S(1)}, bf16[128,2048]{1,0:T(8,128)(2,1)S(1)}, u32[]{:S(2)}, u32[]{:S(2)}) collective-permute-start(bf16[128,2048]{1,0:T(8,128)(2,1)S(1)} %pad_maximum_fusion.10), channel_id=1, source_target_pairs={{0,16},{8,24},{16,0},{24,8},{1,17},{9,25},{17,1},{25,9},{2,18},{10... | collective-permute-start | bytes 1572872 | tf_op jit(solution)/shard_map/ppermute | solution.py:52
  308.9 14.1 %collective-permute-start.21 = (bf16[128,2048]{1,0:T(8,128)(2,1)S(1)}, bf16[128,2048]{1,0:T(8,128)(2,1)S(1)}, u32[]{:S(2)}, u32[]{:S(2)}) collective-permute-start(bf16[128,2048]{1,0:T(8,128)(2,1)S(1)} %pad_maximum_fusion.13), channel_id=1, source_target_pairs={{0,8},{8,0},{16,24},{24,16},{1,9},{9,1},{17,25},{25,17},{2,10},{10... | collective-permute-start | bytes 1572872 | tf_op jit(solution)/shard_map/ppermute | solution.py:52
  310.5 14.3 %collective-permute-start.23 = (bf16[128,2048]{1,0:T(8,128)(2,1)S(1)}, bf16[128,2048]{1,0:T(8,128)(2,1)S(1)}, u32[]{:S(2)}, u32[]{:S(2)}) collective-permute-start(bf16[128,2048]{1,0:T(8,128)(2,1)S(1)} %pad_maximum_fusion.14), channel_id=1, source_target_pairs={{0,16},{8,24},{16,0},{24,8},{1,17},{9,25},{17,1},{25,9},{2,18},{10... | collective-permute-start | bytes 1572872 | tf_op jit(solution)/shard_map/ppermute | solution.py:52
  409.2 215.2 %reduce-scatter.7.cloned.1.call-start = ((), (), s32[]{:S(2)}) async-start(), calls=%async_computation.11 | async-start | bytes 2949120 | tf_op jit(solution)/shard_map/reduce_scatter | solution.py:321
  414.2 212.1 %all-gather.14.cloned.1.call-start = ((), (), s32[]{:S(2)}) async-start(), calls=%async_computation.9 | async-start | bytes 8192000 | tf_op jit(solution)/shard_map/all_gather | solution.py:449
  472.2 197.4 %reduce-scatter.11.cloned.1.call-start = ((), (), s32[]{:S(2)}) async-start(), calls=%async_computation.13 | async-start | bytes 7077888 | tf_op jit(solution)/shard_map/reduce_scatter | solution.py:321
  480.4 249.7 %reduce-scatter.5.cloned.1.call-start = ((), (), s32[]{:S(2)}) async-start(), calls=%async_computation.10 | async-start | bytes 5898240 | tf_op jit(solution)/shard_map/reduce_scatter | solution.py:321
  487.7 372.3 %reduce-scatter.9.cloned.1.call-start = ((), (), s32[]{:S(2)}) async-start(), calls=%async_computation.12 | async-start | bytes 14155776 | tf_op jit(solution)/shard_map/reduce_scatter | solution.py:321
  509.5 14.6 %collective-permute-start.15 = (bf16[128,2048]{1,0:T(8,128)(2,1)S(1)}, bf16[128,2048]{1,0:T(8,128)(2,1)S(1)}, u32[]{:S(2)}, u32[]{:S(2)}) collective-permute-start(bf16[128,2048]{1,0:T(8,128)(2,1)S(1)} %pad_maximum_fusion.12), channel_id=1, source_target_pairs={{0,16},{8,24},{16,0},{24,8},{1,17},{9,25},{17,1},{25,9},{2,18},{10... | collective-permute-start | bytes 1572872 | tf_op jit(solution)/shard_map/ppermute | solution.py:52
  520.6 13.8 %collective-permute-start.14 = (bf16[64,2048]{1,0:T(8,128)(2,1)S(1)}, bf16[64,2048]{1,0:T(8,128)(2,1)S(1)}, u32[]{:S(2)}, u32[]{:S(2)}) collective-permute-start(bf16[64,2048]{1,0:T(8,128)(2,1)S(1)} %fusion.39), channel_id=1, source_target_pairs={{0,16},{8,24},{16,0},{24,8},{1,17},{9,25},{17,1},{25,9},{2,18},{10... | collective-permute-start | bytes 786440 | tf_op jit(solution)/shard_map/ppermute | solution.py:52
  542.9 19.0 %collective-permute-start.30 = (bf16[128,2048]{1,0:T(8,128)(2,1)S(1)}, bf16[128,2048]{1,0:T(8,128)(2,1)S(1)}, u32[]{:S(2)}, u32[]{:S(2)}) collective-permute-start(bf16[128,2048]{1,0:T(8,128)(2,1)S(1)} %pad_maximum_fusion.15), channel_id=1, source_target_pairs={{0,8},{8,0},{16,24},{24,16},{1,9},{9,1},{17,25},{25,17},{2,10},{10... | collective-permute-start | bytes 1572872 | tf_op jit(solution)/shard_map/ppermute | solution.py:52
  545.6 23.0 %collective-permute-start.32 = (bf16[128,2048]{1,0:T(8,128)(2,1)S(1)}, bf16[128,2048]{1,0:T(8,128)(2,1)S(1)}, u32[]{:S(2)}, u32[]{:S(2)}) collective-permute-start(bf16[128,2048]{1,0:T(8,128)(2,1)S(1)} %pad_maximum_fusion.16), channel_id=1, source_target_pairs={{0,16},{8,24},{16,0},{24,8},{1,17},{9,25},{17,1},{25,9},{2,18},{10... | collective-permute-start | bytes 1572872 | tf_op jit(solution)/shard_map/ppermute | solution.py:52
  562.1 14.9 %collective-permute-start.31 = (bf16[64,2048]{1,0:T(8,128)(2,1)S(1)}, bf16[64,2048]{1,0:T(8,128)(2,1)S(1)}, u32[]{:S(2)}, u32[]{:S(2)}) collective-permute-start(bf16[64,2048]{1,0:T(8,128)(2,1)S(1)} %fusion.30), channel_id=1, source_target_pairs={{0,16},{8,24},{16,0},{24,8},{1,17},{9,25},{17,1},{25,9},{2,18},{10... | collective-permute-start | bytes 786440 | tf_op jit(solution)/shard_map/ppermute | solution.py:52
  (81 other events, 852.8 us)
Sparse Core Ops, SparseCore 0:
  10.3 58.7 all-gather.5
  70.7 32.5 all-gather.7
  105.5 115.7 all-gather.9
  222.8 62.9 all-gather.11
  409.4 59.7 all-reduce.9
  471.9 37.3 reduce-scatter.6
  511.1 86.9 all-gather.13
  600.4 69.1 reduce-scatter.10
  671.9 58.2 reduce-scatter.4
  732.3 127.5 reduce-scatter.8

commit v2 on v1

v2 whole, which is shorter than its diff:
```python
import jax
import jax.numpy as jnp
from jax import lax
from jax.experimental import pallas as pl
from jax.experimental.pallas import tpu as pltpu
from jax.sharding import PartitionSpec as P

EPSILON = 1e-06
RATE_SCALE = 8.0
LANES = 128
CHUNK = 64
BF = jnp.bfloat16
F32 = jnp.float32
ORDER = [(3, 0), (1, 0), (3, 1), (2, 1), (0, 0), (0, 1), (2, 0), (1, 1)]


def rms_norm(values, scale_gain):
    factor = lax.rsqrt(jnp.mean(values * values, axis=-1, keepdims=True) + EPSILON)
    return values * factor * scale_gain


def gelu_tanh(values):
    return jax.nn.gelu(values, approximate=True)


def gelu_back(values, grads):
    return jax.vjp(gelu_tanh, values)[1](grads)[0]


def contract_last(left, right):
    return lax.dot_general(left, right, (((1,), (1,)), ((), ())), preferred_element_type=F32)


def contract_first(left, right):
    return lax.dot_general(left, right, (((0,), (0,)), ((), ())), preferred_element_type=F32)


def contract(left, right):
    return jnp.dot(left, right, preferred_element_type=F32)


def conv_apply(padded, taps, offset):
    edge_rows = taps.shape[0] - 1
    length = padded.shape[-2] - edge_rows
    summed = padded[..., edge_rows:, :] * taps[0] + offset
    for back_step in range(1, taps.shape[0]):
        first = edge_rows - back_step
        summed = summed + padded[..., first : first + length, :] * taps[back_step]
    return summed


def swap(value, bit):
    return lax.ppermute(value, "seq", [(i, i ^ bit) for i in range(lax.axis_size("seq"))])


def gather_halves(value):
    half = value.shape[0] // 2
    one = swap(value, 1)
    two = swap(value, 2)
    return value, one, two, swap(one[:half], 2), swap(two[half:], 1)


def gather_seq(value):
    own, one, two, *three = gather_halves(value)
    return own, one, two, jnp.concatenate(three, axis=0)


def assemble_kernel(rows_ref, core_ref, own_ref, one_ref, two_ref, top_ref, bottom_ref, whole_ref, mine_ref, other_ref):
    half = top_ref.shape[0]
    blocks = {
        (0, 0): own_ref[:half], (0, 1): own_ref[half:], (1, 0): one_ref[:half], (1, 1): one_ref[half:],
        (2, 0): two_ref[:half], (2, 1): two_ref[half:], (3, 0): top_ref[...], (3, 1): bottom_ref[...],
    }
    for k, which in enumerate(ORDER):
        whole_ref[pl.ds(pl.multiple_of(rows_ref[k], half), half), :] = blocks[which]

    @pl.when(pl.program_id(1) == 0)
    def _():
        mine_ref[...] = whole_ref[...].T

    @pl.when(pl.program_id(1) == 1)
    def _():
        other_ref[...] = whole_ref[...].T


def assemble(rows, core, blocks, chips, name):
    length, width = 4 * blocks[0].shape[0], blocks[0].shape[1]
    part = width // (2 * chips)
    if part % LANES:
        return assemble_plain(rows, core, blocks, chips)

    def column(i, j, rows, core):
        return (0, 2 * i + (core[0] ^ j))

    def turned():
        return pl.BlockSpec((part, length), lambda i, j, *_: (i, 0))

    return pl.pallas_call(
        assemble_kernel,
        grid_spec=pltpu.PrefetchScalarGridSpec(
            num_scalar_prefetch=2,
            grid=(chips, 2),
            in_specs=[pl.BlockSpec((value.shape[0], part), column) for value in blocks],
            out_specs=[pl.BlockSpec((length, part), column), turned(), turned()],
        ),
        out_shape=[
            jax.ShapeDtypeStruct((length, width), BF),
            jax.ShapeDtypeStruct((width // 2, length), BF),
            jax.ShapeDtypeStruct((width // 2, length), BF),
        ],
        compiler_params=pltpu.CompilerParams(vmem_limit_bytes=32 * 2**20),
        cost_estimate=pl.CostEstimate(flops=0, bytes_accessed=6 * length * width, transcendentals=0),
        name=name,
    )(rows, core, *blocks)


def assemble_plain(rows, core, blocks, chips):
    own, one, two, top, bottom = blocks
    half = top.shape[0]
    halves = {
        (0, 0): own[:half], (0, 1): own[half:], (1, 0): one[:half], (1, 1): one[half:],
        (2, 0): two[:half], (2, 1): two[half:], (3, 0): top, (3, 1): bottom,
    }
    length, width = 8 * half, own.shape[1]
    whole = jnp.zeros((length, width), BF)
    for k, which in enumerate(ORDER):
        whole = lax.dynamic_update_slice_in_dim(whole, halves[which], rows[k], 0)
    turned = whole.T.reshape(chips, 2, width // (2 * chips), length)
    mine, other = (
        lax.dynamic_index_in_dim(turned, which, 1, False).reshape(width // 2, length)
        for which in (core[0], 1 - core[0])
    )
    return whole, mine, other


def scatter_halves(send_one, send_two, keep):
    half = send_one.shape[0] // 2
    from_one = swap(send_one, 1)
    from_two = swap(send_two, 2)
    pass_two = (keep[2 * half : 3 * half] + from_one[:half].astype(F32)).astype(BF)
    pass_one = (keep[3 * half :] + from_two[:half].astype(F32)).astype(BF)
    last_two = swap(pass_two, 2)
    last_one = swap(pass_one, 1)
    near = jnp.concatenate([from_one[half:], from_two[half:]], axis=0).astype(F32)
    far = jnp.concatenate([last_two, last_one], axis=0).astype(F32)
    return keep[: 2 * half] + near + far


def arranged_rows(place, half):
    return jnp.stack([((place ^ step) * 2 + part) * half for step, part in ORDER]).astype(jnp.int32)


def project_kernel(rows_ref, left_ref, right_ref, one_ref, two_ref, keep_ref, order_ref):
    half = left_ref.shape[0] // 8

    @pl.when(pl.program_id(0) == 0)
    def _():
        for k in range(8):
            first = pl.multiple_of(rows_ref[k], half)
            order_ref[k * half : (k + 1) * half, :] = left_ref[pl.ds(first, half), :]

    terms = contract_last(order_ref[...], right_ref[...])
    one_ref[...] = terms[: 2 * half].astype(BF)
    two_ref[...] = terms[2 * half : 4 * half].astype(BF)
    keep_ref[...] = terms[4 * half :]


def project(rows, left, right, column, name):
    length, depth = left.shape
    width = right.shape[0]
    tile = 512
    part = length // 4
    return pl.pallas_call(
        project_kernel,
        grid_spec=pltpu.PrefetchScalarGridSpec(
            num_scalar_prefetch=1,
            grid=(width // tile,),
            in_specs=[
                pl.BlockSpec((length, depth), lambda i, rows: (0, 0), pipeline_mode=pl.Buffered(1)),
                pl.BlockSpec((tile, depth), lambda i, rows: (i, column)),
            ],
            out_specs=[
                pl.BlockSpec((part, tile), lambda i, rows: (0, i)),
                pl.BlockSpec((part, tile), lambda i, rows: (0, i)),
                pl.BlockSpec((2 * part, tile), lambda i, rows: (0, i)),
                pl.BlockSpec((length, depth), lambda i, rows: (0, 0)),
            ],
        ),
        out_shape=[
            jax.ShapeDtypeStruct((part, width), BF),
            jax.ShapeDtypeStruct((part, width), BF),
            jax.ShapeDtypeStruct((2 * part, width), F32),
            jax.ShapeDtypeStruct((length, depth), BF),
        ],
        compiler_params=pltpu.CompilerParams(vmem_limit_bytes=40 * 2**20),
        cost_estimate=pl.CostEstimate(
            flops=2 * length * depth * width,
            bytes_accessed=2 * width * depth + 8 * length * width,
            transcendentals=0,
        ),
        name=name,
    )(rows, left, right)


def swap_core(value):
    return lax.ppermute(value, "seg", [(i, i ^ 1) for i in range(lax.axis_size("seg"))])


def along(value, sources, step):
    pairs = [(2 * i + core, 2 * (i + step) + core) for i in sources for core in range(2)]
    return lax.ppermute(value, "seg", pairs)


def short_chain():
    return lax.axis_size("seg") == 8


def gather_chain(block):
    if not short_chain():
        return lax.all_gather(block, "seg", axis=0, tiled=True)
    place, core = lax.axis_index("seg") // 2, lax.axis_index("seg") % 2
    up, down = [block], [block]
    for hop in range(1, 4):
        up.append(along(up[-1], range(hop - 1, 3), 1))
        down.append(along(down[-1], range(1, 5 - hop), -1))
    held = [
        block,
        jnp.where(place <= 2, down[1], up[3]),
        jnp.where(place >= 2, up[2], down[2]),
        jnp.where(place >= 1, up[1], down[3]),
    ]
    rows = block.shape[0]
    whole = jnp.zeros((8 * rows,) + block.shape[1:], block.dtype)
    for step, value in enumerate(held):
        first = ((place + step) % 4) * 2
        whole = lax.dynamic_update_slice_in_dim(whole, value, (first + core) * rows, 0)
        other = swap_core(value)
        whole = lax.dynamic_update_slice_in_dim(whole, other, (first + 1 - core) * rows, 0)
    return whole


def scatter_chain(value, stages=(None,) * 3):
    if not short_chain():
        summed = lax.psum_scatter(value.astype(BF), "seg", scatter_dimension=0, tiled=True)
        return summed.astype(F32)
    place, core = lax.axis_index("seg") // 2, lax.axis_index("seg") % 2
    rows = value.shape[0] // 8
    value = value.astype(BF).reshape(4, 2, rows, value.shape[1])

    def of_core(which):
        return lax.dynamic_index_in_dim(value, which, 1, False)

    paired = of_core(core).astype(F32) + swap_core(of_core(1 - core)).astype(F32)
    paired = paired.astype(BF)

    def block(index):
        return lax.dynamic_index_in_dim(paired, jnp.clip(index, 0, 3), 0, False)

    up = down = None
    for hop in range(1, 4):
        rising, falling = block(4 - hop + place), block(place - 4 + hop)
        stage = stages[hop - 1]
        if stage is not None and hop == 1:
            rising, falling = after(rising, stage), after(falling, stage)
        if stage is not None and hop > 1:
            up, down = after(up, stage), after(down, stage)
        if hop > 1:
            rising = (rising.astype(F32) + up.astype(F32)).astype(BF)
            falling = (falling.astype(F32) + down.astype(F32)).astype(BF)
        up = along(rising, range(hop), 1)
        down = along(falling, range(4 - hop, 4), -1)
    return block(place).astype(F32) + up.astype(F32) + down.astype(F32)


def sum_small(value):
    core = lax.axis_index("seg") % 2
    mine = lax.dynamic_index_in_dim(value, core, 0, False)
    if not short_chain():
        return lax.dynamic_index_in_dim(lax.psum(value, "seg"), core, 0, False)
    total = mine.astype(F32) + swap_core(lax.dynamic_index_in_dim(value, 1 - core, 0, False)).astype(F32)
    for bit in (2, 4):
        low = total.astype(BF)
        other = lax.ppermute(low, "seg", [(i, i ^ bit) for i in range(8)])
        total = low.astype(F32) + other.astype(F32)
    return total.astype(BF)


def sum_all(value):
    if not short_chain():
        return lax.psum(value, ("seq", "seg"))
    for axis, bits in (("seg", (1, 2, 4)), ("seq", (1, 2))):
        for bit in bits:
            pairs = [(i, i ^ bit) for i in range(lax.axis_size(axis))]
            value = value + lax.ppermute(value, axis, pairs)
    return value


def after(value, earlier):
    return lax.optimization_barrier((value, earlier))[0]


def neg_expm1(values):
    total = 1.0 + values * (1.0 / 9.0)
    for order in range(8, 1, -1):
        total = 1.0 + values * (1.0 / order) * total
    return jnp.where(values > -0.7, -values * total, 1.0 - jnp.exp(values))


def scan_kernel(
    blk_ref, low_ref, wd_ref, wi_ref, par_ref, conv_ref, branch_ref,
    states_ref, decay_ref, rate_ref, open_ref, mixed_ref,
):
    length = conv_ref.shape[0]
    par = par_ref[...]
    soft = par[2:3]
    row = lax.broadcasted_iota(jnp.int32, (CHUNK // 8, 8, LANES), 1)

    def body(step, carry):
        rows = pl.ds(pl.multiple_of(step * CHUNK, CHUNK), CHUNK)
        low = low_ref[rows, :]
        rate = jax.nn.sigmoid(contract(low, wd_ref[0]) + par[0:1])
        opened = jax.nn.sigmoid(contract(low, wi_ref[0]) + par[1:2])
        log_decay = -RATE_SCALE * rate * soft
        decay = jnp.exp(log_decay)
        drive = jnp.sqrt(neg_expm1(2.0 * log_decay)) * opened * conv_ref[rows, :]
        rate_ref[rows, :] = rate
        open_ref[rows, :] = opened
        decay_ref[rows, :] = decay
        prod = decay.reshape(CHUNK // 8, 8, LANES)
        total = drive.reshape(CHUNK // 8, 8, LANES)
        for shift in (1, 2, 4):
            inside = row >= shift
            moved = jnp.where(inside, pltpu.roll(total, shift, 1), 0.0)
            total = total + prod * moved
            prod = prod * jnp.where(inside, pltpu.roll(prod, shift, 1), 1.0)
        pieces = []
        for group in range(CHUNK // 8):
            piece = total[group] + prod[group] * carry
            carry = piece[7:8]
            pieces.append(piece)
        states = jnp.concatenate(pieces, axis=0)
        states_ref[rows, :] = states
        mixed_ref[rows, :] = (states * gelu_tanh(branch_ref[rows, :])).astype(BF)
        return carry

    lax.fori_loop(0, length // CHUNK, body, par[3:4])


def scan_forward(blk, conv_ext, decay_w, input_w, params, conv_out, projected):
    length, width = conv_out.shape
    tiles = width // LANES
    tile = pl.BlockSpec((length, LANES), lambda i, blk: (0, i))
    weight = pl.BlockSpec((1, decay_w.shape[1], LANES), lambda i, blk: (i, 0, 0))
    whole = jax.ShapeDtypeStruct((length, width), F32)
    return pl.pallas_call(
        scan_kernel,
        grid_spec=pltpu.PrefetchScalarGridSpec(
            num_scalar_prefetch=1,
            grid=(tiles,),
            in_specs=[
                pl.BlockSpec((length, decay_w.shape[1]), lambda i, blk: (0, blk[i])),
                weight,
                weight,
                pl.BlockSpec((8, LANES), lambda i, blk: (0, i)),
                tile,
                tile,
            ],
            out_specs=[tile] * 5,
        ),
        out_shape=[whole, whole, whole, whole, jax.ShapeDtypeStruct((length, width), BF)],
        compiler_params=pltpu.CompilerParams(vmem_limit_bytes=32 * 2**20),
        cost_estimate=pl.CostEstimate(
            flops=4 * length * width * 256, bytes_accessed=length * width * 28, transcendentals=0
        ),
        name="scan_forward",
    )(blk, conv_ext, decay_w, input_w, params, conv_out, projected)


def back_kernel(
    rows_ref, strip_ref, par_ref, mixer_ref, out_w_ref, branch_ref, states_ref, decay_ref, rate_ref, open_ref, conv_ref,
    proj_out, gate_out, input_out, direct_out, sums_out, strips_out, mixed_ref,
):
    length = conv_ref.shape[0]
    groups = CHUNK // 8
    par = par_ref[...]
    soft = par[2:3]
    row = lax.broadcasted_iota(jnp.int32, (groups, 8, LANES), 1)
    flat_row = lax.broadcasted_iota(jnp.int32, (CHUNK, LANES), 0)
    steps = length // CHUNK
    half = length // 8
    mixed = contract(mixer_ref[...], out_w_ref[...])
    for k in range(8):
        mixed_ref[pl.ds(pl.multiple_of(rows_ref[k], half), half), :] = mixed[k * half : (k + 1) * half]

    def body(turn, carried):
        carry, gate_sum, input_sum, logit_sum = carried
        step = steps - 1 - turn
        first = pl.multiple_of(step * CHUNK, CHUNK)
        rows = pl.ds(first, CHUNK)
        mixed_grad = mixed_ref[rows, :]
        branch = branch_ref[rows, :]
        states = states_ref[rows, :]
        decay = decay_ref[rows, :]
        branch_act, pull = jax.vjp(gelu_tanh, branch)
        proj_out[rows, :] = pull(mixed_grad * states)[0].astype(BF)
        state_grad = mixed_grad * branch_act
        prod = decay.reshape(groups, 8, LANES)
        total = (decay * state_grad).reshape(groups, 8, LANES)
        for shift in (1, 2, 4):
            inside = row < 8 - shift
            moved = jnp.where(inside, pltpu.roll(total, 8 - shift, 1), 0.0)
            total = total + prod * moved
            prod = prod * jnp.where(inside, pltpu.roll(prod, 8 - shift, 1), 1.0)
        pieces = [None] * groups
        after = carry
        for group in reversed(range(groups)):
            piece = total[group] + prod[group] * after
            after = piece[0:1]
            pieces[group] = piece
        passed = jnp.concatenate(pieces, axis=0)
        shifted = jnp.where(flat_row == CHUNK - 1, carry, pltpu.roll(passed, CHUNK - 1, 0))
        adjoint = state_grad + shifted
        before = states_ref[pl.ds(pl.multiple_of(jnp.maximum(first - 8, 0), 8), 8), :][7:8]
        before = jnp.where(step == 0, par[3:4], before)
        previous = jnp.where(flat_row == 0, before, pltpu.roll(states, 1, 0))
        rate = rate_ref[rows, :]
        opened = open_ref[rows, :]
        conv = conv_ref[rows, :]
        log_decay = -RATE_SCALE * rate * soft
        scale = jnp.sqrt(neg_expm1(2.0 * log_decay))
        opened_conv = opened * conv
        log_grad = decay * (adjoint * previous - adjoint * opened_conv * (decay / scale))
        scaled = adjoint * scale
        direct_out[rows, :] = scaled * opened
        input_grad = (scaled * conv * opened * (1.0 - opened)).astype(BF)
        rate_grad = log_grad * rate
        gate_grad = (rate_grad * (1.0 - rate) * (-RATE_SCALE * soft)).astype(BF)
        gate_out[rows, :] = gate_grad
        input_out[rows, :] = input_grad

        def folded(value):
            return jnp.sum(value.astype(F32).reshape(groups, 8, LANES), axis=0)

        return (
            after,
            gate_sum + folded(gate_grad),
            input_sum + folded(input_grad),
            logit_sum + folded(rate_grad),
        )

    zero = jnp.zeros((8, LANES), F32)
    after, gate_sum, input_sum, logit_sum = lax.fori_loop(
        0, steps, body, (jnp.zeros((1, LANES), F32), zero, zero, zero)
    )
    sums_out[...] = jnp.concatenate(
        [
            jnp.sum(gate_sum, axis=0, keepdims=True),
            jnp.sum(input_sum, axis=0, keepdims=True),
            jnp.sum(logit_sum, axis=0, keepdims=True) * (-RATE_SCALE * par[4:5]),
            after,
            jnp.zeros((4, LANES), F32),
        ],
        axis=0,
    )

    @pl.when(pl.program_id(0) == strip_ref[0])
    def _():
        strips_out[0] = gate_out[...]
        strips_out[1] = input_out[...]


def scan_backward(rows, strip_tile, params, mixer_grad, recur, projected, states, decays, rate, opened, conv_out):
    length, width = conv_out.shape
    tiles = width // LANES
    out_tile = recur.shape[1] // LANES - tiles
    tile = pl.BlockSpec((length, LANES), lambda i, *_: (0, i))
    small = pl.BlockSpec((8, LANES), lambda i, *_: (0, i))
    low = jax.ShapeDtypeStruct((length, width), BF)
    return pl.pallas_call(
        back_kernel,
        grid_spec=pltpu.PrefetchScalarGridSpec(
            num_scalar_prefetch=2,
            grid=(tiles,),
            in_specs=[
                small,
                pl.BlockSpec(mixer_grad.shape, lambda i, *_: (0, 0), pipeline_mode=pl.Buffered(1)),
                pl.BlockSpec((recur.shape[0], LANES), lambda i, *_: (0, out_tile + i)),
            ]
            + [tile] * 6,
            out_specs=[tile] * 4 + [small, pl.BlockSpec((2, length, LANES), lambda i, *_: (0, 0, 0))],
            scratch_shapes=[pltpu.VMEM((length, LANES), F32)],
        ),
        out_shape=[
            jax.ShapeDtypeStruct((length, 2 * width), BF),
            low,
            low,
            jax.ShapeDtypeStruct((length, width), F32),
            jax.ShapeDtypeStruct((8, width), F32),
            jax.ShapeDtypeStruct((2, length, LANES), BF),
        ],
        compiler_params=pltpu.CompilerParams(vmem_limit_bytes=40 * 2**20),
        cost_estimate=pl.CostEstimate(
            flops=2 * length * width * recur.shape[0], bytes_accessed=length * width * 44, transcendentals=0
        ),
        name="scan_backward",
    )(rows, strip_tile, params, mixer_grad, recur, projected, states, decays, rate, opened, conv_out)


def gates_kernel(
    blk_ref, near_ref, edge_ref, par_ref, sums_ref, gate_ref, gate_near, input_ref, input_near, strips_ref,
    wd_ref, wi_ref, direct_ref, low_t_ref, conv_in_ref, proj_in, proj_out, small_out, single_out,
):
    length = direct_ref.shape[0]
    block = low_t_ref.shape[0]
    edge = edge_ref[pl.program_id(0)] == 1
    gate, opened = gate_ref[...], input_ref[...]
    gate_both = jnp.concatenate([gate, jnp.where(edge, strips_ref[0], gate_near[...])], axis=1)
    input_both = jnp.concatenate([opened, jnp.where(edge, strips_ref[1], input_near[...])], axis=1)
    conv_grad = direct_ref[...] + contract_last(gate_both, wd_ref[0]) + contract_last(input_both, wi_ref[0])
    row = lax.broadcasted_iota(jnp.int32, (length, LANES), 0)
    par = par_ref[...]
    conv_in = conv_in_ref[...]
    conv_in_grad = par[0:1] * conv_grad
    tap_sums = [jnp.sum(conv_grad * conv_in, axis=0, keepdims=True)]
    for k in range(1, 4):
        moved = jnp.where(row < length - k, pltpu.roll(conv_grad, length - k, 0), 0.0)
        conv_in_grad = conv_in_grad + par[k : k + 1] * moved
        total = jnp.sum(moved * conv_in, axis=0, keepdims=True)
        for t in range(k):
            total = total + conv_grad[t : t + 1] * par[7 + t - k : 8 + t - k]
        tap_sums.append(total)
    proj_out[...] = conv_in_grad.astype(BF)
    window = []
    for s in range(3):
        total = par[3 - s : 4 - s] * conv_grad[0:1]
        for k in range(4 - s, 4):
            total = total + par[k : k + 1] * conv_grad[s - 3 + k : s - 2 + k]
        window.append(total)
    sums = sums_ref[...]
    zero = jnp.zeros((8, LANES), F32)
    vectors = jnp.concatenate(
        tap_sums + [jnp.sum(conv_grad, axis=0, keepdims=True), sums[0:3], zero], axis=0
    ).astype(BF)
    low_t = low_t_ref[...]
    small_out[0, :block, :] = contract(low_t, gate).astype(BF)
    small_out[1, :block, :] = contract(low_t, opened).astype(BF)
    small_out[0, block:, :] = vectors
    small_out[1, block:, :] = vectors
    single_out[...] = jnp.concatenate([sums[3:4]] + window + [zero, zero[:4]], axis=0).astype(BF)


def gates_backward(blk, near, edge, params, sums, gate, opened, strips, decay_w, input_w, direct, low_t, projected, proj):
    length, width = direct.shape
    tiles = width // LANES
    block = decay_w.shape[2]
    tile = pl.BlockSpec((length, LANES), lambda i, *_: (0, i))
    beside = pl.BlockSpec((length, LANES), lambda i, blk, near, edge: (0, near[i]))
    small = pl.BlockSpec((8, LANES), lambda i, *_: (0, i))
    weight = pl.BlockSpec((1, LANES, block), lambda i, *_: (i, 0, 0))
    second = pl.BlockSpec((length, LANES), lambda i, *_: (0, tiles + i))
    return pl.pallas_call(
        gates_kernel,
        grid_spec=pltpu.PrefetchScalarGridSpec(
            num_scalar_prefetch=3,
            grid=(tiles,),
            in_specs=[
                small,
                small,
                tile,
                beside,
                tile,
                beside,
                pl.BlockSpec(strips.shape, lambda i, *_: (0, 0, 0)),
                weight,
                weight,
                tile,
                pl.BlockSpec((block, length), lambda i, blk, near, edge: (blk[i], 0)),
                second,
                pl.BlockSpec(memory_space=pl.ANY),
            ],
            out_specs=[
                second,
                pl.BlockSpec((2, block + 16, LANES), lambda i, *_: (0, 0, i)),
                pl.BlockSpec((16, LANES), lambda i, *_: (0, i)),
            ],
        ),
        out_shape=[
            jax.ShapeDtypeStruct(proj.shape, BF),
            jax.ShapeDtypeStruct((2, block + 16, width), BF),
            jax.ShapeDtypeStruct((16, width), BF),
        ],
        input_output_aliases={15: 0},
        compiler_params=pltpu.CompilerParams(vmem_limit_bytes=32 * 2**20),
        cost_estimate=pl.CostEstimate(
            flops=8 * length * width * block, bytes_accessed=length * width * 20, transcendentals=0
        ),
        name="gates_backward",
    )(blk, near, edge, params, sums, gate, gate, opened, opened, strips, decay_w, input_w, direct, low_t, projected, proj)


def mlp_data(tile, low_ref, cot_ref, weight_ref):
    gate_up = contract(low_ref[...], weight_ref[:, : 2 * tile])
    hidden_grad = contract(cot_ref[...], weight_ref[:, 2 * tile :])
    gate_val, up_val = gate_up[:, :tile], gate_up[:, tile:]
    gate_act, pull = jax.vjp(gelu_tanh, gate_val)
    hidden = (gate_act * up_val).astype(BF)
    gate_grad = pull(hidden_grad * up_val)[0].astype(BF)
    up_grad = (hidden_grad * gate_act).astype(BF)
    return jnp.concatenate([gate_grad, up_grad], axis=1), hidden


def add_term(total_ref, term):
    @pl.when(pl.program_id(0) == 0)
    def _():
        total_ref[...] = term

    @pl.when(pl.program_id(0) > 0)
    def _():
        total_ref[...] += term


def give_halves(total_ref, before_ref, one_ref, two_ref, keep_ref):
    @pl.when(pl.program_id(0) == pl.num_programs(0) - 1)
    def _():
        part = total_ref.shape[0] // 4
        one_ref[...] = (total_ref[:part] + before_ref[:part]).astype(BF)
        two_ref[...] = (total_ref[part : 2 * part] + before_ref[part : 2 * part]).astype(BF)
        keep_ref[...] = total_ref[2 * part :] + before_ref[2 * part :]


def mlp_first_kernel(tile, low_ref, cot_ref, weight_ref, units_ref, back_ref, out_ref):
    both, hidden = mlp_data(tile, low_ref, cot_ref, weight_ref)
    units_ref[:, : 2 * tile] = both
    units_ref[:, 2 * tile :] = hidden
    add_term(back_ref, contract_last(both, weight_ref[:, : 2 * tile]))
    add_term(out_ref, contract_last(hidden, weight_ref[:, 2 * tile :]))


def mlp_last_kernel(tile, low_ref, cot_ref, weight_ref, before_ref, units_ref, one_ref, two_ref, keep_ref, back_ref):
    both, hidden = mlp_data(tile, low_ref, cot_ref, weight_ref)
    units_ref[:, : 2 * tile] = both
    units_ref[:, 2 * tile :] = hidden
    add_term(back_ref, contract_last(both, weight_ref[:, : 2 * tile]))
    give_halves(back_ref, before_ref, one_ref, two_ref, keep_ref)


def mlp_out_kernel(tile, weight_ref, units_ref, before_ref, one_ref, two_ref, keep_ref, out_ref):
    add_term(out_ref, contract_last(units_ref[:, 2 * tile :], weight_ref[:, 2 * tile :]))
    give_halves(out_ref, before_ref, one_ref, two_ref, keep_ref)


def mlp_grad_kernel(tile, low_ref, low_other, cot_ref, cot_other, units_ref, units_other, grad_ref):
    cut = 2 * tile
    grad_ref[:, :cut] = (
        contract(low_ref[...], units_ref[:, :cut]) + contract(low_other[...], units_other[:, :cut])
    ).astype(BF)
    grad_ref[:, cut:] = (
        contract(cot_ref[...], units_ref[:, cut:]) + contract(cot_other[...], units_other[:, cut:])
    ).astype(BF)


def recur_grad_kernel(low_ref, low_other, mixer_ref, mixer_other, proj_ref, proj_other, mixed_ref, mixed_other, grad_ref):
    step = pl.program_id(0)

    @pl.when(step < 2)
    def _():
        grad_ref[...] = (
            contract(low_ref[...], proj_ref[...]) + contract(low_other[...], proj_other[...])
        ).astype(BF)

    @pl.when(step == 2)
    def _():
        grad_ref[...] = (
            contract(mixer_ref[...], mixed_ref[...]) + contract(mixer_other[...], mixed_other[...])
        ).astype(BF)


def recur_grad(low_t, mixer_t, proj, mixed):
    depth, length = low_t[0].shape
    width = mixed[0].shape[1]
    fixed = pl.BlockSpec((depth, length), lambda i: (0, 0), pipeline_mode=pl.Buffered(1))
    moving = pl.BlockSpec((length, width), lambda i: (0, jnp.minimum(i, 1)))
    whole = pl.BlockSpec((length, width), lambda i: (0, 0))
    return pl.pallas_call(
        recur_grad_kernel,
        grid=(3,),
        in_specs=[fixed] * 4 + [moving] * 2 + [whole] * 2,
        out_specs=pl.BlockSpec((depth, width), lambda i: (0, i)),
        out_shape=jax.ShapeDtypeStruct((depth, 3 * width), BF),
        compiler_params=pltpu.CompilerParams(vmem_limit_bytes=40 * 2**20),
        cost_estimate=pl.CostEstimate(
            flops=12 * depth * length * width, bytes_accessed=6 * depth * width + 8 * depth * length, transcendentals=0
        ),
        name="recur_grad",
    )(*low_t, *mixer_t, *proj, *mixed)


def mlp_call(kernel, tile, products, rows, width, columns, fixed_in, moving_in, fixed_out, moving_out, scratch, name):
    def fixed(shape, single):
        return pl.BlockSpec(shape, lambda i: (0, 0), pipeline_mode=pl.Buffered(1) if single else None)

    def moving(shape):
        return pl.BlockSpec((shape[0], 3 * tile), lambda i: (0, i))

    return pl.pallas_call(
        lambda *refs: kernel(tile, *refs),
        grid=(columns // (3 * tile),),
        in_specs=[
            fixed(value.shape, True) if kind == "fixed" else moving(value.shape)
            for kind, value in fixed_in + moving_in
        ],
        out_specs=[moving(shape) for shape, _ in moving_out] + [fixed(shape, False) for shape, _ in fixed_out],
        out_shape=[jax.ShapeDtypeStruct(shape, kind) for shape, kind in moving_out + fixed_out],
        scratch_shapes=[pltpu.VMEM(shape, kind) for shape, kind in scratch],
        compiler_params=pltpu.CompilerParams(vmem_limit_bytes=60 * 2**20),
        cost_estimate=pl.CostEstimate(
            flops=2 * products * rows * width * columns // 3,
            bytes_accessed=4 * width * columns + 16 * rows * width,
            transcendentals=0,
        ),
        name=name,
    )(*[value for _, value in fixed_in + moving_in])


def half_shapes(rows, width):
    part = rows // 4
    return [((part, width), BF), ((part, width), BF), ((2 * part, width), F32)]


def mlp_first(tile, low2, cot, weight):
    (rows, width), columns = low2.shape, weight.shape[1]
    ins = [("fixed", low2), ("fixed", cot), ("moving", weight)]
    return mlp_call(
        mlp_first_kernel, tile, 6, rows, width, columns, ins, [],
        [((rows, width), F32)] * 2, [((rows, columns), BF)], [], "mlp_first",
    )


def mlp_last(tile, low2, cot, weight, before):
    (rows, width), columns = low2.shape, weight.shape[1]
    ins = [("fixed", low2), ("fixed", cot), ("moving", weight), ("fixed", before)]
    return mlp_call(
        mlp_last_kernel, tile, 5, rows, width, columns, ins, [],
        half_shapes(rows, width), [((rows, columns), BF)], [((rows, width), F32)], "mlp_last",
    )


def mlp_out_last(tile, weight, units, before):
    (width, columns), rows = weight.shape, units.shape[0]
    ins = [("moving", weight), ("moving", units), ("fixed", before)]
    return mlp_call(
        mlp_out_kernel, tile, 1, rows, width, columns, ins, [],
        half_shapes(rows, width), [], [((rows, width), F32)], "mlp_out",
    )


def mlp_grad(tile, low_t, cot_t, units):
    (depth, rows), columns = low_t[0].shape, units[0].shape[1]
    ins = [("fixed", value) for value in (*low_t, *cot_t)] + [("moving", value) for value in units]
    return mlp_call(
        mlp_grad_kernel, tile, 3, rows, 2 * depth, columns, ins, [],
        [], [((depth, columns), BF)], [], "mlp_grad",
    )[0]


def shards(
    tokens,
    cotangent,
    start_state,
    start_window,
    first_gain,
    recur_in,
    conv_taps,
    conv_bias,
    decay_gate,
    input_gate,
    decay_bias,
    input_bias,
    decay_logit,
    recur_out,
    second_gain,
    feed_in,
    feed_out,
):
    segments, length, model_width = tokens.shape
    recur_width = conv_taps.shape[1]
    head_count, block_size = decay_gate.shape[:2]
    edge_rows = conv_taps.shape[0] - 1
    seq_parts = lax.axis_size("seq")
    place = lax.axis_index("seq")
    own_rows, _, recur_part = recur_in.shape
    feed_part = feed_in.shape[2]
    first_channel = place * recur_part
    first_block = first_channel // block_size
    block_count = -(-recur_part // block_size)
    strip = block_count * block_size - recur_part
    odd = place % 2 == 1

    def own(value):
        return lax.dynamic_slice_in_dim(value, first_channel, recur_part, value.ndim - 1)

    def strip_of(value):
        return jnp.where(odd, value[:, :strip], value[:, recur_part - strip :])

    def gather_seg(value):
        return lax.all_gather(value, "seg", axis=0, tiled=True)

    seg_parts = lax.axis_size("seg")
    core = lax.axis_index("seg") % 2

    def scatter_rows(value):
        groups = [list(range(c, seg_parts, 2)) for c in range(2)]
        return lax.psum_scatter(value, "seg", scatter_dimension=0, tiled=True, axis_index_groups=groups)

    def gathered(value, rows, name):
        whole, mine, other = assemble(rows, core[None].astype(jnp.int32), gather_halves(value), seg_parts // 2, name)
        return whole, (mine, swap_core(other))

    def of_both(value):
        return value, swap_core(value)

    unit = 2 * LANES
    first_part = 2 * feed_part // 3 // unit * unit
    cuts = [(0, first_part), (first_part, feed_part)]

    def feed_columns(first, count):
        return [feed_in[:, 0, first : first + count], feed_in[:, 1, first : first + count], feed_out[:, first : first + count]]

    feeds = [
        jnp.concatenate([c for first in range(a, b, unit) for c in feed_columns(first, unit)], axis=1)
        for a, b in cuts
    ]
    recur = gather_seg(jnp.concatenate([recur_in[:, 0], recur_in[:, 1], recur_out], axis=1))
    feed_first = gather_seg(feeds[0])
    feed_last = gather_seg(feeds[1])

    inputs = tokens.astype(F32).reshape(length, model_width)
    upstream = cotangent.reshape(length, model_width)
    low1 = rms_norm(inputs, first_gain).astype(BF)
    rows = arranged_rows(place, length // 2)
    straight = jnp.arange(8, dtype=jnp.int32) * (length // 2)
    all_low1, low1_rows = gathered(low1, rows, "gather_low1")
    all_cot, cot_rows = gathered(upstream, straight, "gather_cot")

    taps = own(conv_taps)
    logit = own(decay_logit[None])
    params = jnp.concatenate(
        [
            own(decay_bias[None]),
            own(input_bias[None]),
            jax.nn.softplus(logit),
            own(start_state),
            jax.nn.sigmoid(logit),
            jnp.zeros((3, recur_part), F32),
        ],
        axis=0,
    )
    window = own(start_window)[0]
    conv_params = jnp.concatenate([taps, window, jnp.zeros((1, recur_part), F32)], axis=0)
    tiles = recur_part // LANES
    halves = block_size // LANES
    first_tile = jnp.where(odd, strip // LANES, 0)
    tile_place = first_tile + jnp.arange(tiles)
    tile_block = (tile_place // halves).astype(jnp.int32)
    near = (tile_place ^ 1) - first_tile
    edge = ((near < 0) | (near >= tiles)).astype(jnp.int32)
    near = jnp.clip(near, 0, tiles - 1).astype(jnp.int32)
    strip_tile = jnp.where(odd, 0, tiles - 1).astype(jnp.int32)[None]

    def gate_tiles(blocks):
        blocks = lax.dynamic_slice_in_dim(blocks, first_block, block_count, 0)
        columns = blocks.reshape(block_count, block_size, halves, LANES).transpose(0, 2, 1, 3)
        columns = columns.reshape(block_count * halves, block_size, LANES)
        lines = blocks.reshape(block_count * halves, LANES, block_size)
        turned = jnp.concatenate([lines[:, :, LANES:], lines[:, :, :LANES]], axis=2)
        swapped = (jnp.arange(block_count * halves) % 2 == 1)[:, None, None]
        lines = jnp.where(swapped, turned, lines)
        return (
            lax.dynamic_slice_in_dim(columns, first_tile, tiles, 0),
            lax.dynamic_slice_in_dim(lines, first_tile, tiles, 0),
        )

    decay_columns, decay_lines = gate_tiles(decay_gate)
    input_columns, input_lines = gate_tiles(input_gate)

    projected = contract(all_low1, recur[:, : 2 * recur_part])
    padded = jnp.concatenate([window, projected[:, recur_part:]], axis=0)
    conv_out = conv_apply(padded, taps, own(conv_bias[None]))
    conv_low = conv_out.astype(BF)
    arrived = swap(strip_of(conv_low), 1)
    conv_ext = jnp.where(
        odd,
        jnp.concatenate([arrived, conv_low], axis=1),
        jnp.concatenate([conv_low, arrived], axis=1),
    )
    states, decays, rate, opened, mixed_low = scan_forward(
        tile_block, conv_ext, decay_columns, input_columns, params, conv_out, projected
    )
    *pieces, mixed_low = project(rows, mixed_low, recur, 2, "mixer_out")
    residual = inputs + scatter_halves(*pieces)

    low2 = rms_norm(residual, second_gain).astype(BF)
    all_low2, low2_rows = gathered(low2, straight, "gather_low2")
    units, back_first, out_first = mlp_first(unit, all_low2, all_cot, feed_first)
    grad_first = scatter_rows(mlp_grad(unit, low2_rows, cot_rows, of_both(units)))
    units, *pieces = mlp_last(unit, all_low2, all_cot, feed_last, back_first)
    normed2_grad = scatter_halves(*pieces)
    mlp_out = scatter_halves(*mlp_out_last(unit, feed_last, units, out_first))
    units_last = units
    output = (residual + mlp_out).astype(BF).reshape(tokens.shape)
    residual_norm_grad, second_gain_grad = jax.vjp(rms_norm, residual, second_gain)[1](normed2_grad)
    residual_grad = upstream.astype(F32) + residual_norm_grad

    mixer_grad, mixer_rows = gathered(residual_grad.astype(BF), straight, "gather_mixer")
    proj_grad, gate_low_grad, input_low_grad, conv_direct, sums, strips = scan_backward(
        rows, strip_tile, params, mixer_grad, recur, projected, states, decays, rate, opened, conv_out
    )
    proj_grad, small, single = gates_backward(
        tile_block, near, edge, conv_params, sums, gate_low_grad, input_low_grad, swap(strips, 1),
        decay_lines, input_lines, conv_direct, conv_ext.T, projected, proj_grad,
    )
    *pieces, _ = project(rows, proj_grad, recur, 0, "normed1_grad")
    grad_last = mlp_grad(unit, low2_rows, cot_rows, of_both(after(units_last, sums)))
    grad_last = scatter_rows(after(grad_last, (grad_first, pieces[2])))
    normed1_grad = scatter_halves(*pieces)
    input_norm_grad, first_gain_grad = jax.vjp(rms_norm, inputs, first_gain)[1](normed1_grad)
    input_grad = (residual_grad + input_norm_grad).astype(BF).reshape(tokens.shape)

    recur_term = recur_grad(low1_rows, mixer_rows, of_both(proj_grad), of_both(mixed_low))
    recur_sum = scatter_rows(after(recur_term, (grad_last, normed1_grad)))

    def columns_of(which):
        return jnp.concatenate(
            [
                part[:, first : first + unit]
                for part in (grad_first, grad_last)
                for first in range(which * unit, part.shape[1], 3 * unit)
            ],
            axis=1,
        ).astype(F32)

    feed_in_grad = jnp.stack([columns_of(0), columns_of(1)], axis=1)
    feed_out_grad = columns_of(2)
    recur_sum = after(recur_sum, (feed_in_grad, feed_out_grad)).astype(F32)
    recur_in_grad, recur_out_grad = recur_sum[:, : 2 * recur_part], recur_sum[:, 2 * recur_part :]

    mine = gather_seq(jnp.concatenate([sum_small(small), single], axis=0))
    swapped = [jnp.where(odd, mine[i ^ 1], mine[i]) for i in range(4)]
    mine = jnp.concatenate([jnp.where(place >= 2, swapped[i ^ 2], swapped[i]) for i in range(4)], axis=1)
    vectors = mine[block_size:].astype(F32)
    other = swap_core(mine[:block_size])

    def as_blocks(which):
        value = jnp.where(core == which, mine[:block_size], other).astype(F32)
        return value.reshape(block_size, head_count, block_size).transpose(1, 0, 2)

    gains = sum_all(jnp.stack([first_gain_grad, second_gain_grad]))
    kernel_taps = conv_taps.shape[0]
    return (
        output,
        input_grad,
        vectors[16:17],
        vectors[17 : 17 + edge_rows][None],
        gains[0],
        recur_in_grad.reshape(own_rows, 2, recur_part),
        vectors[:kernel_taps],
        vectors[kernel_taps],
        as_blocks(0),
        as_blocks(1),
        vectors[kernel_taps + 1],
        vectors[kernel_taps + 2],
        vectors[kernel_taps + 3],
        recur_out_grad,
        gains[1],
        feed_in_grad,
        feed_out_grad,
    )


def solution(mesh):
    placed = (
        P("seg", "seq", None),
        P("seg", "seq", None),
        P("seg", None),
        P("seg", None, None),
        P(),
        P("seg", None, "seq"),
        P(),
        P(),
        P(),
        P(),
        P(),
        P(),
        P(),
        P("seg", "seq"),
        P(),
        P("seg", None, "seq"),
        P("seg", "seq"),
    )
    return jax.shard_map(
        shards,
        mesh=mesh,
        in_specs=placed,
        out_specs=(
            P("seg", "seq", None),
            P("seg", "seq", None),
            P("seg", None),
            P("seg", None, None),
            P(),
            P("seg", None, "seq"),
            P(),
            P(),
            P(),
            P(),
            P(),
            P(),
            P(),
            P("seg", "seq"),
            P(),
            P("seg", None, "seq"),
            P("seg", "seq"),
        ),
        check_vma=False,
    )
```

time: 879 us -> 560 us (0.64)
  waiting for transfers between devices: 527 us -> 226 us
  Pallas kernels: 19.4 us -> 131 us
  matrix products: 98.9 us -> 5.99 us
  blocking collectives: 38.3 us -> 0 us
    reduce_scatter x4 -> x3, waiting for transfers between devices: 206 us -> 18.8 us  [scatter_rows(): lax.psum_scatter(value, 'seg', scatter_dimension=0, tiled=True, axis_inde...]
    pallas_call x1 -> x14, Pallas kernels: 7.63 us -> 120 us  [the longest x5 72.9 us: mlp_call(): pl.pallas_call(lambda *refs: kernel(tile, *refs), grid=(columns // (3 * t...]
    all_gather x4 -> x3, waiting for transfers between devices: 143 us -> 55.7 us  [gather_seg(): return lax.all_gather(value, 'seg', axis=0, tiled=True)]
    dot_general x18 -> x0, matrix products: 68.1 us -> none  [the longest x10 32.2 us: contract_last(): lax.dot_general(left, right, (((1,), (1,)), ((), ())), preferred_element_...]
    psum x1 -> x0, waiting for transfers between devices: 49.8 us -> none  [shards(): lax.psum(jnp.concatenate(gate_grads + [taps_grad, conv_bias_grad, sums[:3...]
    ppermute x0 -> x17, waiting for transfers between devices: none -> 47.5 us  [the longest x2 32 us: sum_small(): other = lax.ppermute(low, 'seg', [(i, i ^ bit) for i in range(8)])]
    psum x1 -> x0, blocking collectives: 38.3 us -> none  [shards(): lax.psum(jnp.stack([first_gain_grad, second_gain_grad]), ('seq', 'seg'))]
    dot_general x4 -> x1, matrix products: 30.8 us -> 5.99 us  [contract(): return jnp.dot(left, right, preferred_element_type=F32)]
  transfers between devices with their start and end apart: 44 -> 61, of which waited for: 33 -> 35; matrix products, arithmetic and copies ran while one was open for 17% -> 15% of each run, Pallas kernels for 1% -> 24%
where the time goes in v2:
time: 560 us; the launch traced here: 555 us
  waiting for transfers between devices  226 us (40%)
  Pallas kernels  131 us (23%)
  local copies, waits for them, and re-layouts  98.8 us (18%)
  starting transfers between devices  47 us (8%)
  other arithmetic  31.1 us (6%)
  between operations  15.6 us (3%)
  matrix products  5.99 us (1%)
    ppermute x38, waiting for transfers between devices, swap(): lax.ppermute(value, 'seq', [(i, i ^ bit) for i in range(lax.axis_size('se...  103 us
    pallas_call x5, Pallas kernels, mlp_call(): pl.pallas_call(lambda *refs: kernel(tile, *refs), grid=(columns // (3 * t...  72.9 us
    unnamed x186, local copies, waits for them, and re-layouts  60.1 us
    all_gather x3, waiting for transfers between devices, gather_seg(): return lax.all_gather(value, 'seg', axis=0, tiled=True)  55.7 us
    ppermute x38, starting transfers between devices, swap(): lax.ppermute(value, 'seq', [(i, i ^ bit) for i in range(lax.axis_size('se...  41.7 us
    ppermute x2, waiting for transfers between devices, sum_small(): other = lax.ppermute(low, 'seg', [(i, i ^ bit) for i in range(8)])  32 us
    reduce_scatter x3, waiting for transfers between devices, scatter_rows(): lax.psum_scatter(value, 'seg', scatter_dimension=0, tiled=True, axis_inde...  18.8 us
    pallas_call x4, Pallas kernels, assemble(): pl.pallas_call(assemble_kernel, grid_spec=pltpu.PrefetchScalarGridSpec(nu...  13.4 us
  transfers between devices with their start and end apart: 61, of which 35 were waited for; matrix products, arithmetic and copies ran while one was open for 15% of the time, Pallas kernels for 24%

profile of v2, /device:TPU:0, one launch (start us, length us, event | category | flops | bytes accessed | tf_op | source)
XLA Modules:
  0.0 555.4 jit_solution(7540212886716190086)
XLA Ops:
  27.3 7.5 %collective-permute-done.one_ref = bf16[128,2048]{1,0:T(8,128)(2,1)S(1)} collective-permute-done((bf16[128,2048]{1,0:T(8,128)(2,1)S(1)}, bf16[128,2048]{1,0:T(8,128)(2,1)S(1)}, u32[]{:S(2)}, u32[]{:S(2)}) %collective-permute-start) | collective-permute-done | bytes 524320 | tf_op jit(solution)/shard_map/ppermute | solution.py:53
  49.9 42.4 %all-gather.4.cloned.1.call-done.right_ref.out_w_ref = bf16[2048,1920]{1,0:T(8,128)(2,1)} async-done(((bf16[256,1920]{1,0:T(8,128)(2,1)}), bf16[2048,1920]{1,0:T(8,128)(2,1)}) %all-gather.4.cloned.1.call-update) | async-done | bytes 7864336 | tf_op jit(solution)/shard_map/all_gather | solution.py:806
  92.3 6.0 %fusion.branch_ref.conv_in_ref = f32[512,1280]{1,0:T(8,128)S(1)} fusion(bf16[512,2048]{1,0:T(8,128)(2,1)} %copy-done.31, bf16[2048,1920]{1,0:T(8,128)(2,1)} %all-gather.4.cloned.1.call-done.right_ref.out_w_ref), kind=kOutput, calls=%fused_computation | convolution fusion | flops 2684354560 | bytes 9961472 | tf_op jit(solution)/shard_map/dot_general | solution.py:39
  102.8 5.9 %fusion.58 = (bf16[512,640]{0,1:T(8,128)(2,1)S(1)}, f32[512,640]{0,1:T(8,128)}) fusion(f32[640]{0:T(1024)S(1)} %get-tuple-element.154, f32[512,640]{0,1:T(8,128)} %copy.87, f32[3,640]{0,1:T(8,128)} %bitcast.164, f32[640]{0:T(1024)S(1)} %get-tuple-element.155, f32[640]{0:T(1024)S(1)} %get-tuple-element.156, f32[640]{0:T(1024)S(1)} %dynamic-slice.12, ...), kind=kLoop, calls=%fused_computation.195 | loop fusion | flops 3932160 | bytes 3297280 | tf_op jit(solution)/shard_map/convert_element_type | solution.py:889
  123.8 11.6 %scan_forward.1 = (f32[512,640]{1,0:T(8,128)S(1)}, f32[512,640]{1,0:T(8,128)S(1)}, f32[512,640]{1,0:T(8,128)S(1)}, f32[512,640]{1,0:T(8,128)S(1)}, bf16[512,640]{1,0:T(8,128)(2,1)S(1)}) custom-call(s32[5]{0:T(128)S(1)} %and_select_fusion.1.blk_ref, bf16[512,768]{1,0:T(8,128)(2,1)S(1)} %copy-done.10, bf16[5,256,128]{2,1,0:T(8,128)(2,1)S(1)} %copy-done.22, ...), custom_call_target="tpu_custom_call" | custom-call | flops 335544320 | bytes 9175040 | tf_op jit(solution)/shard_map/scan_forward/pallas_call | solution.py:355
  148.6 11.8 %collective-permute-done.5 = bf16[128,2048]{1,0:T(8,128)(2,1)S(1)} collective-permute-done((bf16[128,2048]{1,0:T(8,128)(2,1)S(1)}, bf16[128,2048]{1,0:T(8,128)(2,1)S(1)}, u32[]{:S(2)}, u32[]{:S(2)}) %collective-permute-start.5) | collective-permute-done | bytes 524320 | tf_op jit(solution)/shard_map/ppermute | solution.py:53
  174.3 8.5 %collective-permute-done.13.one_ref = bf16[128,2048]{1,0:T(8,128)(2,1)S(1)} collective-permute-done((bf16[128,2048]{1,0:T(8,128)(2,1)S(1)}, bf16[128,2048]{1,0:T(8,128)(2,1)S(1)}, u32[]{:S(2)}, u32[]{:S(2)}) %collective-permute-start.13) | collective-permute-done | bytes 524320 | tf_op jit(solution)/shard_map/ppermute | solution.py:53
  185.0 9.0 %collective-permute-done.9.one_ref = bf16[128,2048]{1,0:T(8,128)(2,1)S(1)} collective-permute-done((bf16[128,2048]{1,0:T(8,128)(2,1)S(1)}, bf16[128,2048]{1,0:T(8,128)(2,1)S(1)}, u32[]{:S(2)}, u32[]{:S(2)}) %collective-permute-start.9) | collective-permute-done | bytes 524320 | tf_op jit(solution)/shard_map/ppermute | solution.py:53
  210.8 29.6 %mlp_first.1 = (bf16[512,3072]{1,0:T(8,128)(2,1)}, f32[512,2048]{1,0:T(8,128)}, f32[512,2048]{1,0:T(8,128)}) custom-call(bf16[512,2048]{1,0:T(8,128)(2,1)} %copy-done.30, bf16[512,2048]{1,0:T(8,128)(2,1)} %copy-done.29, bf16[2048,3072]{1,0:T(8,128)(2,1)} %all-gather.8.cloned.1.call-done.refs_2_), custom_call_target="tpu_custom_call" | custom-call | flops 12884901888 | bytes 41943040 | tf_op jit(solution)/shard_map/mlp_first/pallas_call | solution.py:705
  241.0 6.5 %collective-permute-done.51.refs_3_ = bf16[1024,512]{1,0:T(8,128)(2,1)S(1)} collective-permute-done((bf16[1024,512]{1,0:T(8,128)(2,1)S(1)}, bf16[1024,512]{1,0:T(8,128)(2,1)S(1)}, u32[]{:S(2)}, u32[]{:S(2)}) %collective-permute-start.51) | collective-permute-done | bytes 1048608 | tf_op jit(solution)/shard_map/ppermute | solution.py:206
  249.8 11.3 %mlp_grad.3 = bf16[1024,3072]{1,0:T(8,128)(2,1)} custom-call(bf16[1024,512]{1,0:T(8,128)(2,1)} %copy-done.41, bf16[1024,512]{1,0:T(8,128)(2,1)} %copy-done.77, bf16[1024,512]{1,0:T(8,128)(2,1)} %copy-done.40, bf16[1024,512]{1,0:T(8,128)(2,1)} %copy-done.76, bf16[512,3072]{1,0:T(8,128)(2,1)} %get-tuple-element.107.refs_4_, ...), custom_call_target="tpu_custom_call" | custom-call | flops 6442450944 | bytes 41943040 | tf_op jit(solution)/shard_map/mlp_grad/pallas_call | solution.py:705
  261.2 13.3 %all-gather.6.cloned.1.call-done.refs_2_.refs_0_ = bf16[2048,1536]{1,0:T(8,128)(2,1)} async-done(((bf16[256,1536]{1,0:T(8,128)(2,1)}), bf16[2048,1536]{1,0:T(8,128)(2,1)}) %all-gather.6.cloned.1.call-update) | async-done | bytes 6291472 | tf_op jit(solution)/shard_map/all_gather | solution.py:806
  274.5 16.1 %mlp_last.1 = (bf16[512,1536]{1,0:T(8,128)(2,1)}, bf16[128,2048]{1,0:T(8,128)(2,1)}, bf16[128,2048]{1,0:T(8,128)(2,1)}, f32[256,2048]{1,0:T(8,128)}) custom-call(bf16[512,2048]{1,0:T(8,128)(2,1)} %copy-done.30, bf16[512,2048]{1,0:T(8,128)(2,1)} %copy-done.29, bf16[2048,1536]{1,0:T(8,128)(2,1)} %all-gather.6.cloned.1.call-done.refs_2_.refs_0_, ...), custom_call_target="tpu_custom_call" | custom-call | flops 5368709120 | bytes 29360128 | tf_op jit(solution)/shard_map/mlp_last/pallas_call | solution.py:705
  293.6 11.3 %collective-permute-done.21 = bf16[128,2048]{1,0:T(8,128)(2,1)S(1)} collective-permute-done((bf16[128,2048]{1,0:T(8,128)(2,1)}, bf16[128,2048]{1,0:T(8,128)(2,1)S(1)}, u32[]{:S(2)}, u32[]{:S(2)}) %collective-permute-start.21) | collective-permute-done | bytes 524320 | tf_op jit(solution)/shard_map/ppermute | solution.py:53
  318.9 10.8 %collective-permute-done.25.one_ref = bf16[128,2048]{1,0:T(8,128)(2,1)S(1)} collective-permute-done((bf16[128,2048]{1,0:T(8,128)(2,1)S(1)}, bf16[128,2048]{1,0:T(8,128)(2,1)S(1)}, u32[]{:S(2)}, u32[]{:S(2)}) %collective-permute-start.25) | collective-permute-done | bytes 524320 | tf_op jit(solution)/shard_map/ppermute | solution.py:53
  351.6 12.5 %scan_backward.1 = (bf16[512,1280]{1,0:T(8,128)(2,1)S(1)}, bf16[512,640]{1,0:T(8,128)(2,1)S(1)}, bf16[512,640]{1,0:T(8,128)(2,1)S(1)}, f32[512,640]{1,0:T(8,128)...) custom-call(s32[8]{0:T(128)S(1)} %stack.48.rows_ref, s32[1]{0:T(128)} %bitcast.30.strip_ref, ...), custom_call_target="tpu_custom_call" | custom-call | flops 1342177280 | bytes 14417920 | tf_op jit(solution)/shard_map/scan_backward/pallas_call | solution.py:479
  366.8 7.7 %collective-permute-done.29.strips_ref = bf16[2,512,128]{2,1,0:T(8,128)(2,1)S(1)} collective-permute-done((bf16[2,512,128]{2,1,0:T(8,128)(2,1)S(1)}, bf16[2,512,128]{2,1,0:T(8,128)(2,1)S(1)}, u32[]{:S(2)}, u32[]{:S(2)}) %collective-permute-start.29) | collective-permute-done | bytes 262176 | tf_op jit(solution)/shard_map/ppermute | solution.py:53
  389.6 7.4 %mlp_grad.2 = bf16[1024,1536]{1,0:T(8,128)(2,1)} custom-call(bf16[1024,512]{1,0:T(8,128)(2,1)} %copy-done.41, bf16[1024,512]{1,0:T(8,128)(2,1)} %copy-done.77, bf16[1024,512]{1,0:T(8,128)(2,1)} %copy-done.40, bf16[1024,512]{1,0:T(8,128)(2,1)} %copy-done.76, bf16[512,1536]{1,0:T(8,128)(2,1)} %get-tuple-element.106.refs_1_.refs_4_, ...), custom_call_target="tpu_custom_call" | custom-call | flops 3221225472 | bytes 29360128 | tf_op jit(solution)/shard_map/mlp_grad/pallas_call | solution.py:705
  399.3 8.4 %mlp_out.1 = (bf16[128,2048]{1,0:T(8,128)(2,1)}, bf16[128,2048]{1,0:T(8,128)(2,1)}, f32[256,2048]{1,0:T(8,128)}) custom-call(bf16[2048,1536]{1,0:T(8,128)(2,1)} %all-gather.6.cloned.1.call-done.refs_2_.refs_0_, bf16[512,1536]{1,0:T(8,128)(2,1)} %get-tuple-element.106.refs_1_.refs_4_, f32[512,2048]{1,0:T(8,128)} %get-tuple-element.73.refs_2_), custom_call_target="tpu_custom_call" | custom-call | flops 1073741824 | bytes 29360128 | tf_op jit(solution)/shard_map/mlp_out/pallas_call | solution.py:705
  412.9 9.2 %collective-permute-done.17 = bf16[128,2048]{1,0:T(8,128)(2,1)S(1)} collective-permute-done((bf16[128,2048]{1,0:T(8,128)(2,1)}, bf16[128,2048]{1,0:T(8,128)(2,1)S(1)}, u32[]{:S(2)}, u32[]{:S(2)}) %collective-permute-start.17) | collective-permute-done | bytes 524320 | tf_op jit(solution)/shard_map/ppermute | solution.py:53
  432.4 25.2 %collective-permute-done.35 = bf16[272,640]{1,0:T(8,128)(2,1)S(1)} collective-permute-done((bf16[272,640]{1,0:T(8,128)(2,1)S(1)}, bf16[272,640]{1,0:T(8,128)(2,1)S(1)}, u32[]{:S(2)}, u32[]{:S(2)}) %collective-permute-start.35) | collective-permute-done | bytes 348192 | tf_op jit(solution)/shard_map/ppermute | solution.py:283
  461.5 7.2 %recur_grad.1 = bf16[1024,1920]{1,0:T(8,128)(2,1)S(1)} custom-call(bf16[1024,512]{1,0:T(8,128)(2,1)S(1)} %copy-done.33, bf16[1024,512]{1,0:T(8,128)(2,1)} %collective-permute-done.46.low_other, bf16[1024,512]{1,0:T(8,128)(2,1)S(1)} %copy-done.37, bf16[1024,512]{1,0:T(8,128)(2,1)S(1)} %collective-permute-done.47.mixer_other, ...), custom_call_target="tpu_custom_call" | custom-call | flops 4026531840 | bytes 8126464 | tf_op jit(solution)/shard_map/recur_grad/pallas_call | solution.py:684
  470.7 6.8 %collective-permute-done.36 = bf16[272,640]{1,0:T(8,128)(2,1)S(1)} collective-permute-done((bf16[272,640]{1,0:T(8,128)(2,1)S(1)}, bf16[272,640]{1,0:T(8,128)(2,1)S(1)}, u32[]{:S(2)}, u32[]{:S(2)}) %collective-permute-start.36) | collective-permute-done | bytes 348192 | tf_op jit(solution)/shard_map/ppermute | solution.py:283
  525.5 18.8 %reduce-scatter.8.cloned.1.call-done = bf16[256,1920]{1,0:T(8,128)(2,1)} async-done(((bf16[1024,1920]{1,0:T(8,128)(2,1)}), bf16[256,1920]{1,0:T(8,128)(2,1)}) %reduce-scatter.8.cloned.1.call-update) | async-done | bytes 983056 | tf_op jit(solution)/shard_map/reduce_scatter | solution.py:813
  (416 shorter events, 235.1 us)
Async XLA Ops:
  7.2 85.1 %all-gather.4.cloned.1.call-start = ((), (), s32[]{:S(2)}) async-start(), calls=%async_computation.3 | async-start | bytes 8847360 | tf_op jit(solution)/shard_map/all_gather | solution.py:806
  11.7 199.1 %all-gather.8.cloned.1.call-start = ((), (), s32[]{:S(2)}) async-start(), calls=%async_computation.5 | async-start | bytes 14155776 | tf_op jit(solution)/shard_map/all_gather | solution.py:806
  18.3 256.2 %all-gather.6.cloned.1.call-start = ((), (), s32[]{:S(2)}) async-start(), calls=%async_computation.4 | async-start | bytes 7077888 | tf_op jit(solution)/shard_map/all_gather | solution.py:806
  19.0 378.0 %reduce-scatter.4.cloned.1.call-start = ((), (), s32[]{:S(2)}) async-start(), calls=%async_computation.6 | async-start | bytes 7864320 | tf_op jit(solution)/shard_map/reduce_scatter | solution.py:813
  20.0 14.9 %collective-permute-start = (bf16[128,2048]{1,0:T(8,128)(2,1)S(1)}, bf16[128,2048]{1,0:T(8,128)(2,1)S(1)}, u32[]{:S(2)}, u32[]{:S(2)}) collective-permute-start(bf16[128,2048]{1,0:T(8,128)(2,1)S(1)} %fusion.12.own_ref), channel_id=1, source_target_pairs={{0,8},{8,0},{16,24},{24,16},{1,9},{9,1},{17,25},{25,17},{2,10},{10... | collective-permute-start | bytes 1572872 | tf_op jit(solution)/shard_map/ppermute | solution.py:53
  163.8 18.9 %collective-permute-start.13 = (bf16[128,2048]{1,0:T(8,128)(2,1)S(1)}, bf16[128,2048]{1,0:T(8,128)(2,1)S(1)}, u32[]{:S(2)}, u32[]{:S(2)}) collective-permute-start(bf16[128,2048]{1,0:T(8,128)(2,1)S(1)} %bitcast.155), channel_id=1, source_target_pairs={{0,8},{8,0},{16,24},{24,16},{1,9},{9,1},{17,25},{25,17},{2,10},{10... | collective-permute-start | bytes 1572872 | tf_op jit(solution)/shard_map/ppermute | solution.py:53
  164.3 19.1 %collective-permute-start.14 = (bf16[128,2048]{1,0:T(8,128)(2,1)S(1)}, bf16[128,2048]{1,0:T(8,128)(2,1)S(1)}, u32[]{:S(2)}, u32[]{:S(2)}) collective-permute-start(bf16[128,2048]{1,0:T(8,128)(2,1)S(1)} %bitcast.156), channel_id=1, source_target_pairs={{0,16},{8,24},{16,0},{24,8},{1,17},{9,25},{17,1},{25,9},{2,18},{10... | collective-permute-start | bytes 1572872 | tf_op jit(solution)/shard_map/ppermute | solution.py:53
  172.1 21.9 %collective-permute-start.9 = (bf16[128,2048]{1,0:T(8,128)(2,1)S(1)}, bf16[128,2048]{1,0:T(8,128)(2,1)S(1)}, u32[]{:S(2)}, u32[]{:S(2)}) collective-permute-start(bf16[128,2048]{1,0:T(8,128)(2,1)S(1)} %multiply_convert_fusion.own_ref), channel_id=1, source_target_pairs={{0,8},{8,0},{16,24},{24,16},{1,9},{9,1},{17,25},{25,17},{2,10},{10... | collective-permute-start | bytes 1572872 | tf_op jit(solution)/shard_map/ppermute | solution.py:53
  173.7 20.9 %collective-permute-start.10 = (bf16[128,2048]{1,0:T(8,128)(2,1)S(1)}, bf16[128,2048]{1,0:T(8,128)(2,1)S(1)}, u32[]{:S(2)}, u32[]{:S(2)}) collective-permute-start(bf16[128,2048]{1,0:T(8,128)(2,1)S(1)} %multiply_convert_fusion.own_ref), channel_id=1, source_target_pairs={{0,16},{8,24},{16,0},{24,8},{1,17},{9,25},{17,1},{25,9},{2,18},{10... | collective-permute-start | bytes 1572872 | tf_op jit(solution)/shard_map/ppermute | solution.py:53
  182.8 15.4 %collective-permute-start.15 = (bf16[64,2048]{1,0:T(8,128)(2,1)S(1)}, bf16[64,2048]{1,0:T(8,128)(2,1)S(1)}, u32[]{:S(2)}, u32[]{:S(2)}) collective-permute-start(bf16[64,2048]{1,0:T(8,128)(2,1)S(1)} %slice.450), channel_id=1, source_target_pairs={{0,16},{8,24},{16,0},{24,8},{1,17},{9,25},{17,1},{25,9},{2,18},{10... | collective-permute-start | bytes 786440 | tf_op jit(solution)/shard_map/ppermute | solution.py:53
  183.4 16.2 %collective-permute-start.16 = (bf16[64,2048]{1,0:T(8,128)(2,1)S(1)}, bf16[64,2048]{1,0:T(8,128)(2,1)S(1)}, u32[]{:S(2)}, u32[]{:S(2)}) collective-permute-start(bf16[64,2048]{1,0:T(8,128)(2,1)S(1)} %slice.451), channel_id=1, source_target_pairs={{0,8},{8,0},{16,24},{24,16},{1,9},{9,1},{17,25},{25,17},{2,10},{10... | collective-permute-start | bytes 786440 | tf_op jit(solution)/shard_map/ppermute | solution.py:53
  261.2 209.5 %reduce-scatter.6.cloned.1.call-start = ((), (), s32[]{:S(2)}) async-start(), calls=%async_computation.7 | async-start | bytes 3932160 | tf_op jit(solution)/shard_map/reduce_scatter | solution.py:813
  364.1 25.4 %collective-permute-start.52 = (bf16[512,1536]{1,0:T(8,128)(2,1)S(1)}, bf16[512,1536]{1,0:T(8,128)(2,1)}, u32[]{:S(2)}, u32[]{:S(2)}) collective-permute-start(bf16[512,1536]{1,0:T(8,128)(2,1)S(1)} %copy-done.61), channel_id=1, source_target_pairs={{0,1},{1,0},{2,3},{3,2},{4,5},{5,4},{6,7},{7,6},{8,9},{9,8},{10,11... | collective-permute-start | bytes 4718600 | tf_op jit(solution)/shard_map/ppermute | solution.py:206
  397.0 147.3 %reduce-scatter.8.cloned.1.call-start = ((), (), s32[]{:S(2)}) async-start(), calls=%async_computation.8 | async-start | bytes 4915200 | tf_op jit(solution)/shard_map/reduce_scatter | solution.py:813
  399.2 60.4 %collective-permute-start.46 = (bf16[1024,512]{1,0:T(8,128)(2,1)S(1)}, bf16[1024,512]{1,0:T(8,128)(2,1)}, u32[]{:S(2)}, u32[]{:S(2)}) collective-permute-start(bf16[1024,512]{1,0:T(8,128)(2,1)S(1)} %copy-done.35), channel_id=1, source_target_pairs={{0,1},{1,0},{2,3},{3,2},{4,5},{5,4},{6,7},{7,6},{8,9},{9,8},{10,11... | collective-permute-start | bytes 3145736 | tf_op jit(solution)/shard_map/ppermute | solution.py:206
  410.9 49.0 %collective-permute-start.49 = (bf16[512,640]{1,0:T(8,128)(2,1)}, bf16[512,640]{1,0:T(8,128)(2,1)S(1)}, u32[]{:S(2)}, u32[]{:S(2)}) collective-permute-start(bf16[512,640]{1,0:T(8,128)(2,1)} %copy-done.43), channel_id=1, source_target_pairs={{0,1},{1,0},{2,3},{3,2},{4,5},{5,4},{6,7},{7,6},{8,9},{9,8},{10,11... | collective-permute-start | bytes 1966088 | tf_op jit(solution)/shard_map/ppermute | solution.py:206
  411.2 15.1 %collective-permute-start.34 = (bf16[272,640]{1,0:T(8,128)(2,1)S(1)}, bf16[272,640]{1,0:T(8,128)(2,1)S(1)}, u32[]{:S(2)}, u32[]{:S(2)}) collective-permute-start(bf16[272,640]{1,0:T(8,128)(2,1)S(1)} %dynamic-slice_bitcast_fusion), channel_id=1, source_target_pairs={{0,1},{1,0},{2,3},{3,2},{4,5},{5,4},{6,7},{7,6},{8,9},{9,8},{10,11... | collective-permute-start | bytes 1044488 | tf_op jit(solution)/shard_map/ppermute | solution.py:206
  426.4 35.1 %collective-permute-start.48 = (bf16[512,1280]{1,0:T(8,128)(2,1)S(1)}, bf16[512,1280]{1,0:T(8,128)(2,1)S(1)}, u32[]{:S(2)}, u32[]{:S(2)}) collective-permute-start(bf16[512,1280]{1,0:T(8,128)(2,1)S(1)} %copy-done.24), channel_id=1, source_target_pairs={{0,1},{1,0},{2,3},{3,2},{4,5},{5,4},{6,7},{7,6},{8,9},{9,8},{10,11... | collective-permute-start | bytes 3932168 | tf_op jit(solution)/shard_map/ppermute | solution.py:206
  430.2 29.7 %collective-permute-start.47 = (bf16[1024,512]{1,0:T(8,128)(2,1)S(1)}, bf16[1024,512]{1,0:T(8,128)(2,1)S(1)}, u32[]{:S(2)}, u32[]{:S(2)}) collective-permute-start(bf16[1024,512]{1,0:T(8,128)(2,1)S(1)} %copy-done.39), channel_id=1, source_target_pairs={{0,1},{1,0},{2,3},{3,2},{4,5},{5,4},{6,7},{7,6},{8,9},{9,8},{10,11... | collective-permute-start | bytes 3145736 | tf_op jit(solution)/shard_map/ppermute | solution.py:206
  431.0 26.6 %collective-permute-start.35 = (bf16[272,640]{1,0:T(8,128)(2,1)S(1)}, bf16[272,640]{1,0:T(8,128)(2,1)S(1)}, u32[]{:S(2)}, u32[]{:S(2)}) collective-permute-start(bf16[272,640]{1,0:T(8,128)(2,1)S(1)} %fusion.19), channel_id=1, source_target_pairs={{0,2},{1,3},{2,0},{3,1},{4,6},{5,7},{6,4},{7,5},{8,10},{9,11},{10,... | collective-permute-start | bytes 1044488 | tf_op jit(solution)/shard_map/ppermute | solution.py:283
  458.7 36.6 %collective-permute-start.19 = (bf16[64,2048]{1,0:T(8,128)(2,1)}, bf16[64,2048]{1,0:T(8,128)(2,1)}, u32[]{:S(2)}, u32[]{:S(2)}) collective-permute-start(bf16[64,2048]{1,0:T(8,128)(2,1)} %get-tuple-element.169), channel_id=1, source_target_pairs={{0,16},{8,24},{16,0},{24,8},{1,17},{9,25},{17,1},{25,9},{2,18},{10... | collective-permute-start | bytes 786440 | tf_op jit(solution)/shard_map/ppermute | solution.py:53
  459.7 35.6 %collective-permute-start.20 = (bf16[64,2048]{1,0:T(8,128)(2,1)}, bf16[64,2048]{1,0:T(8,128)(2,1)}, u32[]{:S(2)}, u32[]{:S(2)}) collective-permute-start(bf16[64,2048]{1,0:T(8,128)(2,1)} %get-tuple-element.170), channel_id=1, source_target_pairs={{0,8},{8,0},{16,24},{24,16},{1,9},{9,1},{17,25},{25,17},{2,10},{10... | collective-permute-start | bytes 786440 | tf_op jit(solution)/shard_map/ppermute | solution.py:53
  459.9 17.6 %collective-permute-start.36 = (bf16[272,640]{1,0:T(8,128)(2,1)S(1)}, bf16[272,640]{1,0:T(8,128)(2,1)S(1)}, u32[]{:S(2)}, u32[]{:S(2)}) collective-permute-start(bf16[272,640]{1,0:T(8,128)(2,1)S(1)} %add_convert_fusion.2), channel_id=1, source_target_pairs={{0,4},{1,5},{2,6},{3,7},{4,0},{5,1},{6,2},{7,3},{8,12},{9,13},{10,... | collective-permute-start | bytes 1044488 | tf_op jit(solution)/shard_map/ppermute | solution.py:283
  459.9 21.3 %collective-permute-start.42 = (f32[2,2048]{1,0:T(2,128)S(1)}, f32[2,2048]{1,0:T(2,128)S(1)}, u32[]{:S(2)}, u32[]{:S(2)}) collective-permute-start(f32[2,2048]{1,0:T(2,128)S(1)} %fusion.56), channel_id=1, source_target_pairs={{0,2},{1,3},{2,0},{3,1},{4,6},{5,7},{6,4},{7,5},{8,10},{9,11},{10,... | collective-permute-start | bytes 49160 | tf_op jit(solution)/shard_map/ppermute | solution.py:294
  (117 other events, 869.8 us)
Sparse Core Ops, SparseCore 0:
  11.8 80.4 all-gather.3
  94.5 115.2 all-gather.7
  211.5 62.9 all-gather.5
  276.7 109.3 reduce-scatter.3
  397.1 65.4 reduce-scatter.5
  470.8 73.4 reduce-scatter.7

commit v3 on v2

--- a/solution.py
+++ b/solution.py
@@ -215,64 +215,7 @@
     return lax.axis_size("seg") == 8
 
 
-def gather_chain(block):
-    if not short_chain():
-        return lax.all_gather(block, "seg", axis=0, tiled=True)
-    place, core = lax.axis_index("seg") // 2, lax.axis_index("seg") % 2
-    up, down = [block], [block]
-    for hop in range(1, 4):
-        up.append(along(up[-1], range(hop - 1, 3), 1))
-        down.append(along(down[-1], range(1, 5 - hop), -1))
-    held = [
-        block,
-        jnp.where(place <= 2, down[1], up[3]),
-        jnp.where(place >= 2, up[2], down[2]),
-        jnp.where(place >= 1, up[1], down[3]),
-    ]
-    rows = block.shape[0]
-    whole = jnp.zeros((8 * rows,) + block.shape[1:], block.dtype)
-    for step, value in enumerate(held):
-        first = ((place + step) % 4) * 2
-        whole = lax.dynamic_update_slice_in_dim(whole, value, (first + core) * rows, 0)
-        other = swap_core(value)
-        whole = lax.dynamic_update_slice_in_dim(whole, other, (first + 1 - core) * rows, 0)
-    return whole
-
-
-def scatter_chain(value, stages=(None,) * 3):
-    if not short_chain():
-        summed = lax.psum_scatter(value.astype(BF), "seg", scatter_dimension=0, tiled=True)
-        return summed.astype(F32)
-    place, core = lax.axis_index("seg") // 2, lax.axis_index("seg") % 2
-    rows = value.shape[0] // 8
-    value = value.astype(BF).reshape(4, 2, rows, value.shape[1])
-
-    def of_core(which):
-        return lax.dynamic_index_in_dim(value, which, 1, False)
-
-    paired = of_core(core).astype(F32) + swap_core(of_core(1 - core)).astype(F32)
-    paired = paired.astype(BF)
-
-    def block(index):
-        return lax.dynamic_index_in_dim(paired, jnp.clip(index, 0, 3), 0, False)
-
-    up = down = None
-    for hop in range(1, 4):
-        rising, falling = block(4 - hop + place), block(place - 4 + hop)
-        stage = stages[hop - 1]
-        if stage is not None and hop == 1:
-            rising, falling = after(rising, stage), after(falling, stage)
-        if stage is not None and hop > 1:
-            up, down = after(up, stage), after(down, stage)
-        if hop > 1:
-            rising = (rising.astype(F32) + up.astype(F32)).astype(BF)
-            falling = (falling.astype(F32) + down.astype(F32)).astype(BF)
-        up = along(rising, range(hop), 1)
-        down = along(falling, range(4 - hop, 4), -1)
-    return block(place).astype(F32) + up.astype(F32) + down.astype(F32)
-
-
-def sum_small(value):
+def sum_small(value, middle):
     core = lax.axis_index("seg") % 2
     mine = lax.dynamic_index_in_dim(value, core, 0, False)
     if not short_chain():
@@ -281,7 +224,7 @@
     for bit in (2, 4):
         low = total.astype(BF)
         other = lax.ppermute(low, "seg", [(i, i ^ bit) for i in range(8)])
-        total = low.astype(F32) + other.astype(F32)
+        total = low.astype(F32) + after(other, middle).astype(F32)
     return total.astype(BF)
 
 
@@ -659,7 +602,9 @@
     ).astype(BF)
 
 
-def recur_grad_kernel(low_ref, low_other, mixer_ref, mixer_other, proj_ref, proj_other, mixed_ref, mixed_other, grad_ref):
+def recur_grad_kernel(
+    low_ref, low_other, mixer_ref, mixer_other, proj_ref, proj_other, mixed_ref, mixed_other, held_ref, grad_ref
+):
     step = pl.program_id(0)
 
     @pl.when(step < 2)
@@ -675,7 +620,7 @@
         ).astype(BF)
 
 
-def recur_grad(low_t, mixer_t, proj, mixed):
+def recur_grad(low_t, mixer_t, proj, mixed, held):
     depth, length = low_t[0].shape
     width = mixed[0].shape[1]
     fixed = pl.BlockSpec((depth, length), lambda i: (0, 0), pipeline_mode=pl.Buffered(1))
@@ -684,15 +629,86 @@
     return pl.pallas_call(
         recur_grad_kernel,
         grid=(3,),
-        in_specs=[fixed] * 4 + [moving] * 2 + [whole] * 2,
+        in_specs=[fixed] * 4 + [moving] * 2 + [whole] * 2 + [pl.BlockSpec(memory_space=pl.ANY)],
         out_specs=pl.BlockSpec((depth, width), lambda i: (0, i)),
-        out_shape=jax.ShapeDtypeStruct((depth, 3 * width), BF),
+        out_shape=jax.ShapeDtypeStruct(held.shape, BF),
+        input_output_aliases={8: 0},
         compiler_params=pltpu.CompilerParams(vmem_limit_bytes=40 * 2**20),
         cost_estimate=pl.CostEstimate(
             flops=12 * depth * length * width, bytes_accessed=6 * depth * width + 8 * depth * length, transcendentals=0
         ),
         name="recur_grad",
-    )(*low_t, *mixer_t, *proj, *mixed)
+    )(*low_t, *mixer_t, *proj, *mixed, held)
+
+
+def mlp_grad_beside_kernel(
+    tile, first, low_ref, low_other, cot_ref, cot_other, units_ref, units_other, held_ref, grad_ref, sem
+):
+    mlp_grad_kernel(tile, low_ref, low_other, cot_ref, cot_other, units_ref, units_other, grad_ref)
+    columns = pl.ds(pl.multiple_of(first + pl.program_id(0) * 3 * tile, LANES), 3 * tile)
+    copy = pltpu.make_async_copy(grad_ref, held_ref.at[:, columns], sem)
+    copy.start()
+    copy.wait()
+
+
+def mlp_grad_beside(tile, low_t, cot_t, units, first):
+    (depth, rows), columns = low_t[0].shape, units[0].shape[1]
+    fixed = pl.BlockSpec((depth, rows), lambda i: (0, 0), pipeline_mode=pl.Buffered(1))
+    moving = pl.BlockSpec((rows, 3 * tile), lambda i: (0, i))
+    return pl.pallas_call(
+        lambda *refs: mlp_grad_beside_kernel(tile, first, *refs),
+        grid=(columns // (3 * tile),),
+        in_specs=[fixed] * 4 + [moving] * 2,
+        out_specs=pl.BlockSpec(memory_space=pl.ANY),
+        out_shape=jax.ShapeDtypeStruct((depth, first + columns), BF),
+        scratch_shapes=[pltpu.VMEM((depth, 3 * tile), BF), pltpu.SemaphoreType.DMA],
+        compiler_params=pltpu.CompilerParams(vmem_limit_bytes=40 * 2**20),
+        cost_estimate=pl.CostEstimate(
+            flops=4 * rows * depth * columns, bytes_accessed=2 * depth * columns + 8 * rows * depth, transcendentals=0
+        ),
+        name="mlp_grad_last",
+    )(*low_t, *cot_t, *units)
+
+
+def unpack_kernel(tile, first, sums_ref, in_held, out_held, feed_in_ref, feed_out_ref, recur_in_ref, recur_out_ref):
+    width = recur_out_ref.shape[1]
+    for i in range(2):
+        recur_in_ref[:, i, :] = sums_ref[:, i * width : (i + 1) * width].astype(F32)
+    recur_out_ref[...] = sums_ref[:, 2 * width : 3 * width].astype(F32)
+    for k in range(feed_out_ref.shape[1] // tile):
+        at = slice(k * tile, (k + 1) * tile)
+        start = first + 3 * tile * k
+        for i in range(2):
+            feed_in_ref[:, i, at] = sums_ref[:, start + i * tile : start + (i + 1) * tile].astype(F32)
+        feed_out_ref[:, at] = sums_ref[:, start + 2 * tile : start + 3 * tile].astype(F32)
+
+
+def unpack(tile, sums, feed_in, feed_out, recur_width, done):
+    rows = sums.shape[0]
+    units = feed_out.shape[1]
+    part = units - done
+    anywhere = pl.BlockSpec(memory_space=pl.ANY)
+    return pl.pallas_call(
+        lambda *refs: unpack_kernel(tile, 3 * recur_width, *refs),
+        grid=(1,),
+        in_specs=[pl.BlockSpec(sums.shape, lambda i: (0, 0)), anywhere, anywhere],
+        out_specs=[
+            pl.BlockSpec((rows, 2, part), lambda i: (0, 0, done // part)),
+            pl.BlockSpec((rows, part), lambda i: (0, done // part)),
+            pl.BlockSpec((rows, 2, recur_width), lambda i: (0, 0, 0)),
+            pl.BlockSpec((rows, recur_width), lambda i: (0, 0)),
+        ],
+        out_shape=[
+            jax.ShapeDtypeStruct(feed_in.shape, F32),
+            jax.ShapeDtypeStruct(feed_out.shape, F32),
+            jax.ShapeDtypeStruct((rows, 2, recur_width), F32),
+            jax.ShapeDtypeStruct((rows, recur_width), F32),
+        ],
+        input_output_aliases={1: 0, 2: 1},
+        compiler_params=pltpu.CompilerParams(vmem_limit_bytes=40 * 2**20),
+        cost_estimate=pl.CostEstimate(flops=0, bytes_accessed=6 * rows * sums.shape[1], transcendentals=0),
+        name="unpack",
+    )(sums, feed_in, feed_out)
 
 
 def mlp_call(kernel, tile, products, rows, width, columns, fixed_in, moving_in, fixed_out, moving_out, scratch, name):
@@ -812,8 +828,8 @@
         groups = [list(range(c, seg_parts, 2)) for c in range(2)]
         return lax.psum_scatter(value, "seg", scatter_dimension=0, tiled=True, axis_index_groups=groups)
 
-    def gathered(value, rows, name):
-        whole, mine, other = assemble(rows, core[None].astype(jnp.int32), gather_halves(value), seg_parts // 2, name)
+    def gathered(blocks, rows, name):
+        whole, mine, other = assemble(rows, core[None].astype(jnp.int32), blocks, seg_parts // 2, name)
         return whole, (mine, swap_core(other))
 
     def of_both(value):
@@ -839,8 +855,8 @@
     low1 = rms_norm(inputs, first_gain).astype(BF)
     rows = arranged_rows(place, length // 2)
     straight = jnp.arange(8, dtype=jnp.int32) * (length // 2)
-    all_low1, low1_rows = gathered(low1, rows, "gather_low1")
-    all_cot, cot_rows = gathered(upstream, straight, "gather_cot")
+    all_low1, low1_rows = gathered(gather_halves(low1), rows, "gather_low1")
+    all_cot, cot_rows = gathered(gather_halves(upstream), straight, "gather_cot")
 
     taps = own(conv_taps)
     logit = own(decay_logit[None])
@@ -900,18 +916,18 @@
     residual = inputs + scatter_halves(*pieces)
 
     low2 = rms_norm(residual, second_gain).astype(BF)
-    all_low2, low2_rows = gathered(low2, straight, "gather_low2")
+    all_low2, low2_rows = gathered(gather_halves(low2), straight, "gather_low2")
     units, back_first, out_first = mlp_first(unit, all_low2, all_cot, feed_first)
     grad_first = scatter_rows(mlp_grad(unit, low2_rows, cot_rows, of_both(units)))
     units, *pieces = mlp_last(unit, all_low2, all_cot, feed_last, back_first)
     normed2_grad = scatter_halves(*pieces)
-    mlp_out = scatter_halves(*mlp_out_last(unit, feed_last, units, out_first))
     units_last = units
-    output = (residual + mlp_out).astype(BF).reshape(tokens.shape)
     residual_norm_grad, second_gain_grad = jax.vjp(rms_norm, residual, second_gain)[1](normed2_grad)
     residual_grad = upstream.astype(F32) + residual_norm_grad
 
-    mixer_grad, mixer_rows = gathered(residual_grad.astype(BF), straight, "gather_mixer")
+    mixer_blocks = gather_halves(residual_grad.astype(BF))
+    held = mlp_grad_beside(unit, low2_rows, cot_rows, of_both(units_last), 3 * recur_part)
+    mixer_grad, mixer_rows = gathered(after(mixer_blocks, held), straight, "gather_mixer")
     proj_grad, gate_low_grad, input_low_grad, conv_direct, sums, strips = scan_backward(
         rows, strip_tile, params, mixer_grad, recur, projected, states, decays, rate, opened, conv_out
     )
@@ -919,32 +935,33 @@
         tile_block, near, edge, conv_params, sums, gate_low_grad, input_low_grad, swap(strips, 1),
         decay_lines, input_lines, conv_direct, conv_ext.T, projected, proj_grad,
     )
-    *pieces, _ = project(rows, proj_grad, recur, 0, "normed1_grad")
-    grad_last = mlp_grad(unit, low2_rows, cot_rows, of_both(after(units_last, sums)))
-    grad_last = scatter_rows(after(grad_last, (grad_first, pieces[2])))
+    mlp_term = scatter_halves(*mlp_out_last(unit, feed_last, after(units_last, proj_grad), out_first))
+    output = (residual + mlp_term).astype(BF).reshape(tokens.shape)
+    grad_last_term = recur_grad(low1_rows, mixer_rows, of_both(proj_grad), of_both(mixed_low), held)
+    *pieces, _ = project(rows, after(proj_grad, grad_last_term), recur, 0, "normed1_grad")
     normed1_grad = scatter_halves(*pieces)
     input_norm_grad, first_gain_grad = jax.vjp(rms_norm, inputs, first_gain)[1](normed1_grad)
     input_grad = (residual_grad + input_norm_grad).astype(BF).reshape(tokens.shape)
 
-    recur_term = recur_grad(low1_rows, mixer_rows, of_both(proj_grad), of_both(mixed_low))
-    recur_sum = scatter_rows(after(recur_term, (grad_last, normed1_grad)))
-
-    def columns_of(which):
+    grad_last = scatter_rows(after(grad_last_term, grad_first))
+
+    def columns_of(value, which, start):
         return jnp.concatenate(
-            [
-                part[:, first : first + unit]
-                for part in (grad_first, grad_last)
-                for first in range(which * unit, part.shape[1], 3 * unit)
-            ],
-            axis=1,
+            [value[:, at : at + unit] for at in range(start + which * unit, value.shape[1], 3 * unit)], axis=1
         ).astype(F32)
 
-    feed_in_grad = jnp.stack([columns_of(0), columns_of(1)], axis=1)
-    feed_out_grad = columns_of(2)
-    recur_sum = after(recur_sum, (feed_in_grad, feed_out_grad)).astype(F32)
-    recur_in_grad, recur_out_grad = recur_sum[:, : 2 * recur_part], recur_sum[:, 2 * recur_part :]
-
-    mine = gather_seq(jnp.concatenate([sum_small(small), single], axis=0))
+    def feed_grads(value, start):
+        return jnp.stack([columns_of(value, i, start) for i in range(2)], axis=1), columns_of(value, 2, start)
+
+    feed_in_first, feed_out_first = feed_grads(grad_first, 0)
+    feed_in_grad = jnp.pad(feed_in_first, ((0, 0), (0, 0), (0, feed_part - first_part)))
+    feed_out_grad = jnp.pad(feed_out_first, ((0, 0), (0, feed_part - first_part)))
+    grad_last = after(grad_last, (feed_in_grad, feed_out_grad))
+    feed_in_grad, feed_out_grad, recur_in_grad, recur_out_grad = unpack(
+        unit, grad_last, feed_in_grad, feed_out_grad, recur_part, first_part
+    )
+
+    mine = gather_seq(jnp.concatenate([sum_small(small, grad_last_term), single], axis=0))
     swapped = [jnp.where(odd, mine[i ^ 1], mine[i]) for i in range(4)]
     mine = jnp.concatenate([jnp.where(place >= 2, swapped[i ^ 2], swapped[i]) for i in range(4)], axis=1)
     vectors = mine[block_size:].astype(F32)
@@ -962,7 +979,7 @@
         vectors[16:17],
         vectors[17 : 17 + edge_rows][None],
         gains[0],
-        recur_in_grad.reshape(own_rows, 2, recur_part),
+        recur_in_grad,
         vectors[:kernel_taps],
         vectors[kernel_taps],
         as_blocks(0),

time: 560 us -> 542 us (0.968)
  local copies, waits for them, and re-layouts: 98.8 us -> 88.3 us
  waiting for transfers between devices: 226 us -> 218 us
    ppermute x38, waiting for transfers between devices: 103 us -> 85.8 us  [swap(): lax.ppermute(value, 'seq', [(i, i ^ bit) for i in range(lax.axis_size('se...]
    unnamed x186 -> x175, local copies, waits for them, and re-layouts: 60.1 us -> 50.4 us
    ppermute x10, waiting for transfers between devices: 6.9 us -> 16.5 us  [swap_core(): lax.ppermute(value, 'seg', [(i, i ^ 1) for i in range(lax.axis_size('seg'...]
    pallas_call x5 -> x4, Pallas kernels: 72.9 us -> 64.8 us  [mlp_call(): pl.pallas_call(lambda *refs: kernel(tile, *refs), grid=(columns // (3 * t...]
    reduce_scatter x3 -> x2, waiting for transfers between devices: 18.8 us -> 11.5 us  [scatter_rows(): lax.psum_scatter(value, 'seg', scatter_dimension=0, tiled=True, axis_inde...]
    pallas_call x0 -> x2, Pallas kernels: none -> 7.17 us  [the longest x1 5.18 us: mlp_grad_beside(): pl.pallas_call(lambda *refs: mlp_grad_beside_kernel(tile, first, *refs),...]
  transfers between devices with their start and end apart: 61 -> 60, of which waited for: 35 -> 38; matrix products, arithmetic and copies ran while one was open for 15% -> 15% of each run, Pallas kernels for 24% -> 24%
where the time goes in v3:
time: 542 us; the launch traced here: 538 us
  waiting for transfers between devices  218 us (40%)
  Pallas kernels  132 us (24%)
  local copies, waits for them, and re-layouts  88.3 us (16%)
  starting transfers between devices  49.1 us (9%)
  other arithmetic  28.5 us (5%)
  between operations  15.2 us (3%)
  matrix products  5.99 us (1%)
    ppermute x38, waiting for transfers between devices, swap(): lax.ppermute(value, 'seq', [(i, i ^ bit) for i in range(lax.axis_size('se...  85.8 us
    pallas_call x4, Pallas kernels, mlp_call(): pl.pallas_call(lambda *refs: kernel(tile, *refs), grid=(columns // (3 * t...  64.8 us
    all_gather x3, waiting for transfers between devices, gather_seg(): return lax.all_gather(value, 'seg', axis=0, tiled=True)  53.3 us
    unnamed x175, local copies, waits for them, and re-layouts  50.4 us
    ppermute x38, starting transfers between devices, swap(): lax.ppermute(value, 'seq', [(i, i ^ bit) for i in range(lax.axis_size('se...  43.3 us
    ppermute x2, waiting for transfers between devices, sum_small(): other = lax.ppermute(low, 'seg', [(i, i ^ bit) for i in range(8)])  37.2 us
    ppermute x10, waiting for transfers between devices, swap_core(): lax.ppermute(value, 'seg', [(i, i ^ 1) for i in range(lax.axis_size('seg'...  16.5 us
    pallas_call x4, Pallas kernels, assemble(): pl.pallas_call(assemble_kernel, grid_spec=pltpu.PrefetchScalarGridSpec(nu...  15.5 us
  transfers between devices with their start and end apart: 60, of which 38 were waited for; matrix products, arithmetic and copies ran while one was open for 15% of the time, Pallas kernels for 24%

profile of v3, /device:TPU:0, one launch (start us, length us, event | category | flops | bytes accessed | tf_op | source)
XLA Modules:
  0.0 538.0 jit_solution(15656828357726658390)
XLA Ops:
  27.4 7.5 %collective-permute-done.one_ref = bf16[128,2048]{1,0:T(8,128)(2,1)S(1)} collective-permute-done((bf16[128,2048]{1,0:T(8,128)(2,1)S(1)}, bf16[128,2048]{1,0:T(8,128)(2,1)S(1)}, u32[]{:S(2)}, u32[]{:S(2)}) %collective-permute-start) | collective-permute-done | bytes 524320 | tf_op jit(solution)/shard_map/ppermute | solution.py:53
  49.9 42.4 %all-gather.4.cloned.1.call-done.right_ref.out_w_ref = bf16[2048,1920]{1,0:T(8,128)(2,1)} async-done(((bf16[256,1920]{1,0:T(8,128)(2,1)}), bf16[2048,1920]{1,0:T(8,128)(2,1)}) %all-gather.4.cloned.1.call-update) | async-done | bytes 7864336 | tf_op jit(solution)/shard_map/all_gather | solution.py:822
  92.3 6.0 %fusion.branch_ref.conv_in_ref = f32[512,1280]{1,0:T(8,128)S(1)} fusion(bf16[512,2048]{1,0:T(8,128)(2,1)} %copy-done.40, bf16[2048,1920]{1,0:T(8,128)(2,1)} %all-gather.4.cloned.1.call-done.right_ref.out_w_ref), kind=kOutput, calls=%fused_computation | convolution fusion | flops 2684354560 | bytes 9961472 | tf_op jit(solution)/shard_map/dot_general | solution.py:39
  102.8 5.7 %fusion.70 = (bf16[512,640]{0,1:T(8,128)(2,1)S(1)}, f32[512,640]{0,1:T(8,128)}) fusion(f32[640]{0:T(1024)S(1)} %get-tuple-element.176, f32[512,640]{0,1:T(8,128)} %copy.90, f32[3,640]{0,1:T(8,128)} %bitcast.132, f32[640]{0:T(1024)S(1)} %get-tuple-element.177, f32[640]{0:T(1024)S(1)} %get-tuple-element.178, f32[640]{0:T(1024)S(1)} %dynamic-slice.12, ...), kind=kLoop, calls=%fused_computation.198 | loop fusion | flops 3932160 | bytes 3297280 | tf_op jit(solution)/shard_map/convert_element_type | solution.py:905
  123.7 11.6 %scan_forward.1 = (f32[512,640]{1,0:T(8,128)S(1)}, f32[512,640]{1,0:T(8,128)S(1)}, f32[512,640]{1,0:T(8,128)S(1)}, f32[512,640]{1,0:T(8,128)S(1)}, bf16[512,640]{1,0:T(8,128)(2,1)S(1)}) custom-call(s32[5]{0:T(128)S(1)} %and_select_fusion.1.blk_ref, bf16[512,768]{1,0:T(8,128)(2,1)S(1)} %copy-done.12, bf16[5,256,128]{2,1,0:T(8,128)(2,1)S(1)} %copy-done.23, ...), custom_call_target="tpu_custom_call" | custom-call | flops 335544320 | bytes 9175040 | tf_op jit(solution)/shard_map/scan_forward/pallas_call | solution.py:298
  148.4 11.9 %collective-permute-done.5 = bf16[128,2048]{1,0:T(8,128)(2,1)S(1)} collective-permute-done((bf16[128,2048]{1,0:T(8,128)(2,1)S(1)}, bf16[128,2048]{1,0:T(8,128)(2,1)S(1)}, u32[]{:S(2)}, u32[]{:S(2)}) %collective-permute-start.5) | collective-permute-done | bytes 524320 | tf_op jit(solution)/shard_map/ppermute | solution.py:53
  174.1 8.5 %collective-permute-done.13.one_ref = bf16[128,2048]{1,0:T(8,128)(2,1)S(1)} collective-permute-done((bf16[128,2048]{1,0:T(8,128)(2,1)S(1)}, bf16[128,2048]{1,0:T(8,128)(2,1)S(1)}, u32[]{:S(2)}, u32[]{:S(2)}) %collective-permute-start.13) | collective-permute-done | bytes 524320 | tf_op jit(solution)/shard_map/ppermute | solution.py:53
  184.9 8.9 %collective-permute-done.9.one_ref = bf16[128,2048]{1,0:T(8,128)(2,1)S(1)} collective-permute-done((bf16[128,2048]{1,0:T(8,128)(2,1)S(1)}, bf16[128,2048]{1,0:T(8,128)(2,1)S(1)}, u32[]{:S(2)}, u32[]{:S(2)}) %collective-permute-start.9) | collective-permute-done | bytes 524320 | tf_op jit(solution)/shard_map/ppermute | solution.py:53
  212.5 29.7 %mlp_first.1 = (bf16[512,3072]{1,0:T(8,128)(2,1)}, f32[512,2048]{1,0:T(8,128)}, f32[512,2048]{1,0:T(8,128)}) custom-call(bf16[512,2048]{1,0:T(8,128)(2,1)} %copy-done.39, bf16[512,2048]{1,0:T(8,128)(2,1)} %copy-done.38, bf16[2048,3072]{1,0:T(8,128)(2,1)} %all-gather.8.cloned.1.call-done.refs_2_), custom_call_target="tpu_custom_call" | custom-call | flops 12884901888 | bytes 41943040 | tf_op jit(solution)/shard_map/mlp_first/pallas_call | solution.py:721
  242.8 6.7 %collective-permute-done.26.refs_3_ = bf16[1024,512]{1,0:T(8,128)(2,1)S(1)} collective-permute-done((bf16[1024,512]{1,0:T(8,128)(2,1)}, bf16[1024,512]{1,0:T(8,128)(2,1)S(1)}, u32[]{:S(2)}, u32[]{:S(2)}) %collective-permute-start.26) | collective-permute-done | bytes 1048608 | tf_op jit(solution)/shard_map/ppermute | solution.py:206
  252.1 11.4 %mlp_grad.1 = bf16[1024,3072]{1,0:T(8,128)(2,1)} custom-call(bf16[1024,512]{1,0:T(8,128)(2,1)} %copy-done.28, bf16[1024,512]{1,0:T(8,128)(2,1)} %copy-done.32, bf16[1024,512]{1,0:T(8,128)(2,1)} %copy-done.26, bf16[1024,512]{1,0:T(8,128)(2,1)} %copy-done.30, bf16[512,3072]{1,0:T(8,128)(2,1)} %get-tuple-element.126.refs_4_, ...), custom_call_target="tpu_custom_call" | custom-call | flops 6442450944 | bytes 41943040 | tf_op jit(solution)/shard_map/mlp_grad/pallas_call | solution.py:721
  263.6 10.9 %all-gather.6.cloned.1.call-done.refs_2_.refs_0_ = bf16[2048,1536]{1,0:T(8,128)(2,1)} async-done(((bf16[256,1536]{1,0:T(8,128)(2,1)}), bf16[2048,1536]{1,0:T(8,128)(2,1)}) %all-gather.6.cloned.1.call-update) | async-done | bytes 6291472 | tf_op jit(solution)/shard_map/all_gather | solution.py:822
  274.5 16.1 %mlp_last.1 = (bf16[512,1536]{1,0:T(8,128)(2,1)}, bf16[128,2048]{1,0:T(8,128)(2,1)}, bf16[128,2048]{1,0:T(8,128)(2,1)}, f32[256,2048]{1,0:T(8,128)}) custom-call(bf16[512,2048]{1,0:T(8,128)(2,1)} %copy-done.39, bf16[512,2048]{1,0:T(8,128)(2,1)} %copy-done.38, bf16[2048,1536]{1,0:T(8,128)(2,1)} %all-gather.6.cloned.1.call-done.refs_2_.refs_0_, ...), custom_call_target="tpu_custom_call" | custom-call | flops 5368709120 | bytes 29360128 | tf_op jit(solution)/shard_map/mlp_last/pallas_call | solution.py:721
  295.7 9.2 %collective-permute-done.17 = bf16[128,2048]{1,0:T(8,128)(2,1)S(1)} collective-permute-done((bf16[128,2048]{1,0:T(8,128)(2,1)}, bf16[128,2048]{1,0:T(8,128)(2,1)S(1)}, u32[]{:S(2)}, u32[]{:S(2)}) %collective-permute-start.17) | collective-permute-done | bytes 524320 | tf_op jit(solution)/shard_map/ppermute | solution.py:53
  324.8 7.1 %collective-permute-done.21.one_ref = bf16[128,2048]{1,0:T(8,128)(2,1)S(1)} collective-permute-done((bf16[128,2048]{1,0:T(8,128)(2,1)S(1)}, bf16[128,2048]{1,0:T(8,128)(2,1)S(1)}, u32[]{:S(2)}, u32[]{:S(2)}) %collective-permute-start.21) | collective-permute-done | bytes 524320 | tf_op jit(solution)/shard_map/ppermute | solution.py:53
  346.2 5.2 gather_mixer.1
  351.5 12.7 %scan_backward.1 = (bf16[512,1280]{1,0:T(8,128)(2,1)S(1)}, bf16[512,640]{1,0:T(8,128)(2,1)S(1)}, bf16[512,640]{1,0:T(8,128)(2,1)S(1)}, f32[512,640]{1,0:T(8,128)...) custom-call(s32[8]{0:T(128)S(1)} %stack.46.rows_ref, s32[1]{0:T(128)} %bitcast.29.strip_ref, ...), custom_call_target="tpu_custom_call" | custom-call | flops 1342177280 | bytes 14417920 | tf_op jit(solution)/shard_map/scan_backward/pallas_call | solution.py:422
  382.9 7.1 %recur_grad.1 = bf16[1024,3456]{1,0:T(8,128)(2,1)} custom-call(bf16[1024,512]{1,0:T(8,128)(2,1)S(1)} %copy-done.25, bf16[1024,512]{1,0:T(8,128)(2,1)S(1)} %collective-permute-done.33.low_other, bf16[1024,512]{1,0:T(8,128)(2,1)S(1)} %get-tuple-element.115.mixer_ref, ...), custom_call_target="tpu_custom_call", output_to_operand_aliasing={{}: (8, {})} | custom-call | flops 4026531840 | bytes 8126464 | tf_op jit(solution)/shard_map/recur_grad/pallas_call | solution.py:629
  398.2 5.7 %normed1_grad.1 = (bf16[128,2048]{1,0:T(8,128)(2,1)}, bf16[128,2048]{1,0:T(8,128)(2,1)}, f32[256,2048]{1,0:T(8,128)S(1)}, bf16[512,1280]{1,0:T(8,128)(2,1)}) custom-call(s32[8]{0:T(128)S(1)} %stack.46.rows_ref, bf16[512,1280]{1,0:T(8,128)(2,1)S(1)} %get-tuple-element.118.proj_ref.left_ref, bf16[2048,1920]{1,0:T(8,128)(2,1)S(1)} %copy-done.6), custom_call_target="tpu_custom_call" | custom-call | flops 2684354560 | bytes 13631488 | tf_op jit(solution)/shard_map/normed1_grad/pallas_call | solution.py:173
  406.5 7.6 %mlp_out.1 = (bf16[128,2048]{1,0:T(8,128)(2,1)}, bf16[128,2048]{1,0:T(8,128)(2,1)}, f32[256,2048]{1,0:T(8,128)}) custom-call(bf16[2048,1536]{1,0:T(8,128)(2,1)} %all-gather.6.cloned.1.call-done.refs_2_.refs_0_, bf16[512,1536]{1,0:T(8,128)(2,1)} %get-tuple-element.108.refs_4_.refs_1_, f32[512,2048]{1,0:T(8,128)} %get-tuple-element.109.refs_2_), custom_call_target="tpu_custom_call" | custom-call | flops 1073741824 | bytes 29360128 | tf_op jit(solution)/shard_map/mlp_out/pallas_call | solution.py:721
  415.6 5.5 %collective-permute-done.42 = bf16[272,640]{1,0:T(8,128)(2,1)} collective-permute-done((bf16[272,640]{1,0:T(8,128)(2,1)}, bf16[272,640]{1,0:T(8,128)(2,1)}, u32[]{:S(2)}, u32[]{:S(2)}) %collective-permute-start.42) | collective-permute-done | bytes 348192 | tf_op jit(solution)/shard_map/ppermute | solution.py:226
  433.3 31.7 %collective-permute-done.43 = bf16[272,640]{1,0:T(8,128)(2,1)S(1)} collective-permute-done((bf16[272,640]{1,0:T(8,128)(2,1)S(1)}, bf16[272,640]{1,0:T(8,128)(2,1)S(1)}, u32[]{:S(2)}, u32[]{:S(2)}) %collective-permute-start.43) | collective-permute-done | bytes 348192 | tf_op jit(solution)/shard_map/ppermute | solution.py:226
  469.6 5.4 %collective-permute-done.49 = f32[2,2048]{1,0:T(2,128)S(1)} collective-permute-done((f32[2,2048]{1,0:T(2,128)S(1)}, f32[2,2048]{1,0:T(2,128)S(1)}, u32[]{:S(2)}, u32[]{:S(2)}) %collective-permute-start.49) | collective-permute-done | bytes 16416 | tf_op jit(solution)/shard_map/ppermute | solution.py:237
  516.2 11.5 %reduce-scatter.5.cloned.1.call-done.refs_0_ = bf16[256,3456]{1,0:T(8,128)(2,1)} async-done(((bf16[1024,3456]{1,0:T(8,128)(2,1)}), bf16[256,3456]{1,0:T(8,128)(2,1)}) %reduce-scatter.5.cloned.1.call-update) | async-done | bytes 1769488 | tf_op jit(solution)/shard_map/reduce_scatter | solution.py:829
  (401 shorter events, 236.8 us)
Async XLA Ops:
  7.2 85.1 %all-gather.4.cloned.1.call-start = ((), (), s32[]{:S(2)}) async-start(), calls=%async_computation.2 | async-start | bytes 8847360 | tf_op jit(solution)/shard_map/all_gather | solution.py:822
  11.7 200.8 %all-gather.8.cloned.1.call-start = ((), (), s32[]{:S(2)}) async-start(), calls=%async_computation.4 | async-start | bytes 14155776 | tf_op jit(solution)/shard_map/all_gather | solution.py:822
  18.3 256.2 %all-gather.6.cloned.1.call-start = ((), (), s32[]{:S(2)}) async-start(), calls=%async_computation.3 | async-start | bytes 7077888 | tf_op jit(solution)/shard_map/all_gather | solution.py:822
  19.0 371.0 %reduce-scatter.3.cloned.1.call-start = ((), (), s32[]{:S(2)}) async-start(), calls=%async_computation.5 | async-start | bytes 7864320 | tf_op jit(solution)/shard_map/reduce_scatter | solution.py:829
  20.0 14.9 %collective-permute-start = (bf16[128,2048]{1,0:T(8,128)(2,1)S(1)}, bf16[128,2048]{1,0:T(8,128)(2,1)S(1)}, u32[]{:S(2)}, u32[]{:S(2)}) collective-permute-start(bf16[128,2048]{1,0:T(8,128)(2,1)S(1)} %fusion.32.own_ref), channel_id=1, source_target_pairs={{0,8},{8,0},{16,24},{24,16},{1,9},{9,1},{17,25},{25,17},{2,10},{10... | collective-permute-start | bytes 1572872 | tf_op jit(solution)/shard_map/ppermute | solution.py:53
  163.6 19.0 %collective-permute-start.13 = (bf16[128,2048]{1,0:T(8,128)(2,1)S(1)}, bf16[128,2048]{1,0:T(8,128)(2,1)S(1)}, u32[]{:S(2)}, u32[]{:S(2)}) collective-permute-start(bf16[128,2048]{1,0:T(8,128)(2,1)S(1)} %bitcast.123), channel_id=1, source_target_pairs={{0,8},{8,0},{16,24},{24,16},{1,9},{9,1},{17,25},{25,17},{2,10},{10... | collective-permute-start | bytes 1572872 | tf_op jit(solution)/shard_map/ppermute | solution.py:53
  164.1 19.1 %collective-permute-start.14 = (bf16[128,2048]{1,0:T(8,128)(2,1)S(1)}, bf16[128,2048]{1,0:T(8,128)(2,1)S(1)}, u32[]{:S(2)}, u32[]{:S(2)}) collective-permute-start(bf16[128,2048]{1,0:T(8,128)(2,1)S(1)} %bitcast.124), channel_id=1, source_target_pairs={{0,16},{8,24},{16,0},{24,8},{1,17},{9,25},{17,1},{25,9},{2,18},{10... | collective-permute-start | bytes 1572872 | tf_op jit(solution)/shard_map/ppermute | solution.py:53
  171.9 21.9 %collective-permute-start.9 = (bf16[128,2048]{1,0:T(8,128)(2,1)S(1)}, bf16[128,2048]{1,0:T(8,128)(2,1)S(1)}, u32[]{:S(2)}, u32[]{:S(2)}) collective-permute-start(bf16[128,2048]{1,0:T(8,128)(2,1)S(1)} %multiply_convert_fusion.own_ref), channel_id=1, source_target_pairs={{0,8},{8,0},{16,24},{24,16},{1,9},{9,1},{17,25},{25,17},{2,10},{10... | collective-permute-start | bytes 1572872 | tf_op jit(solution)/shard_map/ppermute | solution.py:53
  173.5 21.0 %collective-permute-start.10 = (bf16[128,2048]{1,0:T(8,128)(2,1)S(1)}, bf16[128,2048]{1,0:T(8,128)(2,1)S(1)}, u32[]{:S(2)}, u32[]{:S(2)}) collective-permute-start(bf16[128,2048]{1,0:T(8,128)(2,1)S(1)} %multiply_convert_fusion.own_ref), channel_id=1, source_target_pairs={{0,16},{8,24},{16,0},{24,8},{1,17},{9,25},{17,1},{25,9},{2,18},{10... | collective-permute-start | bytes 1572872 | tf_op jit(solution)/shard_map/ppermute | solution.py:53
  182.6 15.4 %collective-permute-start.15 = (bf16[64,2048]{1,0:T(8,128)(2,1)S(1)}, bf16[64,2048]{1,0:T(8,128)(2,1)S(1)}, u32[]{:S(2)}, u32[]{:S(2)}) collective-permute-start(bf16[64,2048]{1,0:T(8,128)(2,1)S(1)} %slice.418), channel_id=1, source_target_pairs={{0,16},{8,24},{16,0},{24,8},{1,17},{9,25},{17,1},{25,9},{2,18},{10... | collective-permute-start | bytes 786440 | tf_op jit(solution)/shard_map/ppermute | solution.py:53
  183.2 16.2 %collective-permute-start.16 = (bf16[64,2048]{1,0:T(8,128)(2,1)S(1)}, bf16[64,2048]{1,0:T(8,128)(2,1)S(1)}, u32[]{:S(2)}, u32[]{:S(2)}) collective-permute-start(bf16[64,2048]{1,0:T(8,128)(2,1)S(1)} %slice.419), channel_id=1, source_target_pairs={{0,8},{8,0},{16,24},{24,16},{1,9},{9,1},{17,25},{25,17},{2,10},{10... | collective-permute-start | bytes 786440 | tf_op jit(solution)/shard_map/ppermute | solution.py:53
  263.6 264.2 %reduce-scatter.5.cloned.1.call-start = ((), (), s32[]{:S(2)}) async-start(), calls=%async_computation.6 | async-start | bytes 8847360 | tf_op jit(solution)/shard_map/reduce_scatter | solution.py:829
  290.6 14.3 %collective-permute-start.17 = (bf16[128,2048]{1,0:T(8,128)(2,1)}, bf16[128,2048]{1,0:T(8,128)(2,1)S(1)}, u32[]{:S(2)}, u32[]{:S(2)}) collective-permute-start(bf16[128,2048]{1,0:T(8,128)(2,1)} %get-tuple-element.85), channel_id=1, source_target_pairs={{0,8},{8,0},{16,24},{24,16},{1,9},{9,1},{17,25},{25,17},{2,10},{10... | collective-permute-start | bytes 1572872 | tf_op jit(solution)/shard_map/ppermute | solution.py:53
  311.0 24.6 %collective-permute-start.27 = (bf16[512,1536]{1,0:T(8,128)(2,1)S(1)}, bf16[512,1536]{1,0:T(8,128)(2,1)}, u32[]{:S(2)}, u32[]{:S(2)}) collective-permute-start(bf16[512,1536]{1,0:T(8,128)(2,1)S(1)} %copy-done.9), channel_id=1, source_target_pairs={{0,1},{1,0},{2,3},{3,2},{4,5},{5,4},{6,7},{7,6},{8,9},{9,8},{10,11... | collective-permute-start | bytes 4718600 | tf_op jit(solution)/shard_map/ppermute | solution.py:206
  393.7 27.5 %collective-permute-start.42 = (bf16[272,640]{1,0:T(8,128)(2,1)}, bf16[272,640]{1,0:T(8,128)(2,1)}, u32[]{:S(2)}, u32[]{:S(2)}) collective-permute-start(bf16[272,640]{1,0:T(8,128)(2,1)} %fusion.43), channel_id=1, source_target_pairs={{0,2},{1,3},{2,0},{3,1},{4,6},{5,7},{6,4},{7,5},{8,10},{9,11},{10,... | collective-permute-start | bytes 1044488 | tf_op jit(solution)/shard_map/ppermute | solution.py:226
  404.0 18.4 %collective-permute-start.37 = (bf16[128,2048]{1,0:T(8,128)(2,1)}, bf16[128,2048]{1,0:T(8,128)(2,1)S(1)}, u32[]{:S(2)}, u32[]{:S(2)}) collective-permute-start(bf16[128,2048]{1,0:T(8,128)(2,1)} %get-tuple-element.120), channel_id=1, source_target_pairs={{0,8},{8,0},{16,24},{24,16},{1,9},{9,1},{17,25},{25,17},{2,10},{10... | collective-permute-start | bytes 1572872 | tf_op jit(solution)/shard_map/ppermute | solution.py:53
  405.9 16.5 %collective-permute-start.38 = (bf16[128,2048]{1,0:T(8,128)(2,1)}, bf16[128,2048]{1,0:T(8,128)(2,1)S(1)}, u32[]{:S(2)}, u32[]{:S(2)}) collective-permute-start(bf16[128,2048]{1,0:T(8,128)(2,1)} %get-tuple-element.121), channel_id=1, source_target_pairs={{0,16},{8,24},{16,0},{24,8},{1,17},{9,25},{17,1},{25,9},{2,18},{10... | collective-permute-start | bytes 1572872 | tf_op jit(solution)/shard_map/ppermute | solution.py:53
  414.1 16.1 %collective-permute-start.29 = (bf16[128,2048]{1,0:T(8,128)(2,1)}, bf16[128,2048]{1,0:T(8,128)(2,1)S(1)}, u32[]{:S(2)}, u32[]{:S(2)}) collective-permute-start(bf16[128,2048]{1,0:T(8,128)(2,1)} %get-tuple-element.111), channel_id=1, source_target_pairs={{0,8},{8,0},{16,24},{24,16},{1,9},{9,1},{17,25},{25,17},{2,10},{10... | collective-permute-start | bytes 1572872 | tf_op jit(solution)/shard_map/ppermute | solution.py:53
  414.5 17.6 %collective-permute-start.30 = (bf16[128,2048]{1,0:T(8,128)(2,1)}, bf16[128,2048]{1,0:T(8,128)(2,1)S(1)}, u32[]{:S(2)}, u32[]{:S(2)}) collective-permute-start(bf16[128,2048]{1,0:T(8,128)(2,1)} %get-tuple-element.112), channel_id=1, source_target_pairs={{0,16},{8,24},{16,0},{24,8},{1,17},{9,25},{17,1},{25,9},{2,18},{10... | collective-permute-start | bytes 1572872 | tf_op jit(solution)/shard_map/ppermute | solution.py:53
  422.3 42.7 %collective-permute-start.43 = (bf16[272,640]{1,0:T(8,128)(2,1)S(1)}, bf16[272,640]{1,0:T(8,128)(2,1)S(1)}, u32[]{:S(2)}, u32[]{:S(2)}) collective-permute-start(bf16[272,640]{1,0:T(8,128)(2,1)S(1)} %add_convert_fusion.2), channel_id=1, source_target_pairs={{0,4},{1,5},{2,6},{3,7},{4,0},{5,1},{6,2},{7,3},{8,12},{9,13},{10,... | collective-permute-start | bytes 1044488 | tf_op jit(solution)/shard_map/ppermute | solution.py:226
  422.5 42.6 %collective-permute-start.39 = (bf16[64,2048]{1,0:T(8,128)(2,1)S(1)}, bf16[64,2048]{1,0:T(8,128)(2,1)S(1)}, u32[]{:S(2)}, u32[]{:S(2)}) collective-permute-start(bf16[64,2048]{1,0:T(8,128)(2,1)S(1)} %get-tuple-element.186), channel_id=1, source_target_pairs={{0,16},{8,24},{16,0},{24,8},{1,17},{9,25},{17,1},{25,9},{2,18},{10... | collective-permute-start | bytes 786440 | tf_op jit(solution)/shard_map/ppermute | solution.py:53
  423.5 41.6 %collective-permute-start.40 = (bf16[64,2048]{1,0:T(8,128)(2,1)S(1)}, bf16[64,2048]{1,0:T(8,128)(2,1)S(1)}, u32[]{:S(2)}, u32[]{:S(2)}) collective-permute-start(bf16[64,2048]{1,0:T(8,128)(2,1)S(1)} %get-tuple-element.187), channel_id=1, source_target_pairs={{0,8},{8,0},{16,24},{24,16},{1,9},{9,1},{17,25},{25,17},{2,10},{10... | collective-permute-start | bytes 786440 | tf_op jit(solution)/shard_map/ppermute | solution.py:53
  432.3 42.8 %collective-permute-start.31 = (bf16[64,2048]{1,0:T(8,128)(2,1)S(1)}, bf16[64,2048]{1,0:T(8,128)(2,1)S(1)}, u32[]{:S(2)}, u32[]{:S(2)}) collective-permute-start(bf16[64,2048]{1,0:T(8,128)(2,1)S(1)} %get-tuple-element.188), channel_id=1, source_target_pairs={{0,16},{8,24},{16,0},{24,8},{1,17},{9,25},{17,1},{25,9},{2,18},{10... | collective-permute-start | bytes 786440 | tf_op jit(solution)/shard_map/ppermute | solution.py:53
  432.9 42.2 %collective-permute-start.32 = (bf16[64,2048]{1,0:T(8,128)(2,1)S(1)}, bf16[64,2048]{1,0:T(8,128)(2,1)S(1)}, u32[]{:S(2)}, u32[]{:S(2)}) collective-permute-start(bf16[64,2048]{1,0:T(8,128)(2,1)S(1)} %get-tuple-element.189), channel_id=1, source_target_pairs={{0,8},{8,0},{16,24},{24,16},{1,9},{9,1},{17,25},{25,17},{2,10},{10... | collective-permute-start | bytes 786440 | tf_op jit(solution)/shard_map/ppermute | solution.py:53
  (116 other events, 1055.9 us)
Sparse Core Ops, SparseCore 0:
  11.8 80.4 all-gather.3
  94.5 115.2 all-gather.7
  211.5 62.9 all-gather.5
  276.7 109.3 reduce-scatter.2
  390.1 137.5 reduce-scatter.4

commit v4 on v3

--- a/solution.py
+++ b/solution.py
@@ -221,11 +221,26 @@
     if not short_chain():
         return lax.dynamic_index_in_dim(lax.psum(value, "seg"), core, 0, False)
     total = mine.astype(F32) + swap_core(lax.dynamic_index_in_dim(value, 1 - core, 0, False)).astype(F32)
-    for bit in (2, 4):
-        low = total.astype(BF)
-        other = lax.ppermute(low, "seg", [(i, i ^ bit) for i in range(8)])
-        total = low.astype(F32) + after(other, middle).astype(F32)
-    return total.astype(BF)
+    rows = value.shape[1]
+    cut = rows // 32 * 16
+    chip = lax.axis_index("seg") // 2 % 2
+    low = total.astype(BF)
+
+    def half(which):
+        return lax.dynamic_slice_in_dim(low, which * cut, rows - cut, 0)
+
+    def exchange(value, bit):
+        return lax.ppermute(value, "seg", [(i, i ^ bit) for i in range(8)])
+
+    part = (half(chip).astype(F32) + after(exchange(half(1 - chip), 2), middle).astype(F32)).astype(BF)
+    part = (part.astype(F32) + exchange(part, 4).astype(F32)).astype(BF)
+    other = exchange(part, 2)
+    shared = rows - 2 * cut
+    return jnp.where(
+        chip == 0,
+        jnp.concatenate([part, other[shared:]], axis=0),
+        jnp.concatenate([other, part[shared:]], axis=0),
+    )
 
 
 def sum_all(value):
@@ -320,7 +335,7 @@
 
 
 def back_kernel(
-    rows_ref, strip_ref, par_ref, mixer_ref, out_w_ref, branch_ref, states_ref, decay_ref, rate_ref, open_ref, conv_ref,
+    rows_ref, strip_ref, par_ref, mixed_in, branch_ref, states_ref, decay_ref, rate_ref, open_ref, conv_ref,
     proj_out, gate_out, input_out, direct_out, sums_out, strips_out, mixed_ref,
 ):
     length = conv_ref.shape[0]
@@ -331,9 +346,8 @@
     flat_row = lax.broadcasted_iota(jnp.int32, (CHUNK, LANES), 0)
     steps = length // CHUNK
     half = length // 8
-    mixed = contract(mixer_ref[...], out_w_ref[...])
     for k in range(8):
-        mixed_ref[pl.ds(pl.multiple_of(rows_ref[k], half), half), :] = mixed[k * half : (k + 1) * half]
+        mixed_ref[pl.ds(pl.multiple_of(rows_ref[k], half), half), :] = mixed_in[k * half : (k + 1) * half, :]
 
     def body(turn, carried):
         carry, gate_sum, input_sum, logit_sum = carried
@@ -412,10 +426,9 @@
         strips_out[1] = input_out[...]
 
 
-def scan_backward(rows, strip_tile, params, mixer_grad, recur, projected, states, decays, rate, opened, conv_out):
+def scan_backward(rows, strip_tile, params, mixed_grad, projected, states, decays, rate, opened, conv_out):
     length, width = conv_out.shape
     tiles = width // LANES
-    out_tile = recur.shape[1] // LANES - tiles
     tile = pl.BlockSpec((length, LANES), lambda i, *_: (0, i))
     small = pl.BlockSpec((8, LANES), lambda i, *_: (0, i))
     low = jax.ShapeDtypeStruct((length, width), BF)
@@ -426,10 +439,8 @@
             grid=(tiles,),
             in_specs=[
                 small,
-                pl.BlockSpec(mixer_grad.shape, lambda i, *_: (0, 0), pipeline_mode=pl.Buffered(1)),
-                pl.BlockSpec((recur.shape[0], LANES), lambda i, *_: (0, out_tile + i)),
             ]
-            + [tile] * 6,
+            + [tile] * 7,
             out_specs=[tile] * 4 + [small, pl.BlockSpec((2, length, LANES), lambda i, *_: (0, 0, 0))],
             scratch_shapes=[pltpu.VMEM((length, LANES), F32)],
         ),
@@ -443,10 +454,10 @@
         ],
         compiler_params=pltpu.CompilerParams(vmem_limit_bytes=40 * 2**20),
         cost_estimate=pl.CostEstimate(
-            flops=2 * length * width * recur.shape[0], bytes_accessed=length * width * 44, transcendentals=0
+            flops=100 * length * width, bytes_accessed=length * width * 44, transcendentals=0
         ),
         name="scan_backward",
-    )(rows, strip_tile, params, mixer_grad, recur, projected, states, decays, rate, opened, conv_out)
+    )(rows, strip_tile, params, mixed_grad, projected, states, decays, rate, opened, conv_out)
 
 
 def gates_kernel(
@@ -929,7 +940,8 @@
     held = mlp_grad_beside(unit, low2_rows, cot_rows, of_both(units_last), 3 * recur_part)
     mixer_grad, mixer_rows = gathered(after(mixer_blocks, held), straight, "gather_mixer")
     proj_grad, gate_low_grad, input_low_grad, conv_direct, sums, strips = scan_backward(
-        rows, strip_tile, params, mixer_grad, recur, projected, states, decays, rate, opened, conv_out
+        rows, strip_tile, params, contract(mixer_grad, recur[:, 2 * recur_part :]), projected, states, decays, rate,
+        opened, conv_out,
     )
     proj_grad, small, single = gates_backward(
         tile_block, near, edge, conv_params, sums, gate_low_grad, input_low_grad, swap(strips, 1),

time: 542 us -> 536 us (0.989)
  waiting for transfers between devices: 218 us -> 203 us
  starting transfers between devices: 49.1 us -> 63.6 us
  local copies, waits for them, and re-layouts: 88.3 us -> 82 us
    reduce_scatter x2, waiting for transfers between devices: 11.5 us -> 28.2 us  [scatter_rows(): lax.psum_scatter(value, 'seg', scatter_dimension=0, tiled=True, axis_inde...]
    ppermute x2 -> x3, waiting for transfers between devices: 37.2 us -> 21.9 us  [exchange(): return lax.ppermute(value, 'seg', [(i, i ^ bit) for i in range(8)])]
    ppermute x38, waiting for transfers between devices: 85.8 us -> 77 us  [swap(): lax.ppermute(value, 'seq', [(i, i ^ bit) for i in range(lax.axis_size('se...]
    ppermute x5, waiting for transfers between devices: 13.5 us -> 5.89 us  [sum_all(): value = value + lax.ppermute(value, axis, pairs)]
    ppermute x5, starting transfers between devices: 3.54 us -> 10.3 us  [sum_all(): value = value + lax.ppermute(value, axis, pairs)]
    ppermute x2 -> x3, starting transfers between devices: 0.07 us -> 5.91 us  [exchange(): return lax.ppermute(value, 'seg', [(i, i ^ bit) for i in range(8)])]
    unnamed x175 -> x171, local copies, waits for them, and re-layouts: 50.4 us -> 44.9 us
  transfers between devices with their start and end apart: 60 -> 61, of which waited for: 38 -> 34; matrix products, arithmetic and copies ran while one was open for 15% -> 16% of each run, Pallas kernels for 24% -> 24%
where the time goes in v4:
time: 536 us; the launch traced here: 531 us
  waiting for transfers between devices  203 us (38%)
  Pallas kernels  129 us (24%)
  local copies, waits for them, and re-layouts  82 us (15%)
  starting transfers between devices  63.6 us (12%)
  other arithmetic  28.3 us (5%)
  between operations  15.3 us (3%)
  matrix products  9.75 us (2%)
    ppermute x38, waiting for transfers between devices, swap(): lax.ppermute(value, 'seq', [(i, i ^ bit) for i in range(lax.axis_size('se...  77 us
    pallas_call x4, Pallas kernels, mlp_call(): pl.pallas_call(lambda *refs: kernel(tile, *refs), grid=(columns // (3 * t...  64.8 us
    all_gather x3, waiting for transfers between devices, gather_seg(): return lax.all_gather(value, 'seg', axis=0, tiled=True)  53.3 us
    ppermute x38, starting transfers between devices, swap(): lax.ppermute(value, 'seq', [(i, i ^ bit) for i in range(lax.axis_size('se...  45 us
    unnamed x171, local copies, waits for them, and re-layouts  44.9 us
    reduce_scatter x2, waiting for transfers between devices, scatter_rows(): lax.psum_scatter(value, 'seg', scatter_dimension=0, tiled=True, axis_inde...  28.2 us
    ppermute x3, waiting for transfers between devices, exchange(): return lax.ppermute(value, 'seg', [(i, i ^ bit) for i in range(8)])  21.9 us
    ppermute x10, waiting for transfers between devices, swap_core(): lax.ppermute(value, 'seg', [(i, i ^ 1) for i in range(lax.axis_size('seg'...  16.5 us
  transfers between devices with their start and end apart: 61, of which 34 were waited for; matrix products, arithmetic and copies ran while one was open for 16% of the time, Pallas kernels for 24%

profile of v4, /device:TPU:0, one launch (start us, length us, event | category | flops | bytes accessed | tf_op | source)
XLA Modules:
  0.0 531.1 jit_solution(7325052648527011850)
XLA Ops:
  27.4 7.5 %collective-permute-done.one_ref = bf16[128,2048]{1,0:T(8,128)(2,1)S(1)} collective-permute-done((bf16[128,2048]{1,0:T(8,128)(2,1)S(1)}, bf16[128,2048]{1,0:T(8,128)(2,1)S(1)}, u32[]{:S(2)}, u32[]{:S(2)}) %collective-permute-start) | collective-permute-done | bytes 524320 | tf_op jit(solution)/shard_map/ppermute | solution.py:53
  49.9 42.4 %all-gather.4.cloned.1.call-done.right_ref = bf16[2048,1920]{1,0:T(8,128)(2,1)} async-done(((bf16[256,1920]{1,0:T(8,128)(2,1)}), bf16[2048,1920]{1,0:T(8,128)(2,1)}) %all-gather.4.cloned.1.call-update) | async-done | bytes 7864336 | tf_op jit(solution)/shard_map/all_gather | solution.py:833
  92.3 6.0 %fusion.branch_ref.conv_in_ref = f32[512,1280]{1,0:T(8,128)S(1)} fusion(bf16[512,2048]{1,0:T(8,128)(2,1)} %copy-done.38, bf16[2048,1920]{1,0:T(8,128)(2,1)} %all-gather.4.cloned.1.call-done.right_ref), kind=kOutput, calls=%fused_computation | convolution fusion | flops 2684354560 | bytes 9961472 | tf_op jit(solution)/shard_map/dot_general | solution.py:39
  102.8 5.7 %fusion.72 = (bf16[512,640]{0,1:T(8,128)(2,1)S(1)}, f32[512,640]{0,1:T(8,128)}) fusion(f32[640]{0:T(1024)S(1)} %get-tuple-element.174, f32[512,640]{0,1:T(8,128)} %copy.90, f32[3,640]{0,1:T(8,128)} %bitcast.133, f32[640]{0:T(1024)S(1)} %get-tuple-element.175, f32[640]{0:T(1024)S(1)} %get-tuple-element.176, f32[640]{0:T(1024)S(1)} %dynamic-slice.12, ...), kind=kLoop, calls=%fused_computation.202 | loop fusion | flops 3932160 | bytes 3297280 | tf_op jit(solution)/shard_map/convert_element_type | solution.py:916
  123.6 11.6 %scan_forward.1 = (f32[512,640]{1,0:T(8,128)S(1)}, f32[512,640]{1,0:T(8,128)S(1)}, f32[512,640]{1,0:T(8,128)S(1)}, f32[512,640]{1,0:T(8,128)S(1)}, bf16[512,640]{1,0:T(8,128)(2,1)S(1)}) custom-call(s32[5]{0:T(128)S(1)} %and_select_fusion.1.blk_ref, bf16[512,768]{1,0:T(8,128)(2,1)S(1)} %copy-done.12, bf16[5,256,128]{2,1,0:T(8,128)(2,1)S(1)} %copy-done.15, ...), custom_call_target="tpu_custom_call" | custom-call | flops 335544320 | bytes 9175040 | tf_op jit(solution)/shard_map/scan_forward/pallas_call | solution.py:313
  148.4 11.8 %collective-permute-done.5 = bf16[128,2048]{1,0:T(8,128)(2,1)S(1)} collective-permute-done((bf16[128,2048]{1,0:T(8,128)(2,1)S(1)}, bf16[128,2048]{1,0:T(8,128)(2,1)S(1)}, u32[]{:S(2)}, u32[]{:S(2)}) %collective-permute-start.5) | collective-permute-done | bytes 524320 | tf_op jit(solution)/shard_map/ppermute | solution.py:53
  174.1 8.6 %collective-permute-done.13.one_ref = bf16[128,2048]{1,0:T(8,128)(2,1)S(1)} collective-permute-done((bf16[128,2048]{1,0:T(8,128)(2,1)S(1)}, bf16[128,2048]{1,0:T(8,128)(2,1)S(1)}, u32[]{:S(2)}, u32[]{:S(2)}) %collective-permute-start.13) | collective-permute-done | bytes 524320 | tf_op jit(solution)/shard_map/ppermute | solution.py:53
  184.8 9.0 %collective-permute-done.9.one_ref = bf16[128,2048]{1,0:T(8,128)(2,1)S(1)} collective-permute-done((bf16[128,2048]{1,0:T(8,128)(2,1)S(1)}, bf16[128,2048]{1,0:T(8,128)(2,1)S(1)}, u32[]{:S(2)}, u32[]{:S(2)}) %collective-permute-start.9) | collective-permute-done | bytes 524320 | tf_op jit(solution)/shard_map/ppermute | solution.py:53
  212.6 29.7 %mlp_first.1 = (bf16[512,3072]{1,0:T(8,128)(2,1)}, f32[512,2048]{1,0:T(8,128)}, f32[512,2048]{1,0:T(8,128)}) custom-call(bf16[512,2048]{1,0:T(8,128)(2,1)} %copy-done.37, bf16[512,2048]{1,0:T(8,128)(2,1)} %copy-done.36, bf16[2048,3072]{1,0:T(8,128)(2,1)} %all-gather.8.cloned.1.call-done.refs_2_), custom_call_target="tpu_custom_call" | custom-call | flops 12884901888 | bytes 41943040 | tf_op jit(solution)/shard_map/mlp_first/pallas_call | solution.py:732
  242.8 6.7 %collective-permute-done.26.refs_3_ = bf16[1024,512]{1,0:T(8,128)(2,1)S(1)} collective-permute-done((bf16[1024,512]{1,0:T(8,128)(2,1)}, bf16[1024,512]{1,0:T(8,128)(2,1)S(1)}, u32[]{:S(2)}, u32[]{:S(2)}) %collective-permute-start.26) | collective-permute-done | bytes 1048608 | tf_op jit(solution)/shard_map/ppermute | solution.py:206
  252.2 11.4 %mlp_grad.1 = bf16[1024,3072]{1,0:T(8,128)(2,1)} custom-call(bf16[1024,512]{1,0:T(8,128)(2,1)} %copy-done.28, bf16[1024,512]{1,0:T(8,128)(2,1)} %copy-done.32, bf16[1024,512]{1,0:T(8,128)(2,1)} %copy-done.26, bf16[1024,512]{1,0:T(8,128)(2,1)} %copy-done.30, bf16[512,3072]{1,0:T(8,128)(2,1)} %get-tuple-element.124.refs_4_, ...), custom_call_target="tpu_custom_call" | custom-call | flops 6442450944 | bytes 41943040 | tf_op jit(solution)/shard_map/mlp_grad/pallas_call | solution.py:732
  263.6 10.9 %all-gather.6.cloned.1.call-done.refs_2_.refs_0_ = bf16[2048,1536]{1,0:T(8,128)(2,1)} async-done(((bf16[256,1536]{1,0:T(8,128)(2,1)}), bf16[2048,1536]{1,0:T(8,128)(2,1)}) %all-gather.6.cloned.1.call-update) | async-done | bytes 6291472 | tf_op jit(solution)/shard_map/all_gather | solution.py:833
  274.5 16.1 %mlp_last.1 = (bf16[512,1536]{1,0:T(8,128)(2,1)}, bf16[128,2048]{1,0:T(8,128)(2,1)}, bf16[128,2048]{1,0:T(8,128)(2,1)}, f32[256,2048]{1,0:T(8,128)}) custom-call(bf16[512,2048]{1,0:T(8,128)(2,1)} %copy-done.37, bf16[512,2048]{1,0:T(8,128)(2,1)} %copy-done.36, bf16[2048,1536]{1,0:T(8,128)(2,1)} %all-gather.6.cloned.1.call-done.refs_2_.refs_0_, ...), custom_call_target="tpu_custom_call" | custom-call | flops 5368709120 | bytes 29360128 | tf_op jit(solution)/shard_map/mlp_last/pallas_call | solution.py:732
  295.7 9.2 %collective-permute-done.17 = bf16[128,2048]{1,0:T(8,128)(2,1)S(1)} collective-permute-done((bf16[128,2048]{1,0:T(8,128)(2,1)}, bf16[128,2048]{1,0:T(8,128)(2,1)S(1)}, u32[]{:S(2)}, u32[]{:S(2)}) %collective-permute-start.17) | collective-permute-done | bytes 524320 | tf_op jit(solution)/shard_map/ppermute | solution.py:53
  324.1 7.8 %collective-permute-done.21.one_ref = bf16[128,2048]{1,0:T(8,128)(2,1)S(1)} collective-permute-done((bf16[128,2048]{1,0:T(8,128)(2,1)S(1)}, bf16[128,2048]{1,0:T(8,128)(2,1)S(1)}, u32[]{:S(2)}, u32[]{:S(2)}) %collective-permute-start.21) | collective-permute-done | bytes 524320 | tf_op jit(solution)/shard_map/ppermute | solution.py:53
  352.5 9.2 %scan_backward.1 = (bf16[512,1280]{1,0:T(8,128)(2,1)S(1)}, bf16[512,640]{1,0:T(8,128)(2,1)S(1)}, bf16[512,640]{1,0:T(8,128)(2,1)S(1)}, f32[512,640]{1,0:T(8,128)...) custom-call(s32[8]{0:T(128)S(1)} %stack.46.rows_ref, s32[1]{0:T(128)} %bitcast.29.strip_ref, ...), custom_call_target="tpu_custom_call" | custom-call | flops 32768000 | bytes 14417920 | tf_op jit(solution)/shard_map/scan_backward/pallas_call | solution.py:435
  379.5 7.1 %recur_grad.1 = bf16[1024,3456]{1,0:T(8,128)(2,1)} custom-call(bf16[1024,512]{1,0:T(8,128)(2,1)S(1)} %copy-done.25, bf16[1024,512]{1,0:T(8,128)(2,1)S(1)} %collective-permute-done.33.low_other, bf16[1024,512]{1,0:T(8,128)(2,1)S(1)} %get-tuple-element.114.mixer_ref, ...), custom_call_target="tpu_custom_call", output_to_operand_aliasing={{}: (8, {})} | custom-call | flops 4026531840 | bytes 8126464 | tf_op jit(solution)/shard_map/recur_grad/pallas_call | solution.py:640
  389.6 5.8 %collective-permute-done.42 = bf16[144,640]{1,0:T(8,128)(2,1)} collective-permute-done((bf16[144,640]{1,0:T(8,128)(2,1)S(1)}, bf16[144,640]{1,0:T(8,128)(2,1)}, u32[]{:S(2)}, u32[]{:S(2)}) %collective-permute-start.42) | collective-permute-done | bytes 184352 | tf_op jit(solution)/shard_map/ppermute | solution.py:233
  399.1 5.7 %normed1_grad.1 = (bf16[128,2048]{1,0:T(8,128)(2,1)}, bf16[128,2048]{1,0:T(8,128)(2,1)}, f32[256,2048]{1,0:T(8,128)S(1)}, bf16[512,1280]{1,0:T(8,128)(2,1)}) custom-call(s32[8]{0:T(128)S(1)} %stack.46.rows_ref, bf16[512,1280]{1,0:T(8,128)(2,1)S(1)} %get-tuple-element.117.proj_ref.left_ref, bf16[2048,1920]{1,0:T(8,128)(2,1)S(1)} %copy-done.8), custom_call_target="tpu_custom_call" | custom-call | flops 2684354560 | bytes 13631488 | tf_op jit(solution)/shard_map/normed1_grad/pallas_call | solution.py:173
  411.4 7.6 %mlp_out.1 = (bf16[128,2048]{1,0:T(8,128)(2,1)}, bf16[128,2048]{1,0:T(8,128)(2,1)}, f32[256,2048]{1,0:T(8,128)}) custom-call(bf16[2048,1536]{1,0:T(8,128)(2,1)} %all-gather.6.cloned.1.call-done.refs_2_.refs_0_, bf16[512,1536]{1,0:T(8,128)(2,1)} %get-tuple-element.107.refs_4_.refs_1_, f32[512,2048]{1,0:T(8,128)} %get-tuple-element.108.refs_2_), custom_call_target="tpu_custom_call" | custom-call | flops 1073741824 | bytes 29360128 | tf_op jit(solution)/shard_map/mlp_out/pallas_call | solution.py:732
  420.1 9.6 %collective-permute-done.43 = bf16[144,640]{1,0:T(8,128)(2,1)} collective-permute-done((bf16[144,640]{1,0:T(8,128)(2,1)S(1)}, bf16[144,640]{1,0:T(8,128)(2,1)}, u32[]{:S(2)}, u32[]{:S(2)}) %collective-permute-start.43) | collective-permute-done | bytes 184352 | tf_op jit(solution)/shard_map/ppermute | solution.py:233
  437.3 6.6 %collective-permute-done.44 = bf16[144,640]{1,0:T(8,128)(2,1)S(1)} collective-permute-done((bf16[144,640]{1,0:T(8,128)(2,1)S(1)}, bf16[144,640]{1,0:T(8,128)(2,1)S(1)}, u32[]{:S(2)}, u32[]{:S(2)}) %collective-permute-start.44) | collective-permute-done | bytes 184352 | tf_op jit(solution)/shard_map/ppermute | solution.py:233
  450.4 7.1 %collective-permute-start.51 = (f32[2,2048]{1,0:T(2,128)S(1)}, f32[2,2048]{1,0:T(2,128)S(1)}, u32[]{:S(2)}, u32[]{:S(2)}) collective-permute-start(f32[2,2048]{1,0:T(2,128)S(1)} %fusion.82), channel_id=1, source_target_pairs={{0,4},{1,5},{2,6},{3,7},{4,0},{5,1},{6,2},{7,3},{8,12},{9,13},{10,... | collective-permute-start | bytes 49160 | tf_op jit(solution)/shard_map/ppermute | solution.py:252
  492.7 28.2 %reduce-scatter.5.cloned.1.call-done.refs_0_ = bf16[256,3456]{1,0:T(8,128)(2,1)} async-done(((bf16[1024,3456]{1,0:T(8,128)(2,1)}), bf16[256,3456]{1,0:T(8,128)(2,1)}) %reduce-scatter.5.cloned.1.call-update) | async-done | bytes 1769488 | tf_op jit(solution)/shard_map/reduce_scatter | solution.py:840
  (404 shorter events, 234.7 us)
Async XLA Ops:
  7.2 85.1 %all-gather.4.cloned.1.call-start = ((), (), s32[]{:S(2)}) async-start(), calls=%async_computation.2 | async-start | bytes 8847360 | tf_op jit(solution)/shard_map/all_gather | solution.py:833
  11.7 200.9 %all-gather.8.cloned.1.call-start = ((), (), s32[]{:S(2)}) async-start(), calls=%async_computation.4 | async-start | bytes 14155776 | tf_op jit(solution)/shard_map/all_gather | solution.py:833
  18.3 256.2 %all-gather.6.cloned.1.call-start = ((), (), s32[]{:S(2)}) async-start(), calls=%async_computation.3 | async-start | bytes 7077888 | tf_op jit(solution)/shard_map/all_gather | solution.py:833
  19.0 367.6 %reduce-scatter.3.cloned.1.call-start = ((), (), s32[]{:S(2)}) async-start(), calls=%async_computation.5 | async-start | bytes 7864320 | tf_op jit(solution)/shard_map/reduce_scatter | solution.py:840
  20.0 14.9 %collective-permute-start = (bf16[128,2048]{1,0:T(8,128)(2,1)S(1)}, bf16[128,2048]{1,0:T(8,128)(2,1)S(1)}, u32[]{:S(2)}, u32[]{:S(2)}) collective-permute-start(bf16[128,2048]{1,0:T(8,128)(2,1)S(1)} %fusion.34.own_ref), channel_id=1, source_target_pairs={{0,8},{8,0},{16,24},{24,16},{1,9},{9,1},{17,25},{25,17},{2,10},{10... | collective-permute-start | bytes 1572872 | tf_op jit(solution)/shard_map/ppermute | solution.py:53
  23.0 13.8 %collective-permute-start.1 = (bf16[128,2048]{1,0:T(8,128)(2,1)S(1)}, bf16[128,2048]{1,0:T(8,128)(2,1)S(1)}, u32[]{:S(2)}, u32[]{:S(2)}) collective-permute-start(bf16[128,2048]{1,0:T(8,128)(2,1)S(1)} %fusion.34.own_ref), channel_id=1, source_target_pairs={{0,16},{8,24},{16,0},{24,8},{1,17},{9,25},{17,1},{25,9},{2,18},{10... | collective-permute-start | bytes 1572872 | tf_op jit(solution)/shard_map/ppermute | solution.py:53
  146.3 13.9 %collective-permute-start.5 = (bf16[128,2048]{1,0:T(8,128)(2,1)S(1)}, bf16[128,2048]{1,0:T(8,128)(2,1)S(1)}, u32[]{:S(2)}, u32[]{:S(2)}) collective-permute-start(bf16[128,2048]{1,0:T(8,128)(2,1)S(1)} %get-tuple-element.77), channel_id=1, source_target_pairs={{0,8},{8,0},{16,24},{24,16},{1,9},{9,1},{17,25},{25,17},{2,10},{10... | collective-permute-start | bytes 1572872 | tf_op jit(solution)/shard_map/ppermute | solution.py:53
  163.6 19.0 %collective-permute-start.13 = (bf16[128,2048]{1,0:T(8,128)(2,1)S(1)}, bf16[128,2048]{1,0:T(8,128)(2,1)S(1)}, u32[]{:S(2)}, u32[]{:S(2)}) collective-permute-start(bf16[128,2048]{1,0:T(8,128)(2,1)S(1)} %bitcast.124), channel_id=1, source_target_pairs={{0,8},{8,0},{16,24},{24,16},{1,9},{9,1},{17,25},{25,17},{2,10},{10... | collective-permute-start | bytes 1572872 | tf_op jit(solution)/shard_map/ppermute | solution.py:53
  164.2 19.1 %collective-permute-start.14 = (bf16[128,2048]{1,0:T(8,128)(2,1)S(1)}, bf16[128,2048]{1,0:T(8,128)(2,1)S(1)}, u32[]{:S(2)}, u32[]{:S(2)}) collective-permute-start(bf16[128,2048]{1,0:T(8,128)(2,1)S(1)} %bitcast.125), channel_id=1, source_target_pairs={{0,16},{8,24},{16,0},{24,8},{1,17},{9,25},{17,1},{25,9},{2,18},{10... | collective-permute-start | bytes 1572872 | tf_op jit(solution)/shard_map/ppermute | solution.py:53
  172.0 21.9 %collective-permute-start.9 = (bf16[128,2048]{1,0:T(8,128)(2,1)S(1)}, bf16[128,2048]{1,0:T(8,128)(2,1)S(1)}, u32[]{:S(2)}, u32[]{:S(2)}) collective-permute-start(bf16[128,2048]{1,0:T(8,128)(2,1)S(1)} %multiply_convert_fusion.own_ref), channel_id=1, source_target_pairs={{0,8},{8,0},{16,24},{24,16},{1,9},{9,1},{17,25},{25,17},{2,10},{10... | collective-permute-start | bytes 1572872 | tf_op jit(solution)/shard_map/ppermute | solution.py:53
  173.5 21.0 %collective-permute-start.10 = (bf16[128,2048]{1,0:T(8,128)(2,1)S(1)}, bf16[128,2048]{1,0:T(8,128)(2,1)S(1)}, u32[]{:S(2)}, u32[]{:S(2)}) collective-permute-start(bf16[128,2048]{1,0:T(8,128)(2,1)S(1)} %multiply_convert_fusion.own_ref), channel_id=1, source_target_pairs={{0,16},{8,24},{16,0},{24,8},{1,17},{9,25},{17,1},{25,9},{2,18},{10... | collective-permute-start | bytes 1572872 | tf_op jit(solution)/shard_map/ppermute | solution.py:53
  182.6 15.3 %collective-permute-start.15 = (bf16[64,2048]{1,0:T(8,128)(2,1)S(1)}, bf16[64,2048]{1,0:T(8,128)(2,1)S(1)}, u32[]{:S(2)}, u32[]{:S(2)}) collective-permute-start(bf16[64,2048]{1,0:T(8,128)(2,1)S(1)} %slice.430), channel_id=1, source_target_pairs={{0,16},{8,24},{16,0},{24,8},{1,17},{9,25},{17,1},{25,9},{2,18},{10... | collective-permute-start | bytes 786440 | tf_op jit(solution)/shard_map/ppermute | solution.py:53
  183.3 16.2 %collective-permute-start.16 = (bf16[64,2048]{1,0:T(8,128)(2,1)S(1)}, bf16[64,2048]{1,0:T(8,128)(2,1)S(1)}, u32[]{:S(2)}, u32[]{:S(2)}) collective-permute-start(bf16[64,2048]{1,0:T(8,128)(2,1)S(1)} %slice.431), channel_id=1, source_target_pairs={{0,8},{8,0},{16,24},{24,16},{1,9},{9,1},{17,25},{25,17},{2,10},{10... | collective-permute-start | bytes 786440 | tf_op jit(solution)/shard_map/ppermute | solution.py:53
  263.6 257.3 %reduce-scatter.5.cloned.1.call-start = ((), (), s32[]{:S(2)}) async-start(), calls=%async_computation.6 | async-start | bytes 8847360 | tf_op jit(solution)/shard_map/reduce_scatter | solution.py:840
  290.6 14.3 %collective-permute-start.17 = (bf16[128,2048]{1,0:T(8,128)(2,1)}, bf16[128,2048]{1,0:T(8,128)(2,1)S(1)}, u32[]{:S(2)}, u32[]{:S(2)}) collective-permute-start(bf16[128,2048]{1,0:T(8,128)(2,1)} %get-tuple-element.84), channel_id=1, source_target_pairs={{0,8},{8,0},{16,24},{24,16},{1,9},{9,1},{17,25},{25,17},{2,10},{10... | collective-permute-start | bytes 1572872 | tf_op jit(solution)/shard_map/ppermute | solution.py:53
  292.1 14.0 %collective-permute-start.18 = (bf16[128,2048]{1,0:T(8,128)(2,1)}, bf16[128,2048]{1,0:T(8,128)(2,1)S(1)}, u32[]{:S(2)}, u32[]{:S(2)}) collective-permute-start(bf16[128,2048]{1,0:T(8,128)(2,1)} %get-tuple-element.85), channel_id=1, source_target_pairs={{0,16},{8,24},{16,0},{24,8},{1,17},{9,25},{17,1},{25,9},{2,18},{10... | collective-permute-start | bytes 1572872 | tf_op jit(solution)/shard_map/ppermute | solution.py:53
  311.1 24.6 %collective-permute-start.27 = (bf16[512,1536]{1,0:T(8,128)(2,1)S(1)}, bf16[512,1536]{1,0:T(8,128)(2,1)}, u32[]{:S(2)}, u32[]{:S(2)}) collective-permute-start(bf16[512,1536]{1,0:T(8,128)(2,1)S(1)} %copy-done.9), channel_id=1, source_target_pairs={{0,1},{1,0},{2,3},{3,2},{4,5},{5,4},{6,7},{7,6},{8,9},{9,8},{10,11... | collective-permute-start | bytes 4718600 | tf_op jit(solution)/shard_map/ppermute | solution.py:206
  404.8 28.0 %collective-permute-start.37 = (bf16[128,2048]{1,0:T(8,128)(2,1)}, bf16[128,2048]{1,0:T(8,128)(2,1)S(1)}, u32[]{:S(2)}, u32[]{:S(2)}) collective-permute-start(bf16[128,2048]{1,0:T(8,128)(2,1)} %get-tuple-element.119), channel_id=1, source_target_pairs={{0,8},{8,0},{16,24},{24,16},{1,9},{9,1},{17,25},{25,17},{2,10},{10... | collective-permute-start | bytes 1572872 | tf_op jit(solution)/shard_map/ppermute | solution.py:53
  406.7 26.1 %collective-permute-start.38 = (bf16[128,2048]{1,0:T(8,128)(2,1)}, bf16[128,2048]{1,0:T(8,128)(2,1)S(1)}, u32[]{:S(2)}, u32[]{:S(2)}) collective-permute-start(bf16[128,2048]{1,0:T(8,128)(2,1)} %get-tuple-element.120), channel_id=1, source_target_pairs={{0,16},{8,24},{16,0},{24,8},{1,17},{9,25},{17,1},{25,9},{2,18},{10... | collective-permute-start | bytes 1572872 | tf_op jit(solution)/shard_map/ppermute | solution.py:53
  408.7 21.0 %collective-permute-start.43 = (bf16[144,640]{1,0:T(8,128)(2,1)S(1)}, bf16[144,640]{1,0:T(8,128)(2,1)}, u32[]{:S(2)}, u32[]{:S(2)}) collective-permute-start(bf16[144,640]{1,0:T(8,128)(2,1)S(1)} %add_convert_fusion.10), channel_id=1, source_target_pairs={{0,4},{1,5},{2,6},{3,7},{4,0},{5,1},{6,2},{7,3},{8,12},{9,13},{10,... | collective-permute-start | bytes 552968 | tf_op jit(solution)/shard_map/ppermute | solution.py:233
  419.0 16.7 %collective-permute-start.29 = (bf16[128,2048]{1,0:T(8,128)(2,1)}, bf16[128,2048]{1,0:T(8,128)(2,1)S(1)}, u32[]{:S(2)}, u32[]{:S(2)}) collective-permute-start(bf16[128,2048]{1,0:T(8,128)(2,1)} %get-tuple-element.110), channel_id=1, source_target_pairs={{0,8},{8,0},{16,24},{24,16},{1,9},{9,1},{17,25},{25,17},{2,10},{10... | collective-permute-start | bytes 1572872 | tf_op jit(solution)/shard_map/ppermute | solution.py:53
  419.6 16.2 %collective-permute-start.30 = (bf16[128,2048]{1,0:T(8,128)(2,1)}, bf16[128,2048]{1,0:T(8,128)(2,1)S(1)}, u32[]{:S(2)}, u32[]{:S(2)}) collective-permute-start(bf16[128,2048]{1,0:T(8,128)(2,1)} %get-tuple-element.111), channel_id=1, source_target_pairs={{0,16},{8,24},{16,0},{24,8},{1,17},{9,25},{17,1},{25,9},{2,18},{10... | collective-permute-start | bytes 1572872 | tf_op jit(solution)/shard_map/ppermute | solution.py:53
  435.9 21.6 %collective-permute-start.31 = (bf16[64,2048]{1,0:T(8,128)(2,1)S(1)}, bf16[64,2048]{1,0:T(8,128)(2,1)S(1)}, u32[]{:S(2)}, u32[]{:S(2)}) collective-permute-start(bf16[64,2048]{1,0:T(8,128)(2,1)S(1)} %get-tuple-element.186), channel_id=1, source_target_pairs={{0,16},{8,24},{16,0},{24,8},{1,17},{9,25},{17,1},{25,9},{2,18},{10... | collective-permute-start | bytes 786440 | tf_op jit(solution)/shard_map/ppermute | solution.py:53
  436.9 20.6 %collective-permute-start.32 = (bf16[64,2048]{1,0:T(8,128)(2,1)S(1)}, bf16[64,2048]{1,0:T(8,128)(2,1)S(1)}, u32[]{:S(2)}, u32[]{:S(2)}) collective-permute-start(bf16[64,2048]{1,0:T(8,128)(2,1)S(1)} %get-tuple-element.187), channel_id=1, source_target_pairs={{0,8},{8,0},{16,24},{24,16},{1,9},{9,1},{17,25},{25,17},{2,10},{10... | collective-permute-start | bytes 786440 | tf_op jit(solution)/shard_map/ppermute | solution.py:53
  (115 other events, 937.0 us)
Sparse Core Ops, SparseCore 0:
  11.8 80.4 all-gather.3
  94.5 115.2 all-gather.7
  211.5 62.9 all-gather.5
  276.7 109.3 reduce-scatter.2
  388.3 132.6 reduce-scatter.4

commit v5 on v4

--- a/solution.py
+++ b/solution.py
@@ -386,7 +386,8 @@
         log_decay = -RATE_SCALE * rate * soft
         scale = jnp.sqrt(neg_expm1(2.0 * log_decay))
         opened_conv = opened * conv
-        log_grad = decay * (adjoint * previous - adjoint * opened_conv * (decay / scale))
+        ratio = jnp.where(scale > 0.0, decay / scale, 0.0)
+        log_grad = decay * (adjoint * previous - adjoint * opened_conv * ratio)
         scaled = adjoint * scale
         direct_out[rows, :] = scaled * opened
         input_grad = (scaled * conv * opened * (1.0 - opened)).astype(BF)

time: 536 us -> 536 us (level)
  no operation moved by 1% of the time
where the time goes in v5:
time: 536 us; the launch traced here: 531 us
  waiting for transfers between devices  203 us (38%)
  Pallas kernels  129 us (24%)
  local copies, waits for them, and re-layouts  82 us (15%)
  starting transfers between devices  63.5 us (12%)
  other arithmetic  28.3 us (5%)
  between operations  15.3 us (3%)
  matrix products  9.75 us (2%)
    ppermute x38, waiting for transfers between devices, swap(): lax.ppermute(value, 'seq', [(i, i ^ bit) for i in range(lax.axis_size('se...  77 us
    pallas_call x4, Pallas kernels, mlp_call(): pl.pallas_call(lambda *refs: kernel(tile, *refs), grid=(columns // (3 * t...  64.8 us
    all_gather x3, waiting for transfers between devices, gather_seg(): return lax.all_gather(value, 'seg', axis=0, tiled=True)  53.3 us
    ppermute x38, starting transfers between devices, swap(): lax.ppermute(value, 'seq', [(i, i ^ bit) for i in range(lax.axis_size('se...  45 us
    unnamed x171, local copies, waits for them, and re-layouts  44.9 us
    reduce_scatter x2, waiting for transfers between devices, scatter_rows(): lax.psum_scatter(value, 'seg', scatter_dimension=0, tiled=True, axis_inde...  28.2 us
    ppermute x3, waiting for transfers between devices, exchange(): return lax.ppermute(value, 'seg', [(i, i ^ bit) for i in range(8)])  22 us
    ppermute x10, waiting for transfers between devices, swap_core(): lax.ppermute(value, 'seg', [(i, i ^ 1) for i in range(lax.axis_size('seg'...  16.5 us
  transfers between devices with their start and end apart: 61, of which 34 were waited for; matrix products, arithmetic and copies ran while one was open for 16% of the time, Pallas kernels for 24%

profile of v5, /device:TPU:0, one launch (start us, length us, event | category | flops | bytes accessed | tf_op | source)
XLA Modules:
  0.0 531.1 jit_solution(11886656980056082694)
XLA Ops:
  27.4 7.5 %collective-permute-done.one_ref = bf16[128,2048]{1,0:T(8,128)(2,1)S(1)} collective-permute-done((bf16[128,2048]{1,0:T(8,128)(2,1)S(1)}, bf16[128,2048]{1,0:T(8,128)(2,1)S(1)}, u32[]{:S(2)}, u32[]{:S(2)}) %collective-permute-start) | collective-permute-done | bytes 524320 | tf_op jit(solution)/shard_map/ppermute | solution.py:53
  49.9 42.4 %all-gather.4.cloned.1.call-done.right_ref = bf16[2048,1920]{1,0:T(8,128)(2,1)} async-done(((bf16[256,1920]{1,0:T(8,128)(2,1)}), bf16[2048,1920]{1,0:T(8,128)(2,1)}) %all-gather.4.cloned.1.call-update) | async-done | bytes 7864336 | tf_op jit(solution)/shard_map/all_gather | solution.py:834
  92.3 6.0 %fusion.branch_ref.conv_in_ref = f32[512,1280]{1,0:T(8,128)S(1)} fusion(bf16[512,2048]{1,0:T(8,128)(2,1)} %copy-done.38, bf16[2048,1920]{1,0:T(8,128)(2,1)} %all-gather.4.cloned.1.call-done.right_ref), kind=kOutput, calls=%fused_computation | convolution fusion | flops 2684354560 | bytes 9961472 | tf_op jit(solution)/shard_map/dot_general | solution.py:39
  102.8 5.7 %fusion.72 = (bf16[512,640]{0,1:T(8,128)(2,1)S(1)}, f32[512,640]{0,1:T(8,128)}) fusion(f32[640]{0:T(1024)S(1)} %get-tuple-element.174, f32[512,640]{0,1:T(8,128)} %copy.90, f32[3,640]{0,1:T(8,128)} %bitcast.133, f32[640]{0:T(1024)S(1)} %get-tuple-element.175, f32[640]{0:T(1024)S(1)} %get-tuple-element.176, f32[640]{0:T(1024)S(1)} %dynamic-slice.12, ...), kind=kLoop, calls=%fused_computation.202 | loop fusion | flops 3932160 | bytes 3297280 | tf_op jit(solution)/shard_map/convert_element_type | solution.py:917
  123.6 11.6 %scan_forward.1 = (f32[512,640]{1,0:T(8,128)S(1)}, f32[512,640]{1,0:T(8,128)S(1)}, f32[512,640]{1,0:T(8,128)S(1)}, f32[512,640]{1,0:T(8,128)S(1)}, bf16[512,640]{1,0:T(8,128)(2,1)S(1)}) custom-call(s32[5]{0:T(128)S(1)} %and_select_fusion.1.blk_ref, bf16[512,768]{1,0:T(8,128)(2,1)S(1)} %copy-done.12, bf16[5,256,128]{2,1,0:T(8,128)(2,1)S(1)} %copy-done.15, ...), custom_call_target="tpu_custom_call" | custom-call | flops 335544320 | bytes 9175040 | tf_op jit(solution)/shard_map/scan_forward/pallas_call | solution.py:313
  148.4 11.8 %collective-permute-done.5 = bf16[128,2048]{1,0:T(8,128)(2,1)S(1)} collective-permute-done((bf16[128,2048]{1,0:T(8,128)(2,1)S(1)}, bf16[128,2048]{1,0:T(8,128)(2,1)S(1)}, u32[]{:S(2)}, u32[]{:S(2)}) %collective-permute-start.5) | collective-permute-done | bytes 524320 | tf_op jit(solution)/shard_map/ppermute | solution.py:53
  174.1 8.6 %collective-permute-done.13.one_ref = bf16[128,2048]{1,0:T(8,128)(2,1)S(1)} collective-permute-done((bf16[128,2048]{1,0:T(8,128)(2,1)S(1)}, bf16[128,2048]{1,0:T(8,128)(2,1)S(1)}, u32[]{:S(2)}, u32[]{:S(2)}) %collective-permute-start.13) | collective-permute-done | bytes 524320 | tf_op jit(solution)/shard_map/ppermute | solution.py:53
  184.8 9.0 %collective-permute-done.9.one_ref = bf16[128,2048]{1,0:T(8,128)(2,1)S(1)} collective-permute-done((bf16[128,2048]{1,0:T(8,128)(2,1)S(1)}, bf16[128,2048]{1,0:T(8,128)(2,1)S(1)}, u32[]{:S(2)}, u32[]{:S(2)}) %collective-permute-start.9) | collective-permute-done | bytes 524320 | tf_op jit(solution)/shard_map/ppermute | solution.py:53
  212.6 29.7 %mlp_first.1 = (bf16[512,3072]{1,0:T(8,128)(2,1)}, f32[512,2048]{1,0:T(8,128)}, f32[512,2048]{1,0:T(8,128)}) custom-call(bf16[512,2048]{1,0:T(8,128)(2,1)} %copy-done.37, bf16[512,2048]{1,0:T(8,128)(2,1)} %copy-done.36, bf16[2048,3072]{1,0:T(8,128)(2,1)} %all-gather.8.cloned.1.call-done.refs_2_), custom_call_target="tpu_custom_call" | custom-call | flops 12884901888 | bytes 41943040 | tf_op jit(solution)/shard_map/mlp_first/pallas_call | solution.py:733
  242.8 6.7 %collective-permute-done.26.refs_3_ = bf16[1024,512]{1,0:T(8,128)(2,1)S(1)} collective-permute-done((bf16[1024,512]{1,0:T(8,128)(2,1)}, bf16[1024,512]{1,0:T(8,128)(2,1)S(1)}, u32[]{:S(2)}, u32[]{:S(2)}) %collective-permute-start.26) | collective-permute-done | bytes 1048608 | tf_op jit(solution)/shard_map/ppermute | solution.py:206
  252.2 11.4 %mlp_grad.1 = bf16[1024,3072]{1,0:T(8,128)(2,1)} custom-call(bf16[1024,512]{1,0:T(8,128)(2,1)} %copy-done.28, bf16[1024,512]{1,0:T(8,128)(2,1)} %copy-done.32, bf16[1024,512]{1,0:T(8,128)(2,1)} %copy-done.26, bf16[1024,512]{1,0:T(8,128)(2,1)} %copy-done.30, bf16[512,3072]{1,0:T(8,128)(2,1)} %get-tuple-element.124.refs_4_, ...), custom_call_target="tpu_custom_call" | custom-call | flops 6442450944 | bytes 41943040 | tf_op jit(solution)/shard_map/mlp_grad/pallas_call | solution.py:733
  263.6 10.9 %all-gather.6.cloned.1.call-done.refs_2_.refs_0_ = bf16[2048,1536]{1,0:T(8,128)(2,1)} async-done(((bf16[256,1536]{1,0:T(8,128)(2,1)}), bf16[2048,1536]{1,0:T(8,128)(2,1)}) %all-gather.6.cloned.1.call-update) | async-done | bytes 6291472 | tf_op jit(solution)/shard_map/all_gather | solution.py:834
  274.5 16.1 %mlp_last.1 = (bf16[512,1536]{1,0:T(8,128)(2,1)}, bf16[128,2048]{1,0:T(8,128)(2,1)}, bf16[128,2048]{1,0:T(8,128)(2,1)}, f32[256,2048]{1,0:T(8,128)}) custom-call(bf16[512,2048]{1,0:T(8,128)(2,1)} %copy-done.37, bf16[512,2048]{1,0:T(8,128)(2,1)} %copy-done.36, bf16[2048,1536]{1,0:T(8,128)(2,1)} %all-gather.6.cloned.1.call-done.refs_2_.refs_0_, ...), custom_call_target="tpu_custom_call" | custom-call | flops 5368709120 | bytes 29360128 | tf_op jit(solution)/shard_map/mlp_last/pallas_call | solution.py:733
  295.7 9.2 %collective-permute-done.17 = bf16[128,2048]{1,0:T(8,128)(2,1)S(1)} collective-permute-done((bf16[128,2048]{1,0:T(8,128)(2,1)}, bf16[128,2048]{1,0:T(8,128)(2,1)S(1)}, u32[]{:S(2)}, u32[]{:S(2)}) %collective-permute-start.17) | collective-permute-done | bytes 524320 | tf_op jit(solution)/shard_map/ppermute | solution.py:53
  324.1 7.8 %collective-permute-done.21.one_ref = bf16[128,2048]{1,0:T(8,128)(2,1)S(1)} collective-permute-done((bf16[128,2048]{1,0:T(8,128)(2,1)S(1)}, bf16[128,2048]{1,0:T(8,128)(2,1)S(1)}, u32[]{:S(2)}, u32[]{:S(2)}) %collective-permute-start.21) | collective-permute-done | bytes 524320 | tf_op jit(solution)/shard_map/ppermute | solution.py:53
  352.5 9.2 %scan_backward.1 = (bf16[512,1280]{1,0:T(8,128)(2,1)S(1)}, bf16[512,640]{1,0:T(8,128)(2,1)S(1)}, bf16[512,640]{1,0:T(8,128)(2,1)S(1)}, f32[512,640]{1,0:T(8,128)...) custom-call(s32[8]{0:T(128)S(1)} %stack.46.rows_ref, s32[1]{0:T(128)} %bitcast.29.strip_ref, ...), custom_call_target="tpu_custom_call" | custom-call | flops 32768000 | bytes 14417920 | tf_op jit(solution)/shard_map/scan_backward/pallas_call | solution.py:436
  379.5 7.1 %recur_grad.1 = bf16[1024,3456]{1,0:T(8,128)(2,1)} custom-call(bf16[1024,512]{1,0:T(8,128)(2,1)S(1)} %copy-done.25, bf16[1024,512]{1,0:T(8,128)(2,1)S(1)} %collective-permute-done.33.low_other, bf16[1024,512]{1,0:T(8,128)(2,1)S(1)} %get-tuple-element.114.mixer_ref, ...), custom_call_target="tpu_custom_call", output_to_operand_aliasing={{}: (8, {})} | custom-call | flops 4026531840 | bytes 8126464 | tf_op jit(solution)/shard_map/recur_grad/pallas_call | solution.py:641
  389.6 5.8 %collective-permute-done.42 = bf16[144,640]{1,0:T(8,128)(2,1)} collective-permute-done((bf16[144,640]{1,0:T(8,128)(2,1)S(1)}, bf16[144,640]{1,0:T(8,128)(2,1)}, u32[]{:S(2)}, u32[]{:S(2)}) %collective-permute-start.42) | collective-permute-done | bytes 184352 | tf_op jit(solution)/shard_map/ppermute | solution.py:233
  399.1 5.7 %normed1_grad.1 = (bf16[128,2048]{1,0:T(8,128)(2,1)}, bf16[128,2048]{1,0:T(8,128)(2,1)}, f32[256,2048]{1,0:T(8,128)S(1)}, bf16[512,1280]{1,0:T(8,128)(2,1)}) custom-call(s32[8]{0:T(128)S(1)} %stack.46.rows_ref, bf16[512,1280]{1,0:T(8,128)(2,1)S(1)} %get-tuple-element.117.proj_ref.left_ref, bf16[2048,1920]{1,0:T(8,128)(2,1)S(1)} %copy-done.8), custom_call_target="tpu_custom_call" | custom-call | flops 2684354560 | bytes 13631488 | tf_op jit(solution)/shard_map/normed1_grad/pallas_call | solution.py:173
  411.4 7.6 %mlp_out.1 = (bf16[128,2048]{1,0:T(8,128)(2,1)}, bf16[128,2048]{1,0:T(8,128)(2,1)}, f32[256,2048]{1,0:T(8,128)}) custom-call(bf16[2048,1536]{1,0:T(8,128)(2,1)} %all-gather.6.cloned.1.call-done.refs_2_.refs_0_, bf16[512,1536]{1,0:T(8,128)(2,1)} %get-tuple-element.107.refs_4_.refs_1_, f32[512,2048]{1,0:T(8,128)} %get-tuple-element.108.refs_2_), custom_call_target="tpu_custom_call" | custom-call | flops 1073741824 | bytes 29360128 | tf_op jit(solution)/shard_map/mlp_out/pallas_call | solution.py:733
  420.1 9.6 %collective-permute-done.43 = bf16[144,640]{1,0:T(8,128)(2,1)} collective-permute-done((bf16[144,640]{1,0:T(8,128)(2,1)S(1)}, bf16[144,640]{1,0:T(8,128)(2,1)}, u32[]{:S(2)}, u32[]{:S(2)}) %collective-permute-start.43) | collective-permute-done | bytes 184352 | tf_op jit(solution)/shard_map/ppermute | solution.py:233
  437.3 6.6 %collective-permute-done.44 = bf16[144,640]{1,0:T(8,128)(2,1)S(1)} collective-permute-done((bf16[144,640]{1,0:T(8,128)(2,1)S(1)}, bf16[144,640]{1,0:T(8,128)(2,1)S(1)}, u32[]{:S(2)}, u32[]{:S(2)}) %collective-permute-start.44) | collective-permute-done | bytes 184352 | tf_op jit(solution)/shard_map/ppermute | solution.py:233
  450.4 7.1 %collective-permute-start.51 = (f32[2,2048]{1,0:T(2,128)S(1)}, f32[2,2048]{1,0:T(2,128)S(1)}, u32[]{:S(2)}, u32[]{:S(2)}) collective-permute-start(f32[2,2048]{1,0:T(2,128)S(1)} %fusion.82), channel_id=1, source_target_pairs={{0,4},{1,5},{2,6},{3,7},{4,0},{5,1},{6,2},{7,3},{8,12},{9,13},{10,... | collective-permute-start | bytes 49160 | tf_op jit(solution)/shard_map/ppermute | solution.py:252
  492.7 28.2 %reduce-scatter.5.cloned.1.call-done.refs_0_ = bf16[256,3456]{1,0:T(8,128)(2,1)} async-done(((bf16[1024,3456]{1,0:T(8,128)(2,1)}), bf16[256,3456]{1,0:T(8,128)(2,1)}) %reduce-scatter.5.cloned.1.call-update) | async-done | bytes 1769488 | tf_op jit(solution)/shard_map/reduce_scatter | solution.py:841
  (404 shorter events, 234.7 us)
Async XLA Ops:
  7.2 85.1 %all-gather.4.cloned.1.call-start = ((), (), s32[]{:S(2)}) async-start(), calls=%async_computation.2 | async-start | bytes 8847360 | tf_op jit(solution)/shard_map/all_gather | solution.py:834
  11.7 200.9 %all-gather.8.cloned.1.call-start = ((), (), s32[]{:S(2)}) async-start(), calls=%async_computation.4 | async-start | bytes 14155776 | tf_op jit(solution)/shard_map/all_gather | solution.py:834
  18.3 256.2 %all-gather.6.cloned.1.call-start = ((), (), s32[]{:S(2)}) async-start(), calls=%async_computation.3 | async-start | bytes 7077888 | tf_op jit(solution)/shard_map/all_gather | solution.py:834
  19.0 367.6 %reduce-scatter.3.cloned.1.call-start = ((), (), s32[]{:S(2)}) async-start(), calls=%async_computation.5 | async-start | bytes 7864320 | tf_op jit(solution)/shard_map/reduce_scatter | solution.py:841
  20.0 14.9 %collective-permute-start = (bf16[128,2048]{1,0:T(8,128)(2,1)S(1)}, bf16[128,2048]{1,0:T(8,128)(2,1)S(1)}, u32[]{:S(2)}, u32[]{:S(2)}) collective-permute-start(bf16[128,2048]{1,0:T(8,128)(2,1)S(1)} %fusion.34.own_ref), channel_id=1, source_target_pairs={{0,8},{8,0},{16,24},{24,16},{1,9},{9,1},{17,25},{25,17},{2,10},{10... | collective-permute-start | bytes 1572872 | tf_op jit(solution)/shard_map/ppermute | solution.py:53
  23.0 13.8 %collective-permute-start.1 = (bf16[128,2048]{1,0:T(8,128)(2,1)S(1)}, bf16[128,2048]{1,0:T(8,128)(2,1)S(1)}, u32[]{:S(2)}, u32[]{:S(2)}) collective-permute-start(bf16[128,2048]{1,0:T(8,128)(2,1)S(1)} %fusion.34.own_ref), channel_id=1, source_target_pairs={{0,16},{8,24},{16,0},{24,8},{1,17},{9,25},{17,1},{25,9},{2,18},{10... | collective-permute-start | bytes 1572872 | tf_op jit(solution)/shard_map/ppermute | solution.py:53
  146.3 13.9 %collective-permute-start.5 = (bf16[128,2048]{1,0:T(8,128)(2,1)S(1)}, bf16[128,2048]{1,0:T(8,128)(2,1)S(1)}, u32[]{:S(2)}, u32[]{:S(2)}) collective-permute-start(bf16[128,2048]{1,0:T(8,128)(2,1)S(1)} %get-tuple-element.77), channel_id=1, source_target_pairs={{0,8},{8,0},{16,24},{24,16},{1,9},{9,1},{17,25},{25,17},{2,10},{10... | collective-permute-start | bytes 1572872 | tf_op jit(solution)/shard_map/ppermute | solution.py:53
  163.6 19.0 %collective-permute-start.13 = (bf16[128,2048]{1,0:T(8,128)(2,1)S(1)}, bf16[128,2048]{1,0:T(8,128)(2,1)S(1)}, u32[]{:S(2)}, u32[]{:S(2)}) collective-permute-start(bf16[128,2048]{1,0:T(8,128)(2,1)S(1)} %bitcast.124), channel_id=1, source_target_pairs={{0,8},{8,0},{16,24},{24,16},{1,9},{9,1},{17,25},{25,17},{2,10},{10... | collective-permute-start | bytes 1572872 | tf_op jit(solution)/shard_map/ppermute | solution.py:53
  164.2 19.1 %collective-permute-start.14 = (bf16[128,2048]{1,0:T(8,128)(2,1)S(1)}, bf16[128,2048]{1,0:T(8,128)(2,1)S(1)}, u32[]{:S(2)}, u32[]{:S(2)}) collective-permute-start(bf16[128,2048]{1,0:T(8,128)(2,1)S(1)} %bitcast.125), channel_id=1, source_target_pairs={{0,16},{8,24},{16,0},{24,8},{1,17},{9,25},{17,1},{25,9},{2,18},{10... | collective-permute-start | bytes 1572872 | tf_op jit(solution)/shard_map/ppermute | solution.py:53
  172.0 21.9 %collective-permute-start.9 = (bf16[128,2048]{1,0:T(8,128)(2,1)S(1)}, bf16[128,2048]{1,0:T(8,128)(2,1)S(1)}, u32[]{:S(2)}, u32[]{:S(2)}) collective-permute-start(bf16[128,2048]{1,0:T(8,128)(2,1)S(1)} %multiply_convert_fusion.own_ref), channel_id=1, source_target_pairs={{0,8},{8,0},{16,24},{24,16},{1,9},{9,1},{17,25},{25,17},{2,10},{10... | collective-permute-start | bytes 1572872 | tf_op jit(solution)/shard_map/ppermute | solution.py:53
  173.5 21.0 %collective-permute-start.10 = (bf16[128,2048]{1,0:T(8,128)(2,1)S(1)}, bf16[128,2048]{1,0:T(8,128)(2,1)S(1)}, u32[]{:S(2)}, u32[]{:S(2)}) collective-permute-start(bf16[128,2048]{1,0:T(8,128)(2,1)S(1)} %multiply_convert_fusion.own_ref), channel_id=1, source_target_pairs={{0,16},{8,24},{16,0},{24,8},{1,17},{9,25},{17,1},{25,9},{2,18},{10... | collective-permute-start | bytes 1572872 | tf_op jit(solution)/shard_map/ppermute | solution.py:53
  182.6 15.3 %collective-permute-start.15 = (bf16[64,2048]{1,0:T(8,128)(2,1)S(1)}, bf16[64,2048]{1,0:T(8,128)(2,1)S(1)}, u32[]{:S(2)}, u32[]{:S(2)}) collective-permute-start(bf16[64,2048]{1,0:T(8,128)(2,1)S(1)} %slice.430), channel_id=1, source_target_pairs={{0,16},{8,24},{16,0},{24,8},{1,17},{9,25},{17,1},{25,9},{2,18},{10... | collective-permute-start | bytes 786440 | tf_op jit(solution)/shard_map/ppermute | solution.py:53
  183.3 16.2 %collective-permute-start.16 = (bf16[64,2048]{1,0:T(8,128)(2,1)S(1)}, bf16[64,2048]{1,0:T(8,128)(2,1)S(1)}, u32[]{:S(2)}, u32[]{:S(2)}) collective-permute-start(bf16[64,2048]{1,0:T(8,128)(2,1)S(1)} %slice.431), channel_id=1, source_target_pairs={{0,8},{8,0},{16,24},{24,16},{1,9},{9,1},{17,25},{25,17},{2,10},{10... | collective-permute-start | bytes 786440 | tf_op jit(solution)/shard_map/ppermute | solution.py:53
  263.6 257.3 %reduce-scatter.5.cloned.1.call-start = ((), (), s32[]{:S(2)}) async-start(), calls=%async_computation.6 | async-start | bytes 8847360 | tf_op jit(solution)/shard_map/reduce_scatter | solution.py:841
  290.6 14.3 %collective-permute-start.17 = (bf16[128,2048]{1,0:T(8,128)(2,1)}, bf16[128,2048]{1,0:T(8,128)(2,1)S(1)}, u32[]{:S(2)}, u32[]{:S(2)}) collective-permute-start(bf16[128,2048]{1,0:T(8,128)(2,1)} %get-tuple-element.84), channel_id=1, source_target_pairs={{0,8},{8,0},{16,24},{24,16},{1,9},{9,1},{17,25},{25,17},{2,10},{10... | collective-permute-start | bytes 1572872 | tf_op jit(solution)/shard_map/ppermute | solution.py:53
  292.1 14.0 %collective-permute-start.18 = (bf16[128,2048]{1,0:T(8,128)(2,1)}, bf16[128,2048]{1,0:T(8,128)(2,1)S(1)}, u32[]{:S(2)}, u32[]{:S(2)}) collective-permute-start(bf16[128,2048]{1,0:T(8,128)(2,1)} %get-tuple-element.85), channel_id=1, source_target_pairs={{0,16},{8,24},{16,0},{24,8},{1,17},{9,25},{17,1},{25,9},{2,18},{10... | collective-permute-start | bytes 1572872 | tf_op jit(solution)/shard_map/ppermute | solution.py:53
  311.1 24.6 %collective-permute-start.27 = (bf16[512,1536]{1,0:T(8,128)(2,1)S(1)}, bf16[512,1536]{1,0:T(8,128)(2,1)}, u32[]{:S(2)}, u32[]{:S(2)}) collective-permute-start(bf16[512,1536]{1,0:T(8,128)(2,1)S(1)} %copy-done.9), channel_id=1, source_target_pairs={{0,1},{1,0},{2,3},{3,2},{4,5},{5,4},{6,7},{7,6},{8,9},{9,8},{10,11... | collective-permute-start | bytes 4718600 | tf_op jit(solution)/shard_map/ppermute | solution.py:206
  404.8 28.0 %collective-permute-start.37 = (bf16[128,2048]{1,0:T(8,128)(2,1)}, bf16[128,2048]{1,0:T(8,128)(2,1)S(1)}, u32[]{:S(2)}, u32[]{:S(2)}) collective-permute-start(bf16[128,2048]{1,0:T(8,128)(2,1)} %get-tuple-element.119), channel_id=1, source_target_pairs={{0,8},{8,0},{16,24},{24,16},{1,9},{9,1},{17,25},{25,17},{2,10},{10... | collective-permute-start | bytes 1572872 | tf_op jit(solution)/shard_map/ppermute | solution.py:53
  406.8 26.0 %collective-permute-start.38 = (bf16[128,2048]{1,0:T(8,128)(2,1)}, bf16[128,2048]{1,0:T(8,128)(2,1)S(1)}, u32[]{:S(2)}, u32[]{:S(2)}) collective-permute-start(bf16[128,2048]{1,0:T(8,128)(2,1)} %get-tuple-element.120), channel_id=1, source_target_pairs={{0,16},{8,24},{16,0},{24,8},{1,17},{9,25},{17,1},{25,9},{2,18},{10... | collective-permute-start | bytes 1572872 | tf_op jit(solution)/shard_map/ppermute | solution.py:53
  408.7 21.0 %collective-permute-start.43 = (bf16[144,640]{1,0:T(8,128)(2,1)S(1)}, bf16[144,640]{1,0:T(8,128)(2,1)}, u32[]{:S(2)}, u32[]{:S(2)}) collective-permute-start(bf16[144,640]{1,0:T(8,128)(2,1)S(1)} %add_convert_fusion.10), channel_id=1, source_target_pairs={{0,4},{1,5},{2,6},{3,7},{4,0},{5,1},{6,2},{7,3},{8,12},{9,13},{10,... | collective-permute-start | bytes 552968 | tf_op jit(solution)/shard_map/ppermute | solution.py:233
  419.0 16.7 %collective-permute-start.29 = (bf16[128,2048]{1,0:T(8,128)(2,1)}, bf16[128,2048]{1,0:T(8,128)(2,1)S(1)}, u32[]{:S(2)}, u32[]{:S(2)}) collective-permute-start(bf16[128,2048]{1,0:T(8,128)(2,1)} %get-tuple-element.110), channel_id=1, source_target_pairs={{0,8},{8,0},{16,24},{24,16},{1,9},{9,1},{17,25},{25,17},{2,10},{10... | collective-permute-start | bytes 1572872 | tf_op jit(solution)/shard_map/ppermute | solution.py:53
  419.6 16.2 %collective-permute-start.30 = (bf16[128,2048]{1,0:T(8,128)(2,1)}, bf16[128,2048]{1,0:T(8,128)(2,1)S(1)}, u32[]{:S(2)}, u32[]{:S(2)}) collective-permute-start(bf16[128,2048]{1,0:T(8,128)(2,1)} %get-tuple-element.111), channel_id=1, source_target_pairs={{0,16},{8,24},{16,0},{24,8},{1,17},{9,25},{17,1},{25,9},{2,18},{10... | collective-permute-start | bytes 1572872 | tf_op jit(solution)/shard_map/ppermute | solution.py:53
  435.9 21.6 %collective-permute-start.31 = (bf16[64,2048]{1,0:T(8,128)(2,1)S(1)}, bf16[64,2048]{1,0:T(8,128)(2,1)S(1)}, u32[]{:S(2)}, u32[]{:S(2)}) collective-permute-start(bf16[64,2048]{1,0:T(8,128)(2,1)S(1)} %get-tuple-element.186), channel_id=1, source_target_pairs={{0,16},{8,24},{16,0},{24,8},{1,17},{9,25},{17,1},{25,9},{2,18},{10... | collective-permute-start | bytes 786440 | tf_op jit(solution)/shard_map/ppermute | solution.py:53
  436.9 20.6 %collective-permute-start.32 = (bf16[64,2048]{1,0:T(8,128)(2,1)S(1)}, bf16[64,2048]{1,0:T(8,128)(2,1)S(1)}, u32[]{:S(2)}, u32[]{:S(2)}) collective-permute-start(bf16[64,2048]{1,0:T(8,128)(2,1)S(1)} %get-tuple-element.187), channel_id=1, source_target_pairs={{0,8},{8,0},{16,24},{24,16},{1,9},{9,1},{17,25},{25,17},{2,10},{10... | collective-permute-start | bytes 786440 | tf_op jit(solution)/shard_map/ppermute | solution.py:53
  (115 other events, 937.1 us)
Sparse Core Ops, SparseCore 0:
  11.8 80.4 all-gather.3
  94.5 115.2 all-gather.7
  211.5 62.9 all-gather.5
  276.7 109.3 reduce-scatter.2
  388.3 132.6 reduce-scatter.4

commit v6 on v5

--- a/solution.py
+++ b/solution.py
@@ -858,7 +858,7 @@
         jnp.concatenate([c for first in range(a, b, unit) for c in feed_columns(first, unit)], axis=1)
         for a, b in cuts
     ]
-    recur = gather_seg(jnp.concatenate([recur_in[:, 0], recur_in[:, 1], recur_out], axis=1))
+    recur = gather_seg(jnp.concatenate([recur_in.reshape(own_rows, 2 * recur_part), recur_out], axis=1))
     feed_first = gather_seg(feeds[0])
     feed_last = gather_seg(feeds[1])
 

time: 536 us -> 540 us (level)
    unnamed x171 -> x170, local copies, waits for them, and re-layouts: 44.9 us -> 45.4 us
  transfers between devices with their start and end apart: 61 -> 61, of which waited for: 34 -> 35; matrix products, arithmetic and copies ran while one was open for 16% -> 16% of each run, Pallas kernels for 24% -> 24%
where the time goes in v6:
time: 540 us; the launch traced here: 530 us
  waiting for transfers between devices  203 us (38%)
  Pallas kernels  129 us (24%)
  local copies, waits for them, and re-layouts  80.1 us (15%)
  starting transfers between devices  64.2 us (12%)
  other arithmetic  29.4 us (5%)
  between operations  15.2 us (3%)
  matrix products  9.69 us (2%)
    ppermute x38, waiting for transfers between devices, swap(): lax.ppermute(value, 'seq', [(i, i ^ bit) for i in range(lax.axis_size('se...  76.7 us
    pallas_call x4, Pallas kernels, mlp_call(): pl.pallas_call(lambda *refs: kernel(tile, *refs), grid=(columns // (3 * t...  64.5 us
    all_gather x3, waiting for transfers between devices, gather_seg(): return lax.all_gather(value, 'seg', axis=0, tiled=True)  53.4 us
    unnamed x170, local copies, waits for them, and re-layouts  45.4 us
    ppermute x38, starting transfers between devices, swap(): lax.ppermute(value, 'seq', [(i, i ^ bit) for i in range(lax.axis_size('se...  45.4 us
    reduce_scatter x2, waiting for transfers between devices, scatter_rows(): lax.psum_scatter(value, 'seg', scatter_dimension=0, tiled=True, axis_inde...  28.3 us
    ppermute x3, waiting for transfers between devices, exchange(): return lax.ppermute(value, 'seg', [(i, i ^ bit) for i in range(8)])  21.4 us
    ppermute x10, waiting for transfers between devices, swap_core(): lax.ppermute(value, 'seg', [(i, i ^ 1) for i in range(lax.axis_size('seg'...  16.5 us
  transfers between devices with their start and end apart: 61, of which 35 were waited for; matrix products, arithmetic and copies ran while one was open for 16% of the time, Pallas kernels for 24%

profile of v6, /device:TPU:0, one launch (start us, length us, event | category | flops | bytes accessed | tf_op | source)
XLA Modules:
  0.0 530.0 jit_solution(6403617125576957171)
XLA Ops:
  26.0 7.5 %collective-permute-done.one_ref = bf16[128,2048]{1,0:T(8,128)(2,1)S(1)} collective-permute-done((bf16[128,2048]{1,0:T(8,128)(2,1)S(1)}, bf16[128,2048]{1,0:T(8,128)(2,1)S(1)}, u32[]{:S(2)}, u32[]{:S(2)}) %collective-permute-start) | collective-permute-done | bytes 524320 | tf_op jit(solution)/shard_map/ppermute | solution.py:53
  48.6 42.6 %all-gather.4.cloned.1.call-done.right_ref = bf16[2048,1920]{1,0:T(8,128)(2,1)} async-done(((bf16[256,1920]{1,0:T(8,128)(2,1)}), bf16[2048,1920]{1,0:T(8,128)(2,1)}) %all-gather.4.cloned.1.call-update) | async-done | bytes 7864336 | tf_op jit(solution)/shard_map/all_gather | solution.py:834
  91.1 6.0 %fusion.branch_ref.conv_in_ref = f32[512,1280]{1,0:T(8,128)S(1)} fusion(bf16[512,2048]{1,0:T(8,128)(2,1)} %copy-done.38, bf16[2048,1920]{1,0:T(8,128)(2,1)} %all-gather.4.cloned.1.call-done.right_ref), kind=kOutput, calls=%fused_computation | convolution fusion | flops 2684354560 | bytes 9961472 | tf_op jit(solution)/shard_map/dot_general | solution.py:39
  101.7 5.7 %fusion.72 = (bf16[512,640]{0,1:T(8,128)(2,1)S(1)}, f32[512,640]{0,1:T(8,128)}) fusion(f32[640]{0:T(1024)S(1)} %get-tuple-element.174, f32[512,640]{0,1:T(8,128)} %copy.84, f32[3,640]{0,1:T(8,128)} %bitcast.131, f32[640]{0:T(1024)S(1)} %get-tuple-element.175, f32[640]{0:T(1024)S(1)} %get-tuple-element.176, f32[640]{0:T(1024)S(1)} %dynamic-slice.12, ...), kind=kLoop, calls=%fused_computation.200 | loop fusion | flops 3932160 | bytes 3297280 | tf_op jit(solution)/shard_map/convert_element_type | solution.py:917
  122.5 11.6 %scan_forward.1 = (f32[512,640]{1,0:T(8,128)S(1)}, f32[512,640]{1,0:T(8,128)S(1)}, f32[512,640]{1,0:T(8,128)S(1)}, f32[512,640]{1,0:T(8,128)S(1)}, bf16[512,640]{1,0:T(8,128)(2,1)S(1)}) custom-call(s32[5]{0:T(128)S(1)} %and_select_fusion.1.blk_ref, bf16[512,768]{1,0:T(8,128)(2,1)S(1)} %copy-done.12, bf16[5,256,128]{2,1,0:T(8,128)(2,1)S(1)} %copy-done.15, ...), custom_call_target="tpu_custom_call" | custom-call | flops 335544320 | bytes 9175040 | tf_op jit(solution)/shard_map/scan_forward/pallas_call | solution.py:313
  147.3 11.8 %collective-permute-done.5 = bf16[128,2048]{1,0:T(8,128)(2,1)S(1)} collective-permute-done((bf16[128,2048]{1,0:T(8,128)(2,1)S(1)}, bf16[128,2048]{1,0:T(8,128)(2,1)S(1)}, u32[]{:S(2)}, u32[]{:S(2)}) %collective-permute-start.5) | collective-permute-done | bytes 524320 | tf_op jit(solution)/shard_map/ppermute | solution.py:53
  173.0 8.5 %collective-permute-done.13.one_ref = bf16[128,2048]{1,0:T(8,128)(2,1)S(1)} collective-permute-done((bf16[128,2048]{1,0:T(8,128)(2,1)S(1)}, bf16[128,2048]{1,0:T(8,128)(2,1)S(1)}, u32[]{:S(2)}, u32[]{:S(2)}) %collective-permute-start.13) | collective-permute-done | bytes 524320 | tf_op jit(solution)/shard_map/ppermute | solution.py:53
  183.7 9.0 %collective-permute-done.9.one_ref = bf16[128,2048]{1,0:T(8,128)(2,1)S(1)} collective-permute-done((bf16[128,2048]{1,0:T(8,128)(2,1)S(1)}, bf16[128,2048]{1,0:T(8,128)(2,1)S(1)}, u32[]{:S(2)}, u32[]{:S(2)}) %collective-permute-start.9) | collective-permute-done | bytes 524320 | tf_op jit(solution)/shard_map/ppermute | solution.py:53
  211.4 29.8 %mlp_first.1 = (bf16[512,3072]{1,0:T(8,128)(2,1)}, f32[512,2048]{1,0:T(8,128)}, f32[512,2048]{1,0:T(8,128)}) custom-call(bf16[512,2048]{1,0:T(8,128)(2,1)} %copy-done.37, bf16[512,2048]{1,0:T(8,128)(2,1)} %copy-done.36, bf16[2048,3072]{1,0:T(8,128)(2,1)} %all-gather.8.cloned.1.call-done.refs_2_), custom_call_target="tpu_custom_call" | custom-call | flops 12884901888 | bytes 41943040 | tf_op jit(solution)/shard_map/mlp_first/pallas_call | solution.py:733
  241.8 6.7 %collective-permute-done.26.refs_3_ = bf16[1024,512]{1,0:T(8,128)(2,1)S(1)} collective-permute-done((bf16[1024,512]{1,0:T(8,128)(2,1)}, bf16[1024,512]{1,0:T(8,128)(2,1)S(1)}, u32[]{:S(2)}, u32[]{:S(2)}) %collective-permute-start.26) | collective-permute-done | bytes 1048608 | tf_op jit(solution)/shard_map/ppermute | solution.py:206
  251.1 11.4 %mlp_grad.1 = bf16[1024,3072]{1,0:T(8,128)(2,1)} custom-call(bf16[1024,512]{1,0:T(8,128)(2,1)} %copy-done.28, bf16[1024,512]{1,0:T(8,128)(2,1)} %copy-done.32, bf16[1024,512]{1,0:T(8,128)(2,1)} %copy-done.26, bf16[1024,512]{1,0:T(8,128)(2,1)} %copy-done.30, bf16[512,3072]{1,0:T(8,128)(2,1)} %get-tuple-element.124.refs_4_, ...), custom_call_target="tpu_custom_call" | custom-call | flops 6442450944 | bytes 41943040 | tf_op jit(solution)/shard_map/mlp_grad/pallas_call | solution.py:733
  262.6 10.8 %all-gather.6.cloned.1.call-done.refs_2_.refs_0_ = bf16[2048,1536]{1,0:T(8,128)(2,1)} async-done(((bf16[256,1536]{1,0:T(8,128)(2,1)}), bf16[2048,1536]{1,0:T(8,128)(2,1)}) %all-gather.6.cloned.1.call-update) | async-done | bytes 6291472 | tf_op jit(solution)/shard_map/all_gather | solution.py:834
  273.4 15.7 %mlp_last.1 = (bf16[512,1536]{1,0:T(8,128)(2,1)}, bf16[128,2048]{1,0:T(8,128)(2,1)}, bf16[128,2048]{1,0:T(8,128)(2,1)}, f32[256,2048]{1,0:T(8,128)}) custom-call(bf16[512,2048]{1,0:T(8,128)(2,1)} %copy-done.37, bf16[512,2048]{1,0:T(8,128)(2,1)} %copy-done.36, bf16[2048,1536]{1,0:T(8,128)(2,1)} %all-gather.6.cloned.1.call-done.refs_2_.refs_0_, ...), custom_call_target="tpu_custom_call" | custom-call | flops 5368709120 | bytes 29360128 | tf_op jit(solution)/shard_map/mlp_last/pallas_call | solution.py:733
  294.1 9.2 %collective-permute-done.17 = bf16[128,2048]{1,0:T(8,128)(2,1)S(1)} collective-permute-done((bf16[128,2048]{1,0:T(8,128)(2,1)}, bf16[128,2048]{1,0:T(8,128)(2,1)S(1)}, u32[]{:S(2)}, u32[]{:S(2)}) %collective-permute-start.17) | collective-permute-done | bytes 524320 | tf_op jit(solution)/shard_map/ppermute | solution.py:53
  322.5 7.8 %collective-permute-done.21.one_ref = bf16[128,2048]{1,0:T(8,128)(2,1)S(1)} collective-permute-done((bf16[128,2048]{1,0:T(8,128)(2,1)S(1)}, bf16[128,2048]{1,0:T(8,128)(2,1)S(1)}, u32[]{:S(2)}, u32[]{:S(2)}) %collective-permute-start.21) | collective-permute-done | bytes 524320 | tf_op jit(solution)/shard_map/ppermute | solution.py:53
  341.6 5.3 %gather_mixer.1 = (bf16[512,2048]{1,0:T(8,128)(2,1)S(1)}, bf16[1024,512]{1,0:T(8,128)(2,1)S(1)}, bf16[1024,512]{1,0:T(8,128)(2,1)S(1)}) custom-call(s32[8]{0:T(128)S(1)} %iota_multiply_fusion.rows_ref, s32[1]{0:T(128)} %bitcast.9.core_ref, bf16[128,2048]{1,0:T(8,128)(2,1)S(1)} %fusion.71.own_ref, bf16[128,2048]{1,0:T(8,128)(2,1)S(1)} %collective-permute-done.21.one_ref, ...), custom_call_target="tpu_custom_call" | custom-call | bytes 6291456 | tf_op jit(solution)/shard_map/gather_mixer/pallas_call | solution.py:98
  350.7 9.2 %scan_backward.1 = (bf16[512,1280]{1,0:T(8,128)(2,1)S(1)}, bf16[512,640]{1,0:T(8,128)(2,1)S(1)}, bf16[512,640]{1,0:T(8,128)(2,1)S(1)}, f32[512,640]{1,0:T(8,128)...) custom-call(s32[8]{0:T(128)S(1)} %stack.46.rows_ref, s32[1]{0:T(128)} %bitcast.27.strip_ref, ...), custom_call_target="tpu_custom_call" | custom-call | flops 32768000 | bytes 14417920 | tf_op jit(solution)/shard_map/scan_backward/pallas_call | solution.py:436
  377.8 7.1 %recur_grad.1 = bf16[1024,3456]{1,0:T(8,128)(2,1)} custom-call(bf16[1024,512]{1,0:T(8,128)(2,1)S(1)} %copy-done.25, bf16[1024,512]{1,0:T(8,128)(2,1)S(1)} %collective-permute-done.33.low_other, bf16[1024,512]{1,0:T(8,128)(2,1)S(1)} %get-tuple-element.114.mixer_ref, ...), custom_call_target="tpu_custom_call", output_to_operand_aliasing={{}: (8, {})} | custom-call | flops 4026531840 | bytes 8126464 | tf_op jit(solution)/shard_map/recur_grad/pallas_call | solution.py:641
  397.7 5.7 %normed1_grad.1 = (bf16[128,2048]{1,0:T(8,128)(2,1)}, bf16[128,2048]{1,0:T(8,128)(2,1)}, f32[256,2048]{1,0:T(8,128)S(1)}, bf16[512,1280]{1,0:T(8,128)(2,1)}) custom-call(s32[8]{0:T(128)S(1)} %stack.46.rows_ref, bf16[512,1280]{1,0:T(8,128)(2,1)S(1)} %get-tuple-element.117.proj_ref.left_ref, bf16[2048,1920]{1,0:T(8,128)(2,1)S(1)} %copy-done.8), custom_call_target="tpu_custom_call" | custom-call | flops 2684354560 | bytes 13631488 | tf_op jit(solution)/shard_map/normed1_grad/pallas_call | solution.py:173
  410.3 7.6 %mlp_out.1 = (bf16[128,2048]{1,0:T(8,128)(2,1)}, bf16[128,2048]{1,0:T(8,128)(2,1)}, f32[256,2048]{1,0:T(8,128)}) custom-call(bf16[2048,1536]{1,0:T(8,128)(2,1)} %all-gather.6.cloned.1.call-done.refs_2_.refs_0_, bf16[512,1536]{1,0:T(8,128)(2,1)} %get-tuple-element.107.refs_4_.refs_1_, f32[512,2048]{1,0:T(8,128)} %get-tuple-element.108.refs_2_), custom_call_target="tpu_custom_call" | custom-call | flops 1073741824 | bytes 29360128 | tf_op jit(solution)/shard_map/mlp_out/pallas_call | solution.py:733
  419.0 9.6 %collective-permute-done.43 = bf16[144,640]{1,0:T(8,128)(2,1)} collective-permute-done((bf16[144,640]{1,0:T(8,128)(2,1)S(1)}, bf16[144,640]{1,0:T(8,128)(2,1)}, u32[]{:S(2)}, u32[]{:S(2)}) %collective-permute-start.43) | collective-permute-done | bytes 184352 | tf_op jit(solution)/shard_map/ppermute | solution.py:233
  436.1 6.6 %collective-permute-done.44 = bf16[144,640]{1,0:T(8,128)(2,1)S(1)} collective-permute-done((bf16[144,640]{1,0:T(8,128)(2,1)S(1)}, bf16[144,640]{1,0:T(8,128)(2,1)S(1)}, u32[]{:S(2)}, u32[]{:S(2)}) %collective-permute-start.44) | collective-permute-done | bytes 184352 | tf_op jit(solution)/shard_map/ppermute | solution.py:233
  449.2 7.0 %collective-permute-start.51 = (f32[2,2048]{1,0:T(2,128)S(1)}, f32[2,2048]{1,0:T(2,128)S(1)}, u32[]{:S(2)}, u32[]{:S(2)}) collective-permute-start(f32[2,2048]{1,0:T(2,128)S(1)} %fusion.81), channel_id=1, source_target_pairs={{0,4},{1,5},{2,6},{3,7},{4,0},{5,1},{6,2},{7,3},{8,12},{9,13},{10,... | collective-permute-start | bytes 49160 | tf_op jit(solution)/shard_map/ppermute | solution.py:252
  491.5 28.2 %reduce-scatter.5.cloned.1.call-done.refs_0_ = bf16[256,3456]{1,0:T(8,128)(2,1)} async-done(((bf16[1024,3456]{1,0:T(8,128)(2,1)}), bf16[256,3456]{1,0:T(8,128)(2,1)}) %reduce-scatter.5.cloned.1.call-update) | async-done | bytes 1769488 | tf_op jit(solution)/shard_map/reduce_scatter | solution.py:841
  (401 shorter events, 234.4 us)
Async XLA Ops:
  7.2 83.9 %all-gather.4.cloned.1.call-start = ((), (), s32[]{:S(2)}) async-start(), calls=%async_computation.2 | async-start | bytes 8847360 | tf_op jit(solution)/shard_map/all_gather | solution.py:834
  10.6 200.8 %all-gather.8.cloned.1.call-start = ((), (), s32[]{:S(2)}) async-start(), calls=%async_computation.4 | async-start | bytes 14155776 | tf_op jit(solution)/shard_map/all_gather | solution.py:834
  17.1 256.2 %all-gather.6.cloned.1.call-start = ((), (), s32[]{:S(2)}) async-start(), calls=%async_computation.3 | async-start | bytes 7077888 | tf_op jit(solution)/shard_map/all_gather | solution.py:834
  17.9 367.1 %reduce-scatter.3.cloned.1.call-start = ((), (), s32[]{:S(2)}) async-start(), calls=%async_computation.5 | async-start | bytes 7864320 | tf_op jit(solution)/shard_map/reduce_scatter | solution.py:841
  18.6 14.9 %collective-permute-start = (bf16[128,2048]{1,0:T(8,128)(2,1)S(1)}, bf16[128,2048]{1,0:T(8,128)(2,1)S(1)}, u32[]{:S(2)}, u32[]{:S(2)}) collective-permute-start(bf16[128,2048]{1,0:T(8,128)(2,1)S(1)} %fusion.34.own_ref), channel_id=1, source_target_pairs={{0,8},{8,0},{16,24},{24,16},{1,9},{9,1},{17,25},{25,17},{2,10},{10... | collective-permute-start | bytes 1572872 | tf_op jit(solution)/shard_map/ppermute | solution.py:53
  21.6 13.8 %collective-permute-start.1 = (bf16[128,2048]{1,0:T(8,128)(2,1)S(1)}, bf16[128,2048]{1,0:T(8,128)(2,1)S(1)}, u32[]{:S(2)}, u32[]{:S(2)}) collective-permute-start(bf16[128,2048]{1,0:T(8,128)(2,1)S(1)} %fusion.34.own_ref), channel_id=1, source_target_pairs={{0,16},{8,24},{16,0},{24,8},{1,17},{9,25},{17,1},{25,9},{2,18},{10... | collective-permute-start | bytes 1572872 | tf_op jit(solution)/shard_map/ppermute | solution.py:53
  145.2 13.9 %collective-permute-start.5 = (bf16[128,2048]{1,0:T(8,128)(2,1)S(1)}, bf16[128,2048]{1,0:T(8,128)(2,1)S(1)}, u32[]{:S(2)}, u32[]{:S(2)}) collective-permute-start(bf16[128,2048]{1,0:T(8,128)(2,1)S(1)} %get-tuple-element.77), channel_id=1, source_target_pairs={{0,8},{8,0},{16,24},{24,16},{1,9},{9,1},{17,25},{25,17},{2,10},{10... | collective-permute-start | bytes 1572872 | tf_op jit(solution)/shard_map/ppermute | solution.py:53
  162.5 19.0 %collective-permute-start.13 = (bf16[128,2048]{1,0:T(8,128)(2,1)S(1)}, bf16[128,2048]{1,0:T(8,128)(2,1)S(1)}, u32[]{:S(2)}, u32[]{:S(2)}) collective-permute-start(bf16[128,2048]{1,0:T(8,128)(2,1)S(1)} %bitcast.122), channel_id=1, source_target_pairs={{0,8},{8,0},{16,24},{24,16},{1,9},{9,1},{17,25},{25,17},{2,10},{10... | collective-permute-start | bytes 1572872 | tf_op jit(solution)/shard_map/ppermute | solution.py:53
  163.0 19.1 %collective-permute-start.14 = (bf16[128,2048]{1,0:T(8,128)(2,1)S(1)}, bf16[128,2048]{1,0:T(8,128)(2,1)S(1)}, u32[]{:S(2)}, u32[]{:S(2)}) collective-permute-start(bf16[128,2048]{1,0:T(8,128)(2,1)S(1)} %bitcast.123), channel_id=1, source_target_pairs={{0,16},{8,24},{16,0},{24,8},{1,17},{9,25},{17,1},{25,9},{2,18},{10... | collective-permute-start | bytes 1572872 | tf_op jit(solution)/shard_map/ppermute | solution.py:53
  170.8 21.9 %collective-permute-start.9 = (bf16[128,2048]{1,0:T(8,128)(2,1)S(1)}, bf16[128,2048]{1,0:T(8,128)(2,1)S(1)}, u32[]{:S(2)}, u32[]{:S(2)}) collective-permute-start(bf16[128,2048]{1,0:T(8,128)(2,1)S(1)} %multiply_convert_fusion.own_ref), channel_id=1, source_target_pairs={{0,8},{8,0},{16,24},{24,16},{1,9},{9,1},{17,25},{25,17},{2,10},{10... | collective-permute-start | bytes 1572872 | tf_op jit(solution)/shard_map/ppermute | solution.py:53
  172.4 21.0 %collective-permute-start.10 = (bf16[128,2048]{1,0:T(8,128)(2,1)S(1)}, bf16[128,2048]{1,0:T(8,128)(2,1)S(1)}, u32[]{:S(2)}, u32[]{:S(2)}) collective-permute-start(bf16[128,2048]{1,0:T(8,128)(2,1)S(1)} %multiply_convert_fusion.own_ref), channel_id=1, source_target_pairs={{0,16},{8,24},{16,0},{24,8},{1,17},{9,25},{17,1},{25,9},{2,18},{10... | collective-permute-start | bytes 1572872 | tf_op jit(solution)/shard_map/ppermute | solution.py:53
  181.5 15.4 %collective-permute-start.15 = (bf16[64,2048]{1,0:T(8,128)(2,1)S(1)}, bf16[64,2048]{1,0:T(8,128)(2,1)S(1)}, u32[]{:S(2)}, u32[]{:S(2)}) collective-permute-start(bf16[64,2048]{1,0:T(8,128)(2,1)S(1)} %slice.422), channel_id=1, source_target_pairs={{0,16},{8,24},{16,0},{24,8},{1,17},{9,25},{17,1},{25,9},{2,18},{10... | collective-permute-start | bytes 786440 | tf_op jit(solution)/shard_map/ppermute | solution.py:53
  182.1 16.2 %collective-permute-start.16 = (bf16[64,2048]{1,0:T(8,128)(2,1)S(1)}, bf16[64,2048]{1,0:T(8,128)(2,1)S(1)}, u32[]{:S(2)}, u32[]{:S(2)}) collective-permute-start(bf16[64,2048]{1,0:T(8,128)(2,1)S(1)} %slice.423), channel_id=1, source_target_pairs={{0,8},{8,0},{16,24},{24,16},{1,9},{9,1},{17,25},{25,17},{2,10},{10... | collective-permute-start | bytes 786440 | tf_op jit(solution)/shard_map/ppermute | solution.py:53
  262.5 257.2 %reduce-scatter.5.cloned.1.call-start = ((), (), s32[]{:S(2)}) async-start(), calls=%async_computation.6 | async-start | bytes 8847360 | tf_op jit(solution)/shard_map/reduce_scatter | solution.py:841
  289.0 14.3 %collective-permute-start.17 = (bf16[128,2048]{1,0:T(8,128)(2,1)}, bf16[128,2048]{1,0:T(8,128)(2,1)S(1)}, u32[]{:S(2)}, u32[]{:S(2)}) collective-permute-start(bf16[128,2048]{1,0:T(8,128)(2,1)} %get-tuple-element.84), channel_id=1, source_target_pairs={{0,8},{8,0},{16,24},{24,16},{1,9},{9,1},{17,25},{25,17},{2,10},{10... | collective-permute-start | bytes 1572872 | tf_op jit(solution)/shard_map/ppermute | solution.py:53
  290.5 14.0 %collective-permute-start.18 = (bf16[128,2048]{1,0:T(8,128)(2,1)}, bf16[128,2048]{1,0:T(8,128)(2,1)S(1)}, u32[]{:S(2)}, u32[]{:S(2)}) collective-permute-start(bf16[128,2048]{1,0:T(8,128)(2,1)} %get-tuple-element.85), channel_id=1, source_target_pairs={{0,16},{8,24},{16,0},{24,8},{1,17},{9,25},{17,1},{25,9},{2,18},{10... | collective-permute-start | bytes 1572872 | tf_op jit(solution)/shard_map/ppermute | solution.py:53
  309.5 24.6 %collective-permute-start.27 = (bf16[512,1536]{1,0:T(8,128)(2,1)S(1)}, bf16[512,1536]{1,0:T(8,128)(2,1)}, u32[]{:S(2)}, u32[]{:S(2)}) collective-permute-start(bf16[512,1536]{1,0:T(8,128)(2,1)S(1)} %copy-done.9), channel_id=1, source_target_pairs={{0,1},{1,0},{2,3},{3,2},{4,5},{5,4},{6,7},{7,6},{8,9},{9,8},{10,11... | collective-permute-start | bytes 4718600 | tf_op jit(solution)/shard_map/ppermute | solution.py:206
  403.4 28.2 %collective-permute-start.37 = (bf16[128,2048]{1,0:T(8,128)(2,1)}, bf16[128,2048]{1,0:T(8,128)(2,1)S(1)}, u32[]{:S(2)}, u32[]{:S(2)}) collective-permute-start(bf16[128,2048]{1,0:T(8,128)(2,1)} %get-tuple-element.119), channel_id=1, source_target_pairs={{0,8},{8,0},{16,24},{24,16},{1,9},{9,1},{17,25},{25,17},{2,10},{10... | collective-permute-start | bytes 1572872 | tf_op jit(solution)/shard_map/ppermute | solution.py:53
  405.3 26.3 %collective-permute-start.38 = (bf16[128,2048]{1,0:T(8,128)(2,1)}, bf16[128,2048]{1,0:T(8,128)(2,1)S(1)}, u32[]{:S(2)}, u32[]{:S(2)}) collective-permute-start(bf16[128,2048]{1,0:T(8,128)(2,1)} %get-tuple-element.120), channel_id=1, source_target_pairs={{0,16},{8,24},{16,0},{24,8},{1,17},{9,25},{17,1},{25,9},{2,18},{10... | collective-permute-start | bytes 1572872 | tf_op jit(solution)/shard_map/ppermute | solution.py:53
  407.5 21.0 %collective-permute-start.43 = (bf16[144,640]{1,0:T(8,128)(2,1)S(1)}, bf16[144,640]{1,0:T(8,128)(2,1)}, u32[]{:S(2)}, u32[]{:S(2)}) collective-permute-start(bf16[144,640]{1,0:T(8,128)(2,1)S(1)} %add_convert_fusion.10), channel_id=1, source_target_pairs={{0,4},{1,5},{2,6},{3,7},{4,0},{5,1},{6,2},{7,3},{8,12},{9,13},{10,... | collective-permute-start | bytes 552968 | tf_op jit(solution)/shard_map/ppermute | solution.py:233
  417.9 16.7 %collective-permute-start.29 = (bf16[128,2048]{1,0:T(8,128)(2,1)}, bf16[128,2048]{1,0:T(8,128)(2,1)S(1)}, u32[]{:S(2)}, u32[]{:S(2)}) collective-permute-start(bf16[128,2048]{1,0:T(8,128)(2,1)} %get-tuple-element.110), channel_id=1, source_target_pairs={{0,8},{8,0},{16,24},{24,16},{1,9},{9,1},{17,25},{25,17},{2,10},{10... | collective-permute-start | bytes 1572872 | tf_op jit(solution)/shard_map/ppermute | solution.py:53
  418.4 16.2 %collective-permute-start.30 = (bf16[128,2048]{1,0:T(8,128)(2,1)}, bf16[128,2048]{1,0:T(8,128)(2,1)S(1)}, u32[]{:S(2)}, u32[]{:S(2)}) collective-permute-start(bf16[128,2048]{1,0:T(8,128)(2,1)} %get-tuple-element.111), channel_id=1, source_target_pairs={{0,16},{8,24},{16,0},{24,8},{1,17},{9,25},{17,1},{25,9},{2,18},{10... | collective-permute-start | bytes 1572872 | tf_op jit(solution)/shard_map/ppermute | solution.py:53
  434.7 21.5 %collective-permute-start.31 = (bf16[64,2048]{1,0:T(8,128)(2,1)S(1)}, bf16[64,2048]{1,0:T(8,128)(2,1)S(1)}, u32[]{:S(2)}, u32[]{:S(2)}) collective-permute-start(bf16[64,2048]{1,0:T(8,128)(2,1)S(1)} %get-tuple-element.186), channel_id=1, source_target_pairs={{0,16},{8,24},{16,0},{24,8},{1,17},{9,25},{17,1},{25,9},{2,18},{10... | collective-permute-start | bytes 786440 | tf_op jit(solution)/shard_map/ppermute | solution.py:53
  435.7 20.6 %collective-permute-start.32 = (bf16[64,2048]{1,0:T(8,128)(2,1)S(1)}, bf16[64,2048]{1,0:T(8,128)(2,1)S(1)}, u32[]{:S(2)}, u32[]{:S(2)}) collective-permute-start(bf16[64,2048]{1,0:T(8,128)(2,1)S(1)} %get-tuple-element.187), channel_id=1, source_target_pairs={{0,8},{8,0},{16,24},{24,16},{1,9},{9,1},{17,25},{25,17},{2,10},{10... | collective-permute-start | bytes 786440 | tf_op jit(solution)/shard_map/ppermute | solution.py:53
  (114 other events, 933.9 us)
Sparse Core Ops, SparseCore 0:
  10.7 80.4 all-gather.3
  93.4 115.2 all-gather.7
  210.3 62.9 all-gather.5
  275.5 109.3 reduce-scatter.2
  387.1 132.6 reduce-scatter.4

commit v7 on v5

--- a/solution.py
+++ b/solution.py
@@ -614,43 +614,32 @@
     ).astype(BF)
 
 
-def recur_grad_kernel(
-    low_ref, low_other, mixer_ref, mixer_other, proj_ref, proj_other, mixed_ref, mixed_other, held_ref, grad_ref
-):
-    step = pl.program_id(0)
-
-    @pl.when(step < 2)
-    def _():
-        grad_ref[...] = (
-            contract(low_ref[...], proj_ref[...]) + contract(low_other[...], proj_other[...])
-        ).astype(BF)
-
-    @pl.when(step == 2)
-    def _():
-        grad_ref[...] = (
-            contract(mixer_ref[...], mixed_ref[...]) + contract(mixer_other[...], mixed_other[...])
-        ).astype(BF)
-
-
-def recur_grad(low_t, mixer_t, proj, mixed, held):
-    depth, length = low_t[0].shape
-    width = mixed[0].shape[1]
+def outer_grad_kernel(left_ref, left_other, right_ref, right_other, held_ref, grad_ref):
+    grad_ref[...] = (
+        contract(left_ref[...], right_ref[...]) + contract(left_other[...], right_other[...])
+    ).astype(BF)
+
+
+def outer_grad(left_t, right, held, width, first, name):
+    depth, length = left_t[0].shape
+    steps = right[0].shape[1] // width
     fixed = pl.BlockSpec((depth, length), lambda i: (0, 0), pipeline_mode=pl.Buffered(1))
-    moving = pl.BlockSpec((length, width), lambda i: (0, jnp.minimum(i, 1)))
-    whole = pl.BlockSpec((length, width), lambda i: (0, 0))
+    moving = pl.BlockSpec((length, width), lambda i: (0, i))
     return pl.pallas_call(
-        recur_grad_kernel,
-        grid=(3,),
-        in_specs=[fixed] * 4 + [moving] * 2 + [whole] * 2 + [pl.BlockSpec(memory_space=pl.ANY)],
-        out_specs=pl.BlockSpec((depth, width), lambda i: (0, i)),
+        outer_grad_kernel,
+        grid=(steps,),
+        in_specs=[fixed] * 2 + [moving] * 2 + [pl.BlockSpec(memory_space=pl.ANY)],
+        out_specs=pl.BlockSpec((depth, width), lambda i: (0, first + i)),
         out_shape=jax.ShapeDtypeStruct(held.shape, BF),
-        input_output_aliases={8: 0},
+        input_output_aliases={4: 0},
         compiler_params=pltpu.CompilerParams(vmem_limit_bytes=40 * 2**20),
         cost_estimate=pl.CostEstimate(
-            flops=12 * depth * length * width, bytes_accessed=6 * depth * width + 8 * depth * length, transcendentals=0
-        ),
-        name="recur_grad",
-    )(*low_t, *mixer_t, *proj, *mixed, held)
+            flops=4 * depth * length * width * steps,
+            bytes_accessed=2 * steps * width * (depth + 2 * length) + 4 * depth * length,
+            transcendentals=0,
+        ),
+        name=name,
+    )(*left_t, *right, held)
 
 
 def mlp_grad_beside_kernel(
@@ -944,13 +933,15 @@
         rows, strip_tile, params, contract(mixer_grad, recur[:, 2 * recur_part :]), projected, states, decays, rate,
         opened, conv_out,
     )
+    held = outer_grad(mixer_rows, of_both(mixed_low), held, recur_part, 2, "recur_out_grad")
+    strips = after(swap(strips, 1), held)
     proj_grad, small, single = gates_backward(
-        tile_block, near, edge, conv_params, sums, gate_low_grad, input_low_grad, swap(strips, 1),
+        tile_block, near, edge, conv_params, sums, gate_low_grad, input_low_grad, strips,
         decay_lines, input_lines, conv_direct, conv_ext.T, projected, proj_grad,
     )
     mlp_term = scatter_halves(*mlp_out_last(unit, feed_last, after(units_last, proj_grad), out_first))
     output = (residual + mlp_term).astype(BF).reshape(tokens.shape)
-    grad_last_term = recur_grad(low1_rows, mixer_rows, of_both(proj_grad), of_both(mixed_low), held)
+    grad_last_term = outer_grad(low1_rows, of_both(proj_grad), held, recur_part, 0, "recur_in_grad")
     *pieces, _ = project(rows, after(proj_grad, grad_last_term), recur, 0, "normed1_grad")
     normed1_grad = scatter_halves(*pieces)
     input_norm_grad, first_gain_grad = jax.vjp(rms_norm, inputs, first_gain)[1](normed1_grad)

time: 536 us -> 536 us (level)
  starting transfers between devices: 63.5 us -> 49.4 us
  waiting for transfers between devices: 203 us -> 216 us
    ppermute x5, waiting for transfers between devices: 5.89 us -> 17.1 us  [sum_all(): value = value + lax.ppermute(value, axis, pairs)]
    ppermute x5, starting transfers between devices: 10.3 us -> 0.36 us  [sum_all(): value = value + lax.ppermute(value, axis, pairs)]
    unnamed x171 -> x179, local copies, waits for them, and re-layouts: 44.9 us -> 51.1 us
  transfers between devices with their start and end apart: 61 -> 61, of which waited for: 34 -> 33; matrix products, arithmetic and copies ran while one was open for 16% -> 15% of each run, Pallas kernels for 24% -> 24%
where the time goes in v7:
time: 536 us; the launch traced here: 531 us
  waiting for transfers between devices  216 us (40%)
  Pallas kernels  128 us (24%)
  local copies, waits for them, and re-layouts  87.1 us (16%)
  starting transfers between devices  49.4 us (9%)
  other arithmetic  24.7 us (5%)
  between operations  15.5 us (3%)
  matrix products  9.69 us (2%)
    ppermute x38, waiting for transfers between devices, swap(): lax.ppermute(value, 'seq', [(i, i ^ bit) for i in range(lax.axis_size('se...  76.4 us
    pallas_call x4, Pallas kernels, mlp_call(): pl.pallas_call(lambda *refs: kernel(tile, *refs), grid=(columns // (3 * t...  64.9 us
    all_gather x3, waiting for transfers between devices, gather_seg(): return lax.all_gather(value, 'seg', axis=0, tiled=True)  53.3 us
    unnamed x179, local copies, waits for them, and re-layouts  51.1 us
    ppermute x38, starting transfers between devices, swap(): lax.ppermute(value, 'seq', [(i, i ^ bit) for i in range(lax.axis_size('se...  45.2 us
    reduce_scatter x2, waiting for transfers between devices, scatter_rows(): lax.psum_scatter(value, 'seg', scatter_dimension=0, tiled=True, axis_inde...  29.3 us
    ppermute x3, waiting for transfers between devices, exchange(): return lax.ppermute(value, 'seg', [(i, i ^ bit) for i in range(8)])  25.1 us
    ppermute x5, waiting for transfers between devices, sum_all(): value = value + lax.ppermute(value, axis, pairs)  17.1 us
  transfers between devices with their start and end apart: 61, of which 33 were waited for; matrix products, arithmetic and copies ran while one was open for 15% of the time, Pallas kernels for 24%

profile of v7, /device:TPU:0, one launch (start us, length us, event | category | flops | bytes accessed | tf_op | source)
XLA Modules:
  0.0 531.1 jit_solution(14992536446296195188)
XLA Ops:
  27.4 7.5 %collective-permute-done.one_ref = bf16[128,2048]{1,0:T(8,128)(2,1)S(1)} collective-permute-done((bf16[128,2048]{1,0:T(8,128)(2,1)S(1)}, bf16[128,2048]{1,0:T(8,128)(2,1)S(1)}, u32[]{:S(2)}, u32[]{:S(2)}) %collective-permute-start) | collective-permute-done | bytes 524320 | tf_op jit(solution)/shard_map/ppermute | solution.py:53
  49.9 42.4 %all-gather.4.cloned.1.call-done.right_ref = bf16[2048,1920]{1,0:T(8,128)(2,1)} async-done(((bf16[256,1920]{1,0:T(8,128)(2,1)}), bf16[2048,1920]{1,0:T(8,128)(2,1)}) %all-gather.4.cloned.1.call-update) | async-done | bytes 7864336 | tf_op jit(solution)/shard_map/all_gather | solution.py:823
  92.3 6.0 %fusion.branch_ref.conv_in_ref = f32[512,1280]{1,0:T(8,128)S(1)} fusion(bf16[512,2048]{1,0:T(8,128)(2,1)} %copy-done.40, bf16[2048,1920]{1,0:T(8,128)(2,1)} %all-gather.4.cloned.1.call-done.right_ref), kind=kOutput, calls=%fused_computation | convolution fusion | flops 2684354560 | bytes 9961472 | tf_op jit(solution)/shard_map/dot_general | solution.py:39
  102.9 5.4 %fusion.72 = (bf16[512,640]{0,1:T(8,128)(2,1)S(1)}, f32[512,640]{0,1:T(8,128)}) fusion(f32[640]{0:T(1024)S(1)} %get-tuple-element.176, f32[512,640]{0,1:T(8,128)} %copy.91, f32[3,640]{0,1:T(8,128)S(1)} %bitcast.134, f32[640]{0:T(1024)S(1)} %get-tuple-element.177, f32[640]{0:T(1024)S(1)} %get-tuple-element.178, f32[640]{0:T(1024)S(1)} %dynamic-slice.12, ...), kind=kLoop, calls=%fused_computation.202 | loop fusion | flops 3932160 | bytes 3297280 | tf_op jit(solution)/shard_map/convert_element_type | solution.py:906
  123.5 11.6 %scan_forward.1 = (f32[512,640]{1,0:T(8,128)S(1)}, f32[512,640]{1,0:T(8,128)S(1)}, f32[512,640]{1,0:T(8,128)S(1)}, f32[512,640]{1,0:T(8,128)S(1)}, bf16[512,640]{1,0:T(8,128)(2,1)S(1)}) custom-call(s32[5]{0:T(128)S(1)} %get-tuple-element.242.blk_ref, bf16[512,768]{1,0:T(8,128)(2,1)S(1)} %copy-done.12, bf16[5,256,128]{2,1,0:T(8,128)(2,1)S(1)} %copy-done.15, ...), custom_call_target="tpu_custom_call" | custom-call | flops 335544320 | bytes 9175040 | tf_op jit(solution)/shard_map/scan_forward/pallas_call | solution.py:313
  148.3 11.8 %collective-permute-done.5 = bf16[128,2048]{1,0:T(8,128)(2,1)S(1)} collective-permute-done((bf16[128,2048]{1,0:T(8,128)(2,1)S(1)}, bf16[128,2048]{1,0:T(8,128)(2,1)S(1)}, u32[]{:S(2)}, u32[]{:S(2)}) %collective-permute-start.5) | collective-permute-done | bytes 524320 | tf_op jit(solution)/shard_map/ppermute | solution.py:53
  174.8 6.1 %collective-permute-done.13.one_ref = bf16[128,2048]{1,0:T(8,128)(2,1)S(1)} collective-permute-done((bf16[128,2048]{1,0:T(8,128)(2,1)S(1)}, bf16[128,2048]{1,0:T(8,128)(2,1)S(1)}, u32[]{:S(2)}, u32[]{:S(2)}) %collective-permute-start.13) | collective-permute-done | bytes 524320 | tf_op jit(solution)/shard_map/ppermute | solution.py:53
  184.1 8.1 %collective-permute-done.9.one_ref = bf16[128,2048]{1,0:T(8,128)(2,1)S(1)} collective-permute-done((bf16[128,2048]{1,0:T(8,128)(2,1)S(1)}, bf16[128,2048]{1,0:T(8,128)(2,1)S(1)}, u32[]{:S(2)}, u32[]{:S(2)}) %collective-permute-start.9) | collective-permute-done | bytes 524320 | tf_op jit(solution)/shard_map/ppermute | solution.py:53
  212.5 29.7 %mlp_first.1 = (bf16[512,3072]{1,0:T(8,128)(2,1)}, f32[512,2048]{1,0:T(8,128)}, f32[512,2048]{1,0:T(8,128)}) custom-call(bf16[512,2048]{1,0:T(8,128)(2,1)} %copy-done.39, bf16[512,2048]{1,0:T(8,128)(2,1)} %copy-done.38, bf16[2048,3072]{1,0:T(8,128)(2,1)} %all-gather.8.cloned.1.call-done.refs_2_), custom_call_target="tpu_custom_call" | custom-call | flops 12884901888 | bytes 41943040 | tf_op jit(solution)/shard_map/mlp_first/pallas_call | solution.py:722
  242.8 6.7 %collective-permute-done.26.refs_3_ = bf16[1024,512]{1,0:T(8,128)(2,1)S(1)} collective-permute-done((bf16[1024,512]{1,0:T(8,128)(2,1)}, bf16[1024,512]{1,0:T(8,128)(2,1)S(1)}, u32[]{:S(2)}, u32[]{:S(2)}) %collective-permute-start.26) | collective-permute-done | bytes 1048608 | tf_op jit(solution)/shard_map/ppermute | solution.py:206
  252.1 11.4 %mlp_grad.1 = bf16[1024,3072]{1,0:T(8,128)(2,1)} custom-call(bf16[1024,512]{1,0:T(8,128)(2,1)} %copy-done.28, bf16[1024,512]{1,0:T(8,128)(2,1)} %copy-done.32, bf16[1024,512]{1,0:T(8,128)(2,1)} %copy-done.26, bf16[1024,512]{1,0:T(8,128)(2,1)} %copy-done.30, bf16[512,3072]{1,0:T(8,128)(2,1)} %get-tuple-element.126.refs_4_, ...), custom_call_target="tpu_custom_call" | custom-call | flops 6442450944 | bytes 41943040 | tf_op jit(solution)/shard_map/mlp_grad/pallas_call | solution.py:722
  263.6 11.0 %all-gather.6.cloned.1.call-done.refs_2_.refs_0_ = bf16[2048,1536]{1,0:T(8,128)(2,1)} async-done(((bf16[256,1536]{1,0:T(8,128)(2,1)}), bf16[2048,1536]{1,0:T(8,128)(2,1)}) %all-gather.6.cloned.1.call-update) | async-done | bytes 6291472 | tf_op jit(solution)/shard_map/all_gather | solution.py:823
  274.5 16.1 %mlp_last.1 = (bf16[512,1536]{1,0:T(8,128)(2,1)}, bf16[128,2048]{1,0:T(8,128)(2,1)}, bf16[128,2048]{1,0:T(8,128)(2,1)}, f32[256,2048]{1,0:T(8,128)}) custom-call(bf16[512,2048]{1,0:T(8,128)(2,1)} %copy-done.39, bf16[512,2048]{1,0:T(8,128)(2,1)} %copy-done.38, bf16[2048,1536]{1,0:T(8,128)(2,1)} %all-gather.6.cloned.1.call-done.refs_2_.refs_0_, ...), custom_call_target="tpu_custom_call" | custom-call | flops 5368709120 | bytes 29360128 | tf_op jit(solution)/shard_map/mlp_last/pallas_call | solution.py:722
  293.6 11.3 %collective-permute-done.17 = bf16[128,2048]{1,0:T(8,128)(2,1)S(1)} collective-permute-done((bf16[128,2048]{1,0:T(8,128)(2,1)}, bf16[128,2048]{1,0:T(8,128)(2,1)S(1)}, u32[]{:S(2)}, u32[]{:S(2)}) %collective-permute-start.17) | collective-permute-done | bytes 524320 | tf_op jit(solution)/shard_map/ppermute | solution.py:53
  323.8 5.6 %collective-permute-done.21.one_ref = bf16[128,2048]{1,0:T(8,128)(2,1)S(1)} collective-permute-done((bf16[128,2048]{1,0:T(8,128)(2,1)S(1)}, bf16[128,2048]{1,0:T(8,128)(2,1)S(1)}, u32[]{:S(2)}, u32[]{:S(2)}) %collective-permute-start.21) | collective-permute-done | bytes 524320 | tf_op jit(solution)/shard_map/ppermute | solution.py:53
  341.0 6.0 %gather_mixer.1 = (bf16[512,2048]{1,0:T(8,128)(2,1)S(1)}, bf16[1024,512]{1,0:T(8,128)(2,1)S(1)}, bf16[1024,512]{1,0:T(8,128)(2,1)}) custom-call(s32[8]{0:T(128)S(1)} %iota_multiply_fusion.rows_ref, s32[1]{0:T(128)} %bitcast.9.core_ref, bf16[128,2048]{1,0:T(8,128)(2,1)S(1)} %fusion.71.own_ref, bf16[128,2048]{1,0:T(8,128)(2,1)S(1)} %collective-permute-done.21.one_ref, ...), custom_call_target="tpu_custom_call" | custom-call | bytes 6291456 | tf_op jit(solution)/shard_map/gather_mixer/pallas_call | solution.py:98
  352.0 8.9 %scan_backward.1 = (bf16[512,1280]{1,0:T(8,128)(2,1)S(1)}, bf16[512,640]{1,0:T(8,128)(2,1)S(1)}, bf16[512,640]{1,0:T(8,128)(2,1)S(1)}, f32[512,640]{1,0:T(8,128)...) custom-call(s32[8]{0:T(128)S(1)} %stack.46.rows_ref, s32[1]{0:T(128)} %bitcast.29.strip_ref, ...), custom_call_target="tpu_custom_call" | custom-call | flops 32768000 | bytes 14417920 | tf_op jit(solution)/shard_map/scan_backward/pallas_call | solution.py:436
  364.3 5.4 %collective-permute-done.28.strips_ref = bf16[2,512,128]{2,1,0:T(8,128)(2,1)S(1)} collective-permute-done((bf16[2,512,128]{2,1,0:T(8,128)(2,1)S(1)}, bf16[2,512,128]{2,1,0:T(8,128)(2,1)S(1)}, u32[]{:S(2)}, u32[]{:S(2)}) %collective-permute-start.28) | collective-permute-done | bytes 262176 | tf_op jit(solution)/shard_map/ppermute | solution.py:53
  392.9 5.7 %normed1_grad.1 = (bf16[128,2048]{1,0:T(8,128)(2,1)}, bf16[128,2048]{1,0:T(8,128)(2,1)}, f32[256,2048]{1,0:T(8,128)S(1)}, bf16[512,1280]{1,0:T(8,128)(2,1)}) custom-call(s32[8]{0:T(128)S(1)} %stack.46.rows_ref, bf16[512,1280]{1,0:T(8,128)(2,1)S(1)} %get-tuple-element.119.right_ref.left_ref, bf16[2048,1920]{1,0:T(8,128)(2,1)S(1)} %copy-done.8), custom_call_target="tpu_custom_call" | custom-call | flops 2684354560 | bytes 13631488 | tf_op jit(solution)/shard_map/normed1_grad/pallas_call | solution.py:173
  403.6 7.6 %mlp_out.1 = (bf16[128,2048]{1,0:T(8,128)(2,1)}, bf16[128,2048]{1,0:T(8,128)(2,1)}, f32[256,2048]{1,0:T(8,128)}) custom-call(bf16[2048,1536]{1,0:T(8,128)(2,1)} %all-gather.6.cloned.1.call-done.refs_2_.refs_0_, bf16[512,1536]{1,0:T(8,128)(2,1)} %get-tuple-element.112.refs_4_.refs_1_, f32[512,2048]{1,0:T(8,128)} %get-tuple-element.113.refs_2_), custom_call_target="tpu_custom_call" | custom-call | flops 1073741824 | bytes 29360128 | tf_op jit(solution)/shard_map/mlp_out/pallas_call | solution.py:722
  412.0 14.8 %collective-permute-done.43 = bf16[144,640]{1,0:T(8,128)(2,1)S(1)} collective-permute-done((bf16[144,640]{1,0:T(8,128)(2,1)S(1)}, bf16[144,640]{1,0:T(8,128)(2,1)S(1)}, u32[]{:S(2)}, u32[]{:S(2)}) %collective-permute-start.43) | collective-permute-done | bytes 184352 | tf_op jit(solution)/shard_map/ppermute | solution.py:233
  431.5 10.3 %collective-permute-done.44 = bf16[144,640]{1,0:T(8,128)(2,1)S(1)} collective-permute-done((bf16[144,640]{1,0:T(8,128)(2,1)S(1)}, bf16[144,640]{1,0:T(8,128)(2,1)S(1)}, u32[]{:S(2)}, u32[]{:S(2)}) %collective-permute-start.44) | collective-permute-done | bytes 184352 | tf_op jit(solution)/shard_map/ppermute | solution.py:233
  444.2 6.5 %collective-permute-done.50 = f32[2,2048]{1,0:T(2,128)S(1)} collective-permute-done((f32[2,2048]{1,0:T(2,128)S(1)}, f32[2,2048]{1,0:T(2,128)S(1)}, u32[]{:S(2)}, u32[]{:S(2)}) %collective-permute-start.50) | collective-permute-done | bytes 16416 | tf_op jit(solution)/shard_map/ppermute | solution.py:252
  491.7 29.3 %reduce-scatter.5.cloned.1.call-done.refs_0_ = bf16[256,3456]{1,0:T(8,128)(2,1)} async-done(((bf16[1024,3456]{1,0:T(8,128)(2,1)}), bf16[256,3456]{1,0:T(8,128)(2,1)}) %reduce-scatter.5.cloned.1.call-update) | async-done | bytes 1769488 | tf_op jit(solution)/shard_map/reduce_scatter | solution.py:830
  (412 shorter events, 230.4 us)
Async XLA Ops:
  7.2 85.1 %all-gather.4.cloned.1.call-start = ((), (), s32[]{:S(2)}) async-start(), calls=%async_computation.2 | async-start | bytes 8847360 | tf_op jit(solution)/shard_map/all_gather | solution.py:823
  11.7 200.8 %all-gather.8.cloned.1.call-start = ((), (), s32[]{:S(2)}) async-start(), calls=%async_computation.4 | async-start | bytes 14155776 | tf_op jit(solution)/shard_map/all_gather | solution.py:823
  18.3 256.2 %all-gather.6.cloned.1.call-start = ((), (), s32[]{:S(2)}) async-start(), calls=%async_computation.3 | async-start | bytes 7077888 | tf_op jit(solution)/shard_map/all_gather | solution.py:823
  19.0 367.6 %reduce-scatter.3.cloned.1.call-start = ((), (), s32[]{:S(2)}) async-start(), calls=%async_computation.5 | async-start | bytes 7864320 | tf_op jit(solution)/shard_map/reduce_scatter | solution.py:830
  20.0 14.9 %collective-permute-start = (bf16[128,2048]{1,0:T(8,128)(2,1)S(1)}, bf16[128,2048]{1,0:T(8,128)(2,1)S(1)}, u32[]{:S(2)}, u32[]{:S(2)}) collective-permute-start(bf16[128,2048]{1,0:T(8,128)(2,1)S(1)} %fusion.34.own_ref), channel_id=1, source_target_pairs={{0,8},{8,0},{16,24},{24,16},{1,9},{9,1},{17,25},{25,17},{2,10},{10... | collective-permute-start | bytes 1572872 | tf_op jit(solution)/shard_map/ppermute | solution.py:53
  163.4 17.5 %collective-permute-start.13 = (bf16[128,2048]{1,0:T(8,128)(2,1)S(1)}, bf16[128,2048]{1,0:T(8,128)(2,1)S(1)}, u32[]{:S(2)}, u32[]{:S(2)}) collective-permute-start(bf16[128,2048]{1,0:T(8,128)(2,1)S(1)} %bitcast.124), channel_id=1, source_target_pairs={{0,8},{8,0},{16,24},{24,16},{1,9},{9,1},{17,25},{25,17},{2,10},{10... | collective-permute-start | bytes 1572872 | tf_op jit(solution)/shard_map/ppermute | solution.py:53
  163.9 18.6 %collective-permute-start.14 = (bf16[128,2048]{1,0:T(8,128)(2,1)S(1)}, bf16[128,2048]{1,0:T(8,128)(2,1)S(1)}, u32[]{:S(2)}, u32[]{:S(2)}) collective-permute-start(bf16[128,2048]{1,0:T(8,128)(2,1)S(1)} %bitcast.125), channel_id=1, source_target_pairs={{0,16},{8,24},{16,0},{24,8},{1,17},{9,25},{17,1},{25,9},{2,18},{10... | collective-permute-start | bytes 1572872 | tf_op jit(solution)/shard_map/ppermute | solution.py:53
  172.8 19.3 %collective-permute-start.9 = (bf16[128,2048]{1,0:T(8,128)(2,1)S(1)}, bf16[128,2048]{1,0:T(8,128)(2,1)S(1)}, u32[]{:S(2)}, u32[]{:S(2)}) collective-permute-start(bf16[128,2048]{1,0:T(8,128)(2,1)S(1)} %multiply_convert_fusion.own_ref), channel_id=1, source_target_pairs={{0,8},{8,0},{16,24},{24,16},{1,9},{9,1},{17,25},{25,17},{2,10},{10... | collective-permute-start | bytes 1572872 | tf_op jit(solution)/shard_map/ppermute | solution.py:53
  173.3 20.4 %collective-permute-start.10 = (bf16[128,2048]{1,0:T(8,128)(2,1)S(1)}, bf16[128,2048]{1,0:T(8,128)(2,1)S(1)}, u32[]{:S(2)}, u32[]{:S(2)}) collective-permute-start(bf16[128,2048]{1,0:T(8,128)(2,1)S(1)} %multiply_convert_fusion.own_ref), channel_id=1, source_target_pairs={{0,16},{8,24},{16,0},{24,8},{1,17},{9,25},{17,1},{25,9},{2,18},{10... | collective-permute-start | bytes 1572872 | tf_op jit(solution)/shard_map/ppermute | solution.py:53
  180.9 18.4 %collective-permute-start.15 = (bf16[64,2048]{1,0:T(8,128)(2,1)S(1)}, bf16[64,2048]{1,0:T(8,128)(2,1)S(1)}, u32[]{:S(2)}, u32[]{:S(2)}) collective-permute-start(bf16[64,2048]{1,0:T(8,128)(2,1)S(1)} %slice.430), channel_id=1, source_target_pairs={{0,16},{8,24},{16,0},{24,8},{1,17},{9,25},{17,1},{25,9},{2,18},{10... | collective-permute-start | bytes 786440 | tf_op jit(solution)/shard_map/ppermute | solution.py:53
  182.5 16.8 %collective-permute-start.16 = (bf16[64,2048]{1,0:T(8,128)(2,1)S(1)}, bf16[64,2048]{1,0:T(8,128)(2,1)S(1)}, u32[]{:S(2)}, u32[]{:S(2)}) collective-permute-start(bf16[64,2048]{1,0:T(8,128)(2,1)S(1)} %slice.431), channel_id=1, source_target_pairs={{0,8},{8,0},{16,24},{24,16},{1,9},{9,1},{17,25},{25,17},{2,10},{10... | collective-permute-start | bytes 786440 | tf_op jit(solution)/shard_map/ppermute | solution.py:53
  263.5 257.4 %reduce-scatter.5.cloned.1.call-start = ((), (), s32[]{:S(2)}) async-start(), calls=%async_computation.6 | async-start | bytes 8847360 | tf_op jit(solution)/shard_map/reduce_scatter | solution.py:830
  311.8 21.6 %collective-permute-start.27 = (bf16[512,1536]{1,0:T(8,128)(2,1)S(1)}, bf16[512,1536]{1,0:T(8,128)(2,1)}, u32[]{:S(2)}, u32[]{:S(2)}) collective-permute-start(bf16[512,1536]{1,0:T(8,128)(2,1)S(1)} %copy-done.9), channel_id=1, source_target_pairs={{0,1},{1,0},{2,3},{3,2},{4,5},{5,4},{6,7},{7,6},{8,9},{9,8},{10,11... | collective-permute-start | bytes 4718600 | tf_op jit(solution)/shard_map/ppermute | solution.py:206
  347.0 15.3 %collective-permute-start.29 = (bf16[1024,512]{1,0:T(8,128)(2,1)}, bf16[1024,512]{1,0:T(8,128)(2,1)S(1)}, u32[]{:S(2)}, u32[]{:S(2)}) collective-permute-start(bf16[1024,512]{1,0:T(8,128)(2,1)} %get-tuple-element.106), channel_id=1, source_target_pairs={{0,1},{1,0},{2,3},{3,2},{4,5},{5,4},{6,7},{7,6},{8,9},{9,8},{10,11... | collective-permute-start | bytes 3145736 | tf_op jit(solution)/shard_map/ppermute | solution.py:206
  398.7 28.3 %collective-permute-start.37 = (bf16[128,2048]{1,0:T(8,128)(2,1)}, bf16[128,2048]{1,0:T(8,128)(2,1)S(1)}, u32[]{:S(2)}, u32[]{:S(2)}) collective-permute-start(bf16[128,2048]{1,0:T(8,128)(2,1)} %get-tuple-element.121), channel_id=1, source_target_pairs={{0,8},{8,0},{16,24},{24,16},{1,9},{9,1},{17,25},{25,17},{2,10},{10... | collective-permute-start | bytes 1572872 | tf_op jit(solution)/shard_map/ppermute | solution.py:53
  400.1 26.9 %collective-permute-start.38 = (bf16[128,2048]{1,0:T(8,128)(2,1)}, bf16[128,2048]{1,0:T(8,128)(2,1)S(1)}, u32[]{:S(2)}, u32[]{:S(2)}) collective-permute-start(bf16[128,2048]{1,0:T(8,128)(2,1)} %get-tuple-element.122), channel_id=1, source_target_pairs={{0,16},{8,24},{16,0},{24,8},{1,17},{9,25},{17,1},{25,9},{2,18},{10... | collective-permute-start | bytes 1572872 | tf_op jit(solution)/shard_map/ppermute | solution.py:53
  401.6 25.2 %collective-permute-start.43 = (bf16[144,640]{1,0:T(8,128)(2,1)S(1)}, bf16[144,640]{1,0:T(8,128)(2,1)S(1)}, u32[]{:S(2)}, u32[]{:S(2)}) collective-permute-start(bf16[144,640]{1,0:T(8,128)(2,1)S(1)} %add_convert_fusion.10), channel_id=1, source_target_pairs={{0,4},{1,5},{2,6},{3,7},{4,0},{5,1},{6,2},{7,3},{8,12},{9,13},{10,... | collective-permute-start | bytes 552968 | tf_op jit(solution)/shard_map/ppermute | solution.py:233
  411.2 16.1 %collective-permute-start.32 = (bf16[128,2048]{1,0:T(8,128)(2,1)}, bf16[128,2048]{1,0:T(8,128)(2,1)S(1)}, u32[]{:S(2)}, u32[]{:S(2)}) collective-permute-start(bf16[128,2048]{1,0:T(8,128)(2,1)} %get-tuple-element.116), channel_id=1, source_target_pairs={{0,16},{8,24},{16,0},{24,8},{1,17},{9,25},{17,1},{25,9},{2,18},{10... | collective-permute-start | bytes 1572872 | tf_op jit(solution)/shard_map/ppermute | solution.py:53
  411.7 15.5 %collective-permute-start.31 = (bf16[128,2048]{1,0:T(8,128)(2,1)}, bf16[128,2048]{1,0:T(8,128)(2,1)S(1)}, u32[]{:S(2)}, u32[]{:S(2)}) collective-permute-start(bf16[128,2048]{1,0:T(8,128)(2,1)} %get-tuple-element.115), channel_id=1, source_target_pairs={{0,8},{8,0},{16,24},{24,16},{1,9},{9,1},{17,25},{25,17},{2,10},{10... | collective-permute-start | bytes 1572872 | tf_op jit(solution)/shard_map/ppermute | solution.py:53
  426.9 14.9 %collective-permute-start.44 = (bf16[144,640]{1,0:T(8,128)(2,1)S(1)}, bf16[144,640]{1,0:T(8,128)(2,1)S(1)}, u32[]{:S(2)}, u32[]{:S(2)}) collective-permute-start(bf16[144,640]{1,0:T(8,128)(2,1)S(1)} %add_convert_fusion.9), channel_id=1, source_target_pairs={{0,2},{1,3},{2,0},{3,1},{4,6},{5,7},{6,4},{7,5},{8,10},{9,11},{10,... | collective-permute-start | bytes 552968 | tf_op jit(solution)/shard_map/ppermute | solution.py:233
  427.1 14.8 %collective-permute-start.40 = (bf16[64,2048]{1,0:T(8,128)(2,1)S(1)}, bf16[64,2048]{1,0:T(8,128)(2,1)S(1)}, u32[]{:S(2)}, u32[]{:S(2)}) collective-permute-start(bf16[64,2048]{1,0:T(8,128)(2,1)S(1)} %get-tuple-element.187), channel_id=1, source_target_pairs={{0,8},{8,0},{16,24},{24,16},{1,9},{9,1},{17,25},{25,17},{2,10},{10... | collective-permute-start | bytes 786440 | tf_op jit(solution)/shard_map/ppermute | solution.py:53
  427.2 14.7 %collective-permute-start.39 = (bf16[64,2048]{1,0:T(8,128)(2,1)S(1)}, bf16[64,2048]{1,0:T(8,128)(2,1)S(1)}, u32[]{:S(2)}, u32[]{:S(2)}) collective-permute-start(bf16[64,2048]{1,0:T(8,128)(2,1)S(1)} %get-tuple-element.186), channel_id=1, source_target_pairs={{0,16},{8,24},{16,0},{24,8},{1,17},{9,25},{17,1},{25,9},{2,18},{10... | collective-permute-start | bytes 786440 | tf_op jit(solution)/shard_map/ppermute | solution.py:53
  427.5 23.4 %collective-permute-start.34 = (bf16[64,2048]{1,0:T(8,128)(2,1)S(1)}, bf16[64,2048]{1,0:T(8,128)(2,1)S(1)}, u32[]{:S(2)}, u32[]{:S(2)}) collective-permute-start(bf16[64,2048]{1,0:T(8,128)(2,1)S(1)} %get-tuple-element.189), channel_id=1, source_target_pairs={{0,8},{8,0},{16,24},{24,16},{1,9},{9,1},{17,25},{25,17},{2,10},{10... | collective-permute-start | bytes 786440 | tf_op jit(solution)/shard_map/ppermute | solution.py:53
  429.4 21.4 %collective-permute-start.33 = (bf16[64,2048]{1,0:T(8,128)(2,1)S(1)}, bf16[64,2048]{1,0:T(8,128)(2,1)S(1)}, u32[]{:S(2)}, u32[]{:S(2)}) collective-permute-start(bf16[64,2048]{1,0:T(8,128)(2,1)S(1)} %get-tuple-element.188), channel_id=1, source_target_pairs={{0,16},{8,24},{16,0},{24,8},{1,17},{9,25},{17,1},{25,9},{2,18},{10... | collective-permute-start | bytes 786440 | tf_op jit(solution)/shard_map/ppermute | solution.py:53
  (119 other events, 929.5 us)
Sparse Core Ops, SparseCore 0:
  11.8 80.4 all-gather.3
  94.5 115.2 all-gather.7
  211.5 62.9 all-gather.5
  276.7 109.3 reduce-scatter.2
  388.3 132.6 reduce-scatter.4
